TPU v7x, 256 devices: a whole 4x4x8 slice. The times are simulated.
256 devices in a mesh: row: 16 (over z, core), col: 8 (over x_hi, y), samp: 2 (over x_lo).
Axes of the slice: x: 4 (x_hi: 2, x_lo: 2; x = x_hi * 2 + x_lo), y: 4, z: 8, core: 2. Of those that a mesh axis runs over, the one named last changes fastest.
Arguments:
- acts: bfloat16 [24, 1536, 768], P('samp', 'row'), may hold values from -9 to 9
- cond: bfloat16 [24, 1536, 384], P('samp', 'row'), may hold values from -6 to 6
- pair: bfloat16 [1536, 1536, 128], P(('row', 'samp'), 'col'), may hold values from -6 to 88
- chain_id: int32 [1536], replicated, may hold values from 0 to 7, never falling along the last dimension, each value on 1 to 384 neighbouring positions
- residue_mask: int32 [1536], replicated, may hold values 0 or 1
- w_bias: bfloat16 [128, 16], replicated, may hold values from -25 to 25
- chain_bias: float32 [16], P('col'), may hold values from -2 to 2
- ada1_scale: bfloat16 [384, 768], replicated, may hold values from -0.3125 to 0.3125
- ada1_shift: bfloat16 [384, 768], replicated, may hold values from -0.3125 to 0.3125
- w_qkvg: bfloat16 [4, 768, 768], P(None, None, 'col'), may hold values from -0.21875 to 0.21875
- w_out: bfloat16 [768, 768], replicated, may hold values from -0.21875 to 0.21875
- out_gate1: bfloat16 [384, 768], P(None, 'col'), may hold values from -0.3125 to 0.3125
- ada2_scale: bfloat16 [384, 768], replicated, may hold values from -0.3125 to 0.3125
- ada2_shift: bfloat16 [384, 768], replicated, may hold values from -0.3125 to 0.3125
- w_up: bfloat16 [2, 768, 1536], P(None, None, 'col'), may hold values from -0.21875 to 0.21875
- w_down: bfloat16 [1536, 768], P('col'), may hold values from -0.15625 to 0.15625
- out_gate2: bfloat16 [384, 768], P(None, 'col'), may hold values from -0.3125 to 0.3125
Outputs:
- block_out: bfloat16 [24, 1536, 768], P('samp', 'row', 'col')
All inputs are finite; a program needn't handle non-finite values.
Results may differ from a plain program's by a relative error of at most 0.011.
Values may be sent and summed in bfloat16 or wider, within the bound.
No kernel may reach another device: no remote copies, remote signals or barrier semaphores. Data moves between devices by JAX's collectives and lax.ppermute only.
A program may use at most 128 MiB of HBM per device.

v0:
```python
import math

import jax
import jax.numpy as jnp
from jax import lax
from jax.sharding import PartitionSpec as P

DH = 48


epsilon = 1e-05


def normalize(values):
    row_mean = jnp.mean(values, axis=-1, keepdims=True)
    row_square = jnp.mean(values * values, axis=-1, keepdims=True)
    return (values - row_mean) * lax.rsqrt(row_square - row_mean * row_mean + epsilon)


def cond_mix(left, right):
    return jnp.einsum("snc,cd->snd", left, right, preferred_element_type=jnp.float32)


def per_device(
    acts,
    cond,
    pair,
    chain_id,
    residue_mask,
    w_bias,
    chain_bias,
    ada1_scale,
    ada1_shift,
    w_qkvg,
    w_out,
    out_gate1,
    ada2_scale,
    ada2_shift,
    w_up,
    w_down,
    out_gate2,
):
    samples, row_count, model_width = acts.shape
    tokens_all = chain_id.shape[0]
    col_index = lax.axis_index("col")
    share_width = model_width // lax.axis_size("col")
    local_width = w_qkvg.shape[2]
    local_heads = local_width // DH
    scale_multiplier = 1.0 / math.sqrt(DH)
    cond_norm = normalize(cond.astype(jnp.float32)).astype(jnp.bfloat16)
    attn_input = (
        jax.nn.sigmoid(cond_mix(cond_norm, ada1_scale)) * normalize(acts.astype(jnp.float32))
        + cond_mix(cond_norm, ada1_shift)
    ).astype(jnp.bfloat16)
    projected = jnp.einsum("snd,kde->ksne", attn_input, w_qkvg, preferred_element_type=jnp.float32)
    queries = projected[0].astype(jnp.bfloat16)
    keys = projected[1].astype(jnp.bfloat16)
    values = projected[2].astype(jnp.bfloat16)
    attn_gate = jax.nn.sigmoid(projected[3])
    complete_keys, all_values = (
        lax.all_gather(keys, "row", axis=1, tiled=True),
        lax.all_gather(values, "row", axis=1, tiled=True),
    )
    pair_norm = normalize(pair.astype(jnp.float32)).astype(jnp.bfloat16)
    bias_tile = jnp.einsum(
        "ijc,ch->hij", pair_norm, w_bias, preferred_element_type=jnp.float32
    ).astype(jnp.bfloat16)
    bias_tile = lax.all_gather(bias_tile, "samp", axis=1, tiled=True)
    head_bias = lax.all_to_all(bias_tile, "col", split_axis=0, concat_axis=2, tiled=True)
    row_start = lax.axis_index("row") * row_count
    positions = jnp.arange(tokens_all)
    local_pos = row_start + jnp.arange(row_count)
    chain_rows = lax.dynamic_slice_in_dim(chain_id, row_start, row_count)
    same_chain = (chain_rows[:, None] == chain_id[None, :]).astype(jnp.float32)
    active_keys = (residue_mask[None, :] == 1) | (local_pos[:, None] == positions[None, :])
    key_bias = head_bias.astype(jnp.float32) + chain_bias[:, None, None] * same_chain[None]
    group = max((size for size in (1, 2, 3, 4) if samples % size == 0))

    def grouped(array):
        return array.reshape((samples // group, group) + array.shape[1:])

    def attend(input_rows):
        query_block, key_block, value_block = input_rows
        query_heads = query_block.reshape(group, row_count, local_heads, DH)
        key_heads = key_block.reshape(group, tokens_all, local_heads, DH)
        value_heads = value_block.reshape(group, tokens_all, local_heads, DH)
        logits = (
            jnp.einsum(
                "sihd,sjhd->shij", query_heads, key_heads, preferred_element_type=jnp.float32
            )
            * scale_multiplier
            + key_bias[None]
        )
        logits = jnp.where(active_keys[None, None], logits, -1000000000.0)
        row_max = jnp.max(logits, axis=-1, keepdims=True)
        exp_terms = jnp.exp(logits - row_max)
        weights = (exp_terms / jnp.sum(exp_terms, axis=-1, keepdims=True)).astype(jnp.bfloat16)
        mixed_heads = jnp.einsum(
            "shij,sjhd->sihd", weights, value_heads, preferred_element_type=jnp.float32
        )
        return mixed_heads.reshape(group, row_count, local_width)

    attended = lax.map(
        attend, (grouped(queries), grouped(complete_keys), grouped(all_values))
    ).reshape(samples, row_count, local_width)
    heads_out = (attn_gate * attended).astype(jnp.bfloat16)
    complete_heads = lax.all_gather(heads_out, "col", axis=2, tiled=True)
    output_columns = lax.dynamic_slice_in_dim(w_out, col_index * share_width, share_width, 1)
    attn_share = jnp.einsum(
        "lit,tw->liw", complete_heads, output_columns, preferred_element_type=jnp.float32
    )
    act_share = lax.dynamic_slice_in_dim(acts, col_index * share_width, share_width, 2).astype(
        jnp.float32
    )
    stream = act_share + jax.nn.sigmoid(cond_mix(cond_norm, out_gate1)) * attn_share
    row_sums, row_squares = lax.psum(
        (jnp.sum(stream, axis=-1), jnp.sum(stream * stream, axis=-1)), "col"
    )
    row_mean = (row_sums / model_width)[:, :, None]
    row_square = (row_squares / model_width)[:, :, None]
    normalized = (stream - row_mean) * lax.rsqrt(row_square - row_mean * row_mean + epsilon)
    scale_cols = lax.dynamic_slice_in_dim(ada2_scale, col_index * share_width, share_width, 1)
    shift_columns = lax.dynamic_slice_in_dim(ada2_shift, col_index * share_width, share_width, 1)
    input_share = (
        jax.nn.sigmoid(cond_mix(cond_norm, scale_cols)) * normalized
        + cond_mix(cond_norm, shift_columns)
    ).astype(jnp.bfloat16)
    ffn_input = lax.all_gather(input_share, "col", axis=2, tiled=True)
    up_gate = jnp.einsum("snd,kdf->ksnf", ffn_input, w_up, preferred_element_type=jnp.float32)
    hidden = (jax.nn.silu(up_gate[1]) * up_gate[0]).astype(jnp.bfloat16)
    partial_ffn = jnp.einsum("snf,fd->snd", hidden, w_down, preferred_element_type=jnp.float32)
    ffn_part = lax.psum_scatter(
        partial_ffn.astype(jnp.bfloat16), "col", scatter_dimension=2, tiled=True
    ).astype(jnp.float32)
    return (stream + jax.nn.sigmoid(cond_mix(cond_norm, out_gate2)) * ffn_part).astype(jnp.bfloat16)


def solution(mesh):
    in_specs = (
        P("samp", "row", None),
        P("samp", "row", None),
        P(("row", "samp"), "col", None),
        P(),
        P(),
        P(),
        P("col"),
        P(),
        P(),
        P(None, None, "col"),
        P(),
        P(None, "col"),
        P(),
        P(),
        P(None, None, "col"),
        P("col", None),
        P(None, "col"),
    )
    out_specs = P("samp", "row", "col")
    return jax.shard_map(
        per_device, mesh=mesh, in_specs=in_specs, out_specs=out_specs, check_vma=False
    )
```

profile of v0, /device:TPU:1, one launch (start us, length us, event | category | flops | bytes accessed | tf_op | source)
XLA Modules:
  0.0 448.3 jit_solution(5828016501873880461)
XLA Ops:
  6.5 1.8 convert_reduce_fusion.2
  8.4 2.1 convert_reduce_fusion.1
  10.5 2.9 fusion.73
  13.4 6.6 %fusion.102 = (bf16[4,12,96,96]{3,2,0,1:T(8,128)(2,1)}, f32[4,12,96,96]{3,2,0,1:T(8,128)}) fusion(bf16[4,768,96]{1,2,0:T(8,128)(2,1)S(1)} %copy-done.10, f32[12,96]{1,0:T(8,128)S(1)} %get-tuple-element.133, f32[12,96]{1,0:T(8,128)S(1)} %get-tuple-element.132, bf16[12,96,768]{2,1,0:T(8,128)(2,1)} %param.19, f32[12,96,768]{2,1,0:T(8,128)} %fusion.73, ...), kind=kOutput, calls=%fused_computation.119 | convolution fusion | flops 1369128960 | bytes 10045440 | tf_op jit(solution)/shard_map/snd,kde->ksne/dot_general | solution.py:55
  20.0 2.2 fusion.101
  23.1 2.6 convert_reduce_fusion
  25.7 4.0 fusion.58
  29.6 10.2 %all_gather.17 = bf16[16,96,192]{2,0,1:T(8,128)(2,1)S(1)} all-gather(bf16[16,48,192]{2,0,1:T(8,128)(2,1)S(1)} %fusion.58), channel_id=1, replica_groups=mesh['row'=16,'col'=8,'samp'=2] {'samp'}, dimensions={1}, use_global_device_ids=true | all-gather | bytes 884736 | tf_op jit(solution)/shard_map/all_gather | solution.py:68
  39.9 1.1 copy.60
  41.0 8.0 %all-to-all-start = ((bf16[16,96,192]{2,1,0:T(8,128)(2,1)}), bf16[16,96,192]{2,1,0:T(8,128)(2,1)S(1)}, u32[]{:S(2)}, u32[]{:S(2)}) async-start(bf16[16,96,192]{2,1,0:T(8,128)(2,1)} %copy.60), calls=%async_computation | async-start | bytes 1572864 | tf_op jit(solution)/shard_map/all_to_all | solution.py:69
  49.5 9.8 %all-to-all-done = bf16[16,96,192]{2,1,0:T(8,128)(2,1)S(1)} async-done(((bf16[16,96,192]{2,1,0:T(8,128)(2,1)}), bf16[16,96,192]{2,1,0:T(8,128)(2,1)S(1)}, u32[]{:S(2)}, u32[]{:S(2)}) %all-to-all-start) | async-done | bytes 589856 | tf_op jit(solution)/shard_map/all_to_all | solution.py:69
  60.4 1.6 reshape.140
  62.0 2.5 multiply_add_fusion
  64.6 5.0 %all-gather.11.cloned.1.call-done = bf16[1,12,1536,96]{3,2,0,1:T(8,128)(2,1)} async-done(((bf16[1,12,96,96]{3,2,0,1:T(8,128)(2,1)}), bf16[1,12,1536,96]{3,2,0,1:T(8,128)(2,1)}) %all-gather.11.cloned.1.call-update) | async-done | bytes 3538960 | tf_op jit(solution)/shard_map/all_gather | solution.py:62
  69.6 6.3 %copy.62 = bf16[3,4,1536,96]{2,3,1,0:T(8,128)(2,1)} copy(bf16[3,4,1536,96]{3,2,1,0:T(8,128)(2,1)} %bitcast.121) | data formatting | bytes 7077888
  75.9 36.8 %all-gather.13.cloned.1.call-done = bf16[1,12,1536,96]{3,2,0,1:T(8,128)(2,1)} async-done(((bf16[1,12,96,96]{3,2,0,1:T(8,128)(2,1)}), bf16[1,12,1536,96]{3,2,0,1:T(8,128)(2,1)}) %all-gather.13.cloned.1.call-update) | async-done | bytes 3538960 | tf_op jit(solution)/shard_map/all_gather | solution.py:61
  112.7 6.4 %copy.64 = bf16[3,4,1536,96]{2,3,1,0:T(8,128)(2,1)} copy(bf16[3,4,1536,96]{3,2,1,0:T(8,128)(2,1)} %bitcast.122) | data formatting | bytes 7077888
  119.1 47.8 %while.11 = (s32[]{:T(128)}, f32[3,4,96,96]{3,2,1,0:T(8,128)}, bf16[3,4,1536,96]{2,3,1,0:T(8,128)(2,1)}, bf16[3,4,96,96]{3,2,1,0:T(8,128)(2,1)}, bf16[3,4,1536,9...) while((s32[]{:T(128)}, f32[3,4,96,96]{3,2,1,0:T(8,128)}, ...), condition=%wide.region_9.10_spmd.clone, body=%wide.region_6.9_spmd.clone.sunk | while | flops 235046400 | bytes 19153380 | solution.py:103
  119.1 1.9 constant_dynamic-slice_fusion.6
  120.9 1.5 constant_dynamic-slice_fusion.7
  122.5 1.6 copy.120
  124.9 5.9 %fusion.120 = (f32[4,2,96]{2,1,0:T(2,128)}, f32[4,2,96,1536]{3,2,1,0:T(8,128)}) fusion(bf16[4,96,2,48]{1,3,2,0:T(8,128)(2,1)} %bitcast.124, bf16[4,1536,2,48]{1,3,2,0:T(8,128)(2,1)S(1)} %bitcast.118, f32[2,96,1536]{2,1,0:T(8,128)} %get-tuple-element.221, pred[96,1536]{1,0:T(8,128)(4,1)} %fusion.119), kind=kOutput, calls=%fused_computation.117.clone.1 | convolution fusion | flops 119145984 | bytes 7302144 | tf_op jit(solution)/shard_map/while/body/eval_jaxpr/sub | solution.py:96
  130.9 3.3 fusion.121
  135.0 1.9 constant_dynamic-slice_fusion.6
  136.9 1.5 constant_dynamic-slice_fusion.7
  138.4 1.6 copy.120
  140.9 5.9 %fusion.120 = (f32[4,2,96]{2,1,0:T(2,128)}, f32[4,2,96,1536]{3,2,1,0:T(8,128)}) fusion(bf16[4,96,2,48]{1,3,2,0:T(8,128)(2,1)} %bitcast.124, bf16[4,1536,2,48]{1,3,2,0:T(8,128)(2,1)S(1)} %bitcast.118, f32[2,96,1536]{2,1,0:T(8,128)} %get-tuple-element.221, pred[96,1536]{1,0:T(8,128)(4,1)} %fusion.119), kind=kOutput, calls=%fused_computation.117.clone.1 | convolution fusion | flops 119145984 | bytes 7302144 | tf_op jit(solution)/shard_map/while/body/eval_jaxpr/sub | solution.py:96
  146.8 3.3 fusion.121
  150.9 1.9 constant_dynamic-slice_fusion.6
  152.8 1.5 constant_dynamic-slice_fusion.7
  154.4 1.6 copy.120
  156.8 5.9 %fusion.120 = (f32[4,2,96]{2,1,0:T(2,128)}, f32[4,2,96,1536]{3,2,1,0:T(8,128)}) fusion(bf16[4,96,2,48]{1,3,2,0:T(8,128)(2,1)} %bitcast.124, bf16[4,1536,2,48]{1,3,2,0:T(8,128)(2,1)S(1)} %bitcast.118, f32[2,96,1536]{2,1,0:T(8,128)} %get-tuple-element.221, pred[96,1536]{1,0:T(8,128)(4,1)} %fusion.119), kind=kOutput, calls=%fused_computation.117.clone.1 | convolution fusion | flops 119145984 | bytes 7302144 | tf_op jit(solution)/shard_map/while/body/eval_jaxpr/sub | solution.py:96
  162.7 3.3 fusion.121
  166.9 1.5 fusion.76
  169.5 1.2 constant_dynamic-slice_fusion.3
  171.0 1.5 fusion.55
  172.5 62.6 %all-gather.7.cloned.1.call-done = bf16[12,96,768]{1,0,2:T(8,128)(2,1)} async-done(((bf16[12,96,96]{1,0,2:T(8,128)(2,1)}), bf16[12,96,768]{1,0,2:T(8,128)(2,1)}) %all-gather.7.cloned.1.call-update) | async-done | bytes 1769488 | tf_op jit(solution)/shard_map/all_gather | solution.py:107
  235.1 2.7 fusion.99
  237.9 30.4 %all-reduce = (f32[12,96]{1,0:T(8,128)S(1)}, f32[12,96]{1,0:T(8,128)S(1)}) all-reduce(f32[12,96]{1,0:T(8,128)S(1)} %get-tuple-element.102, f32[12,96]{1,0:T(8,128)S(1)} %get-tuple-element.101), channel_id=1, replica_groups=mesh['row'=16,'col'=8,'samp'=2] {'col'}, use_global_device_ids=true, to_apply=%region_13.14 | all-reduce | flops 2304 | bytes 18432 | tf_op jit(solution)/shard_map/psum | solution.py:116
  268.3 1.8 fusion.47
  270.2 1.8 fusion.57
  273.2 73.3 %all-gather.9.cloned.1.call-done = bf16[12,96,768]{1,0,2:T(8,128)(2,1)} async-done(((bf16[12,96,96]{1,0,2:T(8,128)(2,1)}), bf16[12,96,768]{1,0,2:T(8,128)(2,1)}) %all-gather.9.cloned.1.call-update) | async-done | bytes 1769488 | tf_op jit(solution)/shard_map/all_gather | solution.py:128
  346.5 3.5 fusion.32
  350.0 2.0 convolution_convert_fusion
  352.0 4.8 %copy.86 = bf16[12,96,768]{1,0,2:T(8,128)(2,1)} copy(bf16[12,96,768]{2,1,0:T(8,128)(2,1)} %convolution_convert_fusion) | data formatting | bytes 3538944
  356.8 5.7 %reshape.162 = bf16[768,1152]{1,0:T(8,128)(2,1)} reshape(bf16[768,12,96]{2,1,0:T(8,128)(2,1)} %bitcast.119) | data formatting | bytes 3538944
  362.5 76.1 %reduce-scatter.4.cloned.1.call-done = bf16[96,1152]{1,0:T(8,128)(2,1)} async-done(((bf16[768,1152]{1,0:T(8,128)(2,1)}), bf16[96,1152]{1,0:T(8,128)(2,1)}) %reduce-scatter.4.cloned.1.call-update) | async-done | bytes 221200
  438.7 1.5 reshape.163
  (70 shorter events, 11.4 us)
Async XLA Ops:
  6.5 228.6 %copy-start = (bf16[768,768]{1,0:T(8,128)(2,1)S(1)}, bf16[768,768]{1,0:T(8,128)(2,1)}, u32[]{:S(2)}) copy-start(bf16[768,768]{1,0:T(8,128)(2,1)} %param.29) | copy-start | bytes 3538948
  6.5 3.9 copy-start.1
  6.5 4.0 copy-start.4
  6.5 63.0 %all-gather.11.cloned.1.call-start = ((), (), s32[]{:S(2)}) async-start(), calls=%async_computation.4 | async-start | bytes 5013504 | tf_op jit(solution)/shard_map/all_gather | solution.py:62
  10.5 2.9 copy-start.5
  10.5 2.9 copy-start.10
  20.0 3.0 copy-start.3
  22.3 3.4 copy-start.15
  22.3 90.4 %all-gather.13.cloned.1.call-start = ((), (), s32[]{:S(2)}) async-start(), calls=%async_computation.5 | async-start | bytes 5013504 | tf_op jit(solution)/shard_map/all_gather | solution.py:61
  39.9 9.4 %copy-start.8 = (s32[1536]{0:T(1024)S(1)}, s32[1536]{0:T(1024)}, u32[]{:S(2)}) copy-start(s32[1536]{0:T(1024)} %param.23) | copy-start | bytes 18436
  39.9 9.4 %copy-start.7 = (s32[1536]{0:T(1024)S(1)}, s32[1536]{0:T(1024)}, u32[]{:S(2)}) copy-start(s32[1536]{0:T(1024)} %param.22) | copy-start | bytes 18436
  41.0 18.3 %all-to-all-start = ((bf16[16,96,192]{2,1,0:T(8,128)(2,1)}), bf16[16,96,192]{2,1,0:T(8,128)(2,1)S(1)}, u32[]{:S(2)}, u32[]{:S(2)}) async-start(bf16[16,96,192]{2,1,0:T(8,128)(2,1)} %copy.60), calls=%async_computation | async-start | bytes 1572864 | tf_op jit(solution)/shard_map/all_to_all | solution.py:69
  49.0 186.1 %all-gather.7.cloned.1.call-start = ((), (), s32[]{:S(2)}) async-start(), calls=%async_computation.2 | async-start | bytes 3538944 | tf_op jit(solution)/shard_map/all_gather | solution.py:107
  60.4 1.6 copy-start.9
  166.9 4.0 copy-start.2
  166.9 4.1 copy-start.6
  166.9 4.1 copy-start.13
  169.5 177.1 %all-gather.9.cloned.1.call-start = ((), (), s32[]{:S(2)}) async-start(), calls=%async_computation.3 | async-start | bytes 3538944 | tf_op jit(solution)/shard_map/all_gather | solution.py:128
  237.9 32.3 %copy-start.16 = (f32[12,96,96]{1,2,0:T(8,128)}, f32[12,96,96]{1,2,0:T(8,128)S(1)}, u32[]{:S(2)}) copy-start(f32[12,96,96]{1,2,0:T(8,128)S(1)} %get-tuple-element.138) | copy-start | bytes 1327108
  270.2 76.4 %copy-start.11 = (bf16[2,768,192]{1,2,0:T(8,128)(2,1)S(1)}, bf16[2,768,192]{1,2,0:T(8,128)(2,1)}, u32[]{:S(2)}) copy-start(bf16[2,768,192]{1,2,0:T(8,128)(2,1)} %param.33) | copy-start | bytes 1769476
  272.9 165.8 %reduce-scatter.4.cloned.1.call-start = ((), (), s32[]{:S(2)}) async-start(), calls=%async_computation.6 | async-start | bytes 1990656
  346.5 3.5 copy-start.12
  362.5 77.6 %copy-start.14 = (bf16[384,96]{0,1:T(8,128)(2,1)S(1)}, bf16[384,96]{0,1:T(8,128)(2,1)}, u32[]{:S(2)}) copy-start(bf16[384,96]{0,1:T(8,128)(2,1)} %param.35) | copy-start | bytes 221188
  362.5 77.6 %copy-start.17 = (f32[12,96,96]{1,2,0:T(8,128)S(1)}, f32[12,96,96]{1,2,0:T(8,128)}, u32[]{:S(2)}) copy-start(f32[12,96,96]{1,2,0:T(8,128)} %copy-done.16) | copy-start | bytes 1327108
Sparse Core Ops, SparseCore 0:
  22.4 47.0 all-gather.10
  71.4 41.2 all-gather.12
  169.6 65.4 all-gather.6
  273.0 73.4 all-gather.8
  362.7 75.9 reduce-scatter.3
where the time goes:
time: 450 us; the launch traced here: 448 us
  waiting for transfers between devices  264 us (59%)
  matrix products  55.3 us (12%)
  local copies, waits for them, and re-layouts  52.5 us (12%)
  blocking collectives  40.7 us (9%)
  between operations  13.4 us (3%)
  other arithmetic  13.3 us (3%)
  starting transfers between devices  8.58 us (2%)
    unnamed x6, waiting for transfers between devices  76.9 us
    all_gather x1, waiting for transfers between devices, per_device(): ffn_input = lax.all_gather(input_share, 'col', axis=2, tiled=True)  73.3 us
    all_gather x1, waiting for transfers between devices, per_device(): complete_heads = lax.all_gather(heads_out, 'col', axis=2, tiled=True)  62.6 us
    all_gather x1, waiting for transfers between devices, per_device(): lax.all_gather(keys, 'row', axis=1, tiled=True)  36.8 us
    psum x1, blocking collectives, per_device(): lax.psum((jnp.sum(stream, axis=-1), jnp.sum(stream * stream, axis=-1)), '...  30.4 us
    unnamed x42, local copies, waits for them, and re-layouts  24.9 us
    sub x3, matrix products, attend(): exp_terms = jnp.exp(logits - row_max)  17.8 us
    dynamic_slice x9, local copies, waits for them, and re-layouts, per_device(): lax.map(attend, (grouped(queries), grouped(complete_keys), grouped(all_va...  15.1 us
  transfers between devices with their start and end apart: 6, of which 6 were waited for; matrix products, arithmetic and copies ran while one was open for 5% of the time, Pallas kernels for 0%

commit v1 on v0

v1 whole, which is shorter than its diff:
```python
import functools
import math

import jax
import jax.numpy as jnp
from jax import lax
from jax.experimental import pallas as pl
from jax.experimental.pallas import tpu as pltpu
from jax.sharding import Mesh, PartitionSpec as P

DH = 48
PIECE = 2 * DH
GROUP = 4
WIDE = GROUP * PIECE
EPS = 1e-05
LOG2E = math.log2(math.e)
MASKED = -1000000000.0
COL = ("xh", "y")
PLANE = ("xh", "y", "core")
VMEM = 56 * 1024 * 1024

FIRST = ((0, 128), (0, 256), (128, 256), (256, 384))
SECOND = ((0, 128), (128, 256), (128, 384), (256, 384))

f32 = jnp.float32
bf16 = jnp.bfloat16


def normalize(values):
    mean = jnp.mean(values, axis=-1, keepdims=True)
    square = jnp.mean(values * values, axis=-1, keepdims=True)
    return (values - mean) * lax.rsqrt(square - mean * mean + EPS)


def dot(left, right):
    return jnp.dot(left, right, preferred_element_type=f32)


def dot_t(left, right):
    return lax.dot_general(left, right, (((1,), (1,)), ((), ())), preferred_element_type=f32)


def params():
    return pltpu.CompilerParams(vmem_limit_bytes=VMEM)


def cost(micros):
    return pl.CostEstimate(flops=0, bytes_accessed=int(micros * 3_400_000), transcendentals=0)


def project_kernel(place, acts, cond, scale, shift, w, keep, send, wcat):
    first = place[0] == 0

    @pl.when(pl.program_id(0) == 0)
    def _():
        low = [w[n][:, :DH] for n in range(4)]
        high = [w[n][:, DH:] for n in range(4)]
        kept = [jnp.where(first, low[n], high[n]) for n in (1, 2, 0, 3)]
        sent = [jnp.where(first, high[n], low[n]) for n in (1, 2, 0, 3)]
        wcat[...] = jnp.concatenate(kept + sent, axis=1)

    rows = GROUP * acts.shape[1]
    x = acts[...].reshape(rows, acts.shape[2]).astype(f32)
    c = normalize(cond[...].reshape(rows, cond.shape[2]).astype(f32)).astype(bf16)
    a = (jax.nn.sigmoid(dot(c, scale[...])) * normalize(x) + dot(c, shift[...])).astype(bf16)
    y = dot(a, wcat[...])
    lane = lax.broadcasted_iota(jnp.int32, (1, WIDE), 1) % (2 * PIECE)
    is_query = (lane >= PIECE) & (lane < PIECE + DH)
    y = (y * jnp.where(is_query, LOG2E / math.sqrt(DH), 1.0)).astype(bf16)
    step = acts.shape[1]
    for n, out in enumerate((keep, send)):
        for part in range(2):
            at = (2 * n + part) * PIECE
            out[part] = jnp.concatenate(
                [y[j * step : (j + 1) * step, at : at + PIECE] for j in range(GROUP)], axis=1
            )


def project(core, acts, cond, scale, shift, w):
    samples, rows, width = acts.shape
    groups = samples // GROUP
    out = jax.ShapeDtypeStruct((2, rows, samples * PIECE), bf16)
    whole = lambda shape: pl.BlockSpec(shape, lambda g, p: (0,) * len(shape))
    return pl.pallas_call(
        project_kernel,
        grid_spec=pltpu.PrefetchScalarGridSpec(
            num_scalar_prefetch=1,
            grid=(groups,),
            in_specs=[
                pl.BlockSpec((GROUP, rows, width), lambda g, p: (g, 0, 0)),
                pl.BlockSpec((GROUP, rows, cond.shape[2]), lambda g, p: (g, 0, 0)),
                whole(scale.shape),
                whole(shift.shape),
                whole(w.shape),
            ],
            out_specs=[pl.BlockSpec((2, rows, WIDE), lambda g, p: (0, 0, g))] * 2,
            scratch_shapes=[pltpu.VMEM((width, WIDE), bf16)],
        ),
        out_shape=[out, out],
        compiler_params=params(),
        cost_estimate=cost(8),
        name="project",
    )(core, acts, cond, scale, shift, w)


def bias_kernel(pair, w, out, left, right):
    step = pl.program_id(0)
    heads = w.shape[0]
    rows = left.shape[0] // heads
    spare = jnp.zeros((heads, 256 - out.shape[1]), f32)
    for i in range(pair.shape[0]):
        x = normalize(pair[i].astype(f32)).astype(bf16)
        t = dot_t(w[...], x)
        at = pl.ds(step * pair.shape[0] + i, heads, stride=rows)
        left[at, :] = t[:, :128]
        right[at, :] = jnp.concatenate([t[:, 128:], spare], axis=1)

    @pl.when(step == pl.num_programs(0) - 1)
    def _():
        both = jnp.concatenate([left[...], right[...]], axis=1)
        out[...] = both[:, : out.shape[1]].astype(bf16)


def tile_bias(pair, w_bias):
    rows, keys, width = pair.shape
    heads = w_bias.shape[1]
    block = 8
    flat = pl.pallas_call(
        bias_kernel,
        grid=(rows // block,),
        in_specs=[
            pl.BlockSpec((block, keys, width), lambda g: (g, 0, 0)),
            pl.BlockSpec((heads, width), lambda g: (0, 0)),
        ],
        out_specs=pl.BlockSpec((heads * rows, keys), lambda g: (0, 0)),
        out_shape=jax.ShapeDtypeStruct((heads * rows, keys), bf16),
        scratch_shapes=[pltpu.VMEM((heads * rows, 128), f32)] * 2,
        compiler_params=params(),
        cost_estimate=cost(6),
        name="tile_bias",
    )(pair, w_bias.T)
    return flat.reshape(heads, rows, keys)


def assemble_kernel(place, tile_a, tile_b, chain_a, chain_b, chain_q, mask_a, mask_b, cb, out):
    n = pl.program_id(0)
    keys = tile_a.shape[3]
    total = 2 * keys
    low = place[10] == 0

    def rows_of(tile):
        parts = []
        for k in range(2):
            both = tile[0, k].astype(f32)
            mine, theirs = both[: keys // 4], both[keys // 4 :]
            parts += [jnp.where(low, mine, theirs), jnp.where(low, theirs, mine)]
        return jnp.concatenate(parts, axis=0)

    bias = jnp.concatenate([rows_of(tile_a), rows_of(tile_b)], axis=1)
    chain_k = jnp.concatenate([chain_a[0], chain_b[0]], axis=1)
    mask_k = jnp.concatenate([mask_a[0], mask_b[0]], axis=1)
    row = lax.broadcasted_iota(jnp.int32, (keys, keys), 0)
    col = lax.broadcasted_iota(jnp.int32, (keys, keys), 1)
    chain_rows = jnp.sum(
        jnp.where(row == col, chain_q[0].astype(f32), 0.0), axis=1, keepdims=True
    )
    lane = lax.broadcasted_iota(jnp.int32, (1, total), 1)
    position = jnp.where(lane < keys, place[n] * keys, place[4 + n] * keys - keys) + lane
    query = place[8] * keys + lax.broadcasted_iota(jnp.int32, (keys, 1), 0)
    strength = cb[place[9]]
    bias = bias + jnp.where(chain_rows == chain_k.astype(f32), strength, 0.0)
    active = (mask_k == 1) | (query == position)
    out[0] = jnp.where(active, bias * LOG2E, MASKED)


def assemble(place, tiles, chain_id, residue_mask, chain_bias):
    chunks, cores, rows, keys = tiles.shape
    tile = lambda f: pl.BlockSpec((1, cores, rows, keys), f)
    line = lambda f: pl.BlockSpec((1, 1, keys), f)
    at_a4, at_b4 = (lambda n, p: (p[n], 0, 0, 0)), (lambda n, p: (p[4 + n], 0, 0, 0))
    at_a3, at_b3 = (lambda n, p: (p[n], 0, 0)), (lambda n, p: (p[4 + n], 0, 0))
    at_q3 = lambda n, p: (p[8], 0, 0)
    chain = chain_id.reshape(chunks, 1, keys)
    mask = residue_mask.reshape(chunks, 1, keys)
    return pl.pallas_call(
        assemble_kernel,
        grid_spec=pltpu.PrefetchScalarGridSpec(
            num_scalar_prefetch=1,
            grid=(chunks // 2,),
            in_specs=[
                tile(at_a4),
                tile(at_b4),
                line(at_a3),
                line(at_b3),
                line(at_q3),
                line(at_a3),
                line(at_b3),
                pl.BlockSpec(memory_space=pltpu.SMEM),
            ],
            out_specs=pl.BlockSpec((1, keys, 2 * keys), lambda n, p: (n, 0, 0)),
        ),
        out_shape=jax.ShapeDtypeStruct((chunks // 2, keys, 2 * keys), f32),
        compiler_params=params(),
        cost_estimate=cost(4),
        name="assemble",
    )(place, tiles, tiles, chain, chain, chain, mask, mask, chain_bias)


def attend_kernel(start, last, halves, *refs):
    qg_ref, own_ref = refs[0], refs[1]
    key_refs, refs = refs[1 : 1 + halves], refs[1 + halves :]
    bias_ref, refs = refs[0], refs[1:]
    if not start:
        o_in, ml_in = refs[0], refs[1]
        refs = refs[2:]
    kv = jnp.concatenate([ref[...] for ref in key_refs], axis=0)
    qg = qg_ref[...]
    bias = bias_ref[0]
    rows = qg.shape[0]
    lane = lax.broadcasted_iota(jnp.int32, (1, WIDE), 1)
    ml_lane = lax.broadcasted_iota(jnp.int32, (1, 128), 1)
    o_tiles = [jnp.zeros((rows, 128), f32) for _ in range(3)]
    ml = jnp.zeros((rows, 128), f32)
    for j in range(GROUP):
        a, b = FIRST[j]
        here = lane[:, a:b]
        chosen = (here >= PIECE * j) & (here < PIECE * j + DH)
        q = jnp.where(chosen, qg[:, a:b], jnp.zeros((), bf16))
        s = dot_t(q, kv[:, a:b]) + bias
        top = jnp.max(s, axis=1, keepdims=True)
        if not start:
            top_old = ml_in[0][:, j : j + 1]
            top = jnp.maximum(top, top_old)
            alpha = jnp.exp2(top_old - top)
        p = jnp.exp2(s - top)
        total = jnp.sum(p, axis=1, keepdims=True)
        a, b = SECOND[j]
        o = dot(p.astype(bf16), kv[:, a:b])
        if not start:
            total = total + alpha * ml_in[0][:, GROUP + j : GROUP + j + 1]
            o = o + alpha * o_in[:, a:b]
        if last:
            out = refs[0]
            o = o / total * jax.nn.sigmoid(qg[:, a:b].astype(f32))
            shift = PIECE * j + DH - a
            if shift:
                o = pltpu.roll(o, (b - a) - shift, 1)
            o = o[:, :DH].astype(bf16)
            sample = pl.program_id(0) * GROUP + j
            part, inner = sample // 3, sample % 3
            size = rows // 4
            put = pl.ds(pl.multiple_of(inner * size, 16), size)
            for core in range(2):
                for half in range(2):
                    at = (core * 2 + half) * size
                    out[half * 8 + part * 2 + core, put, :] = o[at : at + size]
        else:
            for t in range(a // 128, b // 128):
                here = lane[:, 128 * t : 128 * t + 128]
                chosen = (here >= PIECE * j + DH) & (here < PIECE * j + PIECE)
                piece = o[:, 128 * t - a : 128 * t - a + 128]
                o_tiles[t] = jnp.where(chosen, piece, o_tiles[t])
            ml = jnp.where(ml_lane == j, top, ml)
            ml = jnp.where(ml_lane == GROUP + j, total, ml)
    if not last:
        o_out, ml_out = refs
        o_out[...] = jnp.concatenate(o_tiles, axis=1)
        ml_out[0] = ml


def attend(place, qg, parts, bias, pair, state, last):
    rows, width = qg.shape
    groups = width // WIDE
    start = state is None
    lanes = lambda n: pl.BlockSpec((n, WIDE), lambda g: (0, g))
    ml_spec = pl.BlockSpec((1, rows, 128), lambda g: (g, 0, 0))
    in_specs = [lanes(rows)] + [lanes(part.shape[0]) for part in parts]
    in_specs += [pl.BlockSpec((1,) + bias.shape[1:], lambda g: (pair, 0, 0))]
    args = [qg, *parts, bias]
    if not start:
        in_specs += [lanes(rows), ml_spec]
        args += list(state)
    if last:
        out_specs = pl.BlockSpec((16, 3 * rows // 4, DH), lambda g: (0, 0, 0))
        out_shape = jax.ShapeDtypeStruct((16, 3 * rows // 4, DH), bf16)
    else:
        out_specs = [lanes(rows), ml_spec]
        out_shape = [
            jax.ShapeDtypeStruct((rows, width), f32),
            jax.ShapeDtypeStruct((groups, rows, 128), f32),
        ]
    keys = sum(part.shape[0] for part in parts)
    return pl.pallas_call(
        functools.partial(attend_kernel, start, last, len(parts)),
        grid=(groups,),
        in_specs=in_specs,
        out_specs=out_specs,
        out_shape=out_shape,
        compiler_params=params(),
        cost_estimate=cost(7),
        name="attend_last" if last else "attend",
    )(*args)


def condition_kernel(place, cond, gates, scale, shift, out):
    rows = cond.shape[0] * cond.shape[1]
    width = cond.shape[2]
    c = normalize(cond[...].reshape(rows, width).astype(f32)).astype(bf16)
    gate = jnp.concatenate([gates[n % 4, n // 4] for n in range(8)], axis=0)
    out[0] = jax.nn.sigmoid(dot_t(c, gate[:, :width]))
    out[1] = jax.nn.sigmoid(dot(c, scale[...]))
    out[2] = dot(c, shift[...])
    out[3] = jax.nn.sigmoid(dot_t(c, gate[:, width:]))


def condition(place, cond, gathered, scale, shift):
    samples, rows, width = cond.shape
    model = scale.shape[1]
    take, size, share = samples // 4, rows // 2, model // 8
    at = gathered.shape[2] // share - 1
    return pl.pallas_call(
        condition_kernel,
        grid_spec=pltpu.PrefetchScalarGridSpec(
            num_scalar_prefetch=1,
            grid=(1,),
            in_specs=[
                pl.BlockSpec((take, size, width), lambda g, p: (p[2], p[1], 0)),
                pl.BlockSpec((4, 2, share, model), lambda g, p: (0, 0, at, 0)),
                pl.BlockSpec(scale.shape, lambda g, p: (0, 0)),
                pl.BlockSpec(shift.shape, lambda g, p: (0, 0)),
            ],
            out_specs=pl.BlockSpec((4, take * size, model), lambda g, p: (0, 0, 0)),
        ),
        out_shape=jax.ShapeDtypeStruct((4, take * size, model), f32),
        compiler_params=params(),
        cost_estimate=cost(4),
        name="condition",
    )(place, cond, gathered, scale, shift)


def transition_kernel(place, heads, acts, mix, w_out, mine, other, out, stream, inputs, acc):
    step = pl.program_id(0)
    first = place[0] == 0
    rows = stream.shape[0]

    @pl.when(step == 0)
    def _():
        x = jnp.concatenate(
            [heads[n] for n in range(heads.shape[0])], axis=1
        )
        s = acts[...].reshape(rows, acts.shape[2]).astype(f32) + mix[0] * dot(x, w_out[...])
        stream[...] = s
        inputs[...] = (mix[1] * normalize(s) + mix[2]).astype(bf16)
        acc[...] = jnp.zeros(acc.shape, f32)

    m, o = mine[0, 0], other[0, 0]
    half = m.shape[0] // 2
    low = half + half // 2
    x = inputs[...]
    a, b = dot_t(x, m[:half]), dot_t(x, o[:half])
    up, gate = jnp.where(first, a, b), jnp.where(first, b, a)
    hidden = (gate / (1.0 + jnp.exp(-gate)) * up).astype(bf16)
    md, od = m[half:low], o[half:low]
    down = jnp.concatenate([jnp.where(first, md, od), jnp.where(first, od, md)], axis=0)
    acc[...] += dot(hidden, down)

    @pl.when(step == pl.num_programs(0) - 1)
    def _():
        result = (stream[...] + mix[3] * acc[...]).astype(bf16)
        share = out.shape[2]
        for n in range(out.shape[0]):
            out[n] = result[:, n * share : (n + 1) * share]


def transition(place, heads, acts, mix, w_out, mine, other):
    samples, rows, width = acts.shape
    take, size = samples // 4, rows // 2
    block = pl.BlockSpec((1, 1) + mine.shape[2:], lambda g, p: (g // 2, g % 2, 0, 0))
    whole = lambda shape: pl.BlockSpec(shape, lambda g, p: (0,) * len(shape))
    return pl.pallas_call(
        transition_kernel,
        grid_spec=pltpu.PrefetchScalarGridSpec(
            num_scalar_prefetch=1,
            grid=(8,),
            in_specs=[
                whole(heads.shape),
                pl.BlockSpec((take, size, width), lambda g, p: (p[2], p[1], 0)),
                whole(mix.shape),
                whole(w_out.shape),
                block,
                block,
            ],
            out_specs=whole((8, take * size, width // 8)),
            scratch_shapes=[
                pltpu.VMEM((take * size, width), f32),
                pltpu.VMEM((take * size, width), bf16),
                pltpu.VMEM((take * size, width), f32),
            ],
        ),
        out_shape=jax.ShapeDtypeStruct((8, take * size, width // 8), bf16),
        compiler_params=params(),
        cost_estimate=cost(10),
        name="transition",
    )(place, heads, acts, mix, w_out, mine, other)


def per_device(
    acts,
    cond,
    pair,
    chain_id,
    residue_mask,
    w_bias,
    chain_bias,
    ada1_scale,
    ada1_shift,
    w_qkvg,
    w_out,
    out_gate1,
    ada2_scale,
    ada2_shift,
    w_up,
    w_down,
    out_gate2,
):
    z, core, xh, y, samp = (lax.axis_index(n) for n in ("z", "core", "xh", "y", "samp"))
    samples, rows, width = acts.shape
    swap = [(0, 1), (1, 0)]
    here = jnp.stack([core, xh, y]).astype(jnp.int32)

    def half_of(array, axis):
        size = array.shape[axis] // 2
        return lax.dynamic_slice_in_dim(array, core * size, size, axis)

    pack = jnp.concatenate(
        [
            lax.dynamic_index_in_dim(w_up, core, 0, keepdims=False).T,
            half_of(w_down, 0),
            jnp.concatenate([out_gate1.T, out_gate2.T], axis=1),
        ],
        axis=0,
    )
    far = lax.ppermute(pack, "xh", swap)

    tile = tile_bias(pair, w_bias)
    tile_other = lax.ppermute(tile, "samp", swap)

    keep, send = project(here, acts, cond, ada1_scale, ada1_shift, w_qkvg)
    send, tile_other = lax.optimization_barrier((send, tile_other))
    got = lax.ppermute(send, "core", swap)
    got, far = lax.optimization_barrier((got, far))
    lower = core == 0
    chip = jnp.concatenate(
        [jnp.where(lower, keep, got), jnp.where(lower, got, keep)], axis=1
    )
    chunk, qg = chip[0], chip[1]

    packs = jnp.where(xh == 0, jnp.stack([pack, far]), jnp.stack([far, pack]))
    mine = lax.all_gather(packs, "y", axis=0)

    tiles = jnp.concatenate([tile, tile_other], axis=1)
    tiles = lax.all_to_all(tiles, PLANE, split_axis=0, concat_axis=0, tiled=True)
    order = [(z + 8 - s) % 8 for s in (1, 2, 3, 8)] + [(z + s) % 8 for s in (1, 2, 3, 4)]
    place = jnp.stack(order + [z, core, samp]).astype(jnp.int32)
    tiles = tiles.reshape((8, 2) + tiles.shape[1:])
    bias = assemble(place, tiles, chain_id, residue_mask, chain_bias)

    up_ring = [(i, (i + 1) % 8) for i in range(8)]
    down_ring = [(i, (i + 7) % 8) for i in range(8)]
    half = chunk.shape[0] // 2
    right = left = chunk
    state = None
    for step in range(3):
        right = lax.ppermute(right, "z", up_ring)
        left = lax.ppermute(left, "z", down_ring)
        state = attend(place, qg, [right, left], bias, step, state, False)
    right = lax.ppermute(right[:half], "z", up_ring)
    left = lax.ppermute(left[half:], "z", down_ring)
    heads = attend(place, qg, [chunk, right, left], bias, 3, state, True)

    heads, mine = lax.optimization_barrier((heads, mine))
    other = lax.ppermute(mine, "core", swap)
    heads = lax.all_to_all(heads, PLANE, split_axis=0, concat_axis=0, tiled=True)
    mix = condition(here, cond, mine, ada2_scale, ada2_shift)
    out = transition(here, heads, acts, mix, w_out, mine, other)
    out = lax.all_to_all(out, COL, split_axis=0, concat_axis=0, tiled=True)
    out = out.reshape(2, 4, samples // 4, rows // 2, width // 8)
    return out.transpose(1, 2, 0, 3, 4).reshape(samples, rows, width // 8)


def solution(mesh):
    fine = Mesh(mesh.devices.reshape(8, 2, 2, 4, 2), ("z", "core", "xh", "y", "samp"))
    row = ("z", "core")
    in_specs = (
        P("samp", row, None),
        P("samp", row, None),
        P(row + ("samp",), COL, None),
        P(),
        P(),
        P(),
        P(COL),
        P(),
        P(),
        P(None, None, COL),
        P(),
        P(None, COL),
        P(),
        P(),
        P(None, None, COL),
        P(COL, None),
        P(None, COL),
    )
    return jax.shard_map(
        per_device,
        mesh=fine,
        in_specs=in_specs,
        out_specs=P("samp", row, COL),
        check_vma=False,
    )
```

time: 450 us -> 182 us (0.40)
  waiting for transfers between devices: 264 us -> 40.5 us
  Pallas kernels: 0 us -> 64.6 us
  matrix products: 55.3 us -> 0 us
  local copies, waits for them, and re-layouts: 52.5 us -> 10 us
  blocking collectives: 40.7 us -> 11.3 us
  starting transfers between devices: 8.58 us -> 36.8 us
  other arithmetic: 13.3 us -> 3.86 us
    all_gather x4 -> x1, waiting for transfers between devices: 178 us -> 0.01 us  [per_device(): mine = lax.all_gather(packs, 'y', axis=0)]
    unnamed x6 -> x1, waiting for transfers between devices: 76.9 us -> 0.02 us
    pallas_call x0 -> x9, Pallas kernels: none -> 64.6 us  [the longest x4 29.5 us: attend(): pl.pallas_call(functools.partial(attend_kernel, start, last, len(parts)),...]
    dot_general x13 -> x0, matrix products: 37.5 us -> none  [the longest x3 9.92 us: attend(): jnp.einsum('shij,sjhd->sihd', weights, value_heads, preferred_element_typ...]
    psum x1 -> x0, blocking collectives: 30.4 us -> none  [per_device(): lax.psum((jnp.sum(stream, axis=-1), jnp.sum(stream * stream, axis=-1)), '...]
    ppermute x0 -> x12, waiting for transfers between devices: none -> 24.5 us  [the longest x3 14.9 us: per_device(): left = lax.ppermute(left, 'z', down_ring)]
    ppermute x0 -> x12, starting transfers between devices: none -> 21.7 us  [the longest x3 12.5 us: per_device(): left = lax.ppermute(left, 'z', down_ring)]
    unnamed x42 -> x35, local copies, waits for them, and re-layouts: 24.9 us -> 3.93 us
  transfers between devices with their start and end apart: 6 -> 15, of which waited for: 6 -> 5; matrix products, arithmetic and copies ran while one was open for 5% -> 5% of each run, Pallas kernels for 0% -> 26%
where the time goes in v1:
time: 182 us; the launch traced here: 181 us
  Pallas kernels  64.6 us (35%)
  waiting for transfers between devices  40.5 us (22%)
  starting transfers between devices  36.8 us (20%)
  between operations  13.7 us (8%)
  blocking collectives  11.3 us (6%)
  local copies, waits for them, and re-layouts  10 us (5%)
  other arithmetic  3.86 us (2%)
    pallas_call x4, Pallas kernels, attend(): pl.pallas_call(functools.partial(attend_kernel, start, last, len(parts)),...  29.5 us
    ppermute x3, waiting for transfers between devices, per_device(): left = lax.ppermute(left, 'z', down_ring)  14.9 us
    ppermute x3, starting transfers between devices, per_device(): left = lax.ppermute(left, 'z', down_ring)  12.5 us
    pallas_call x1, Pallas kernels, transition(): pl.pallas_call(transition_kernel, grid_spec=pltpu.PrefetchScalarGridSpec(...  11.4 us
    all_to_all x1, blocking collectives, per_device(): out = lax.all_to_all(out, COL, split_axis=0, concat_axis=0, tiled=True)  11.3 us
    all_to_all x1, waiting for transfers between devices, per_device(): lax.all_to_all(tiles, PLANE, split_axis=0, concat_axis=0, tiled=True)  10.4 us
    ppermute x1, waiting for transfers between devices, per_device(): far = lax.ppermute(pack, 'xh', swap)  9.54 us
    all_to_all x1, starting transfers between devices, per_device(): lax.all_to_all(tiles, PLANE, split_axis=0, concat_axis=0, tiled=True)  8.53 us
  transfers between devices with their start and end apart: 15, of which 5 were waited for; matrix products, arithmetic and copies ran while one was open for 5% of the time, Pallas kernels for 26%

profile of v1, /device:TPU:1, one launch (start us, length us, event | category | flops | bytes accessed | tf_op | source)
XLA Modules:
  0.0 180.8 jit_solution(5559157341663153309)
XLA Ops:
  6.6 6.5 %tile_bias.1 = bf16[768,192]{1,0:T(8,128)(2,1)} custom-call(bf16[48,192,128]{2,1,0:T(8,128)(2,1)} %pair.1, bf16[16,128]{1,0:T(8,128)(2,1)} %bitcast.41), custom_call_target="tpu_custom_call" | custom-call | bytes 20400000 | tf_op jit(solution)/shard_map/tile_bias/pallas_call | solution.py:128
  13.0 2.0 %collective-permute-start = (bf16[16,48,192]{2,1,0:T(8,128)(2,1)}, bf16[16,48,192]{2,1,0:T(8,128)(2,1)S(1)}, u32[]{:S(2)}, u32[]{:S(2)}) collective-permute-start(bf16[16,48,192]{2,1,0:T(8,128)(2,1)} %bitcast.35), channel_id=1, source_target_pairs={{0,1},{1,0},{2,3},{3,2},{4,5},{5,4},{6,7},{7,6},{8,9},{9,8},{10,11... | collective-permute-start | bytes 884744 | tf_op jit(solution)/shard_map/ppermute | solution.py:446
  15.1 0.0 copy-start.6
  15.2 0.1 fusion.3
  15.3 2.5 %collective-permute-start.2 = (bf16[384,768]{1,0:T(8,128)(2,1)S(1)}, bf16[384,768]{1,0:T(8,128)(2,1)S(1)}, u32[]{:S(2)}, u32[]{:S(2)}) collective-permute-start(bf16[384,768]{1,0:T(8,128)(2,1)S(1)} %get-tuple-element.38), channel_id=1, source_target_pairs={{0,8},{8,0},{1,9},{9,1},{2,10},{10,2},{3,11},{11,3},{4,12},{12,4},... | collective-permute-start | bytes 1769480 | tf_op jit(solution)/shard_map/ppermute | solution.py:443
  17.8 1.2 copy.20.w
  19.0 0.6 pad_add_fusion.place
  19.5 8.5 %project.1 = (bf16[2,96,1152]{2,1,0:T(8,128)(2,1)}, bf16[2,96,1152]{2,1,0:T(8,128)(2,1)}) custom-call(s32[3]{0:T(128)} %pad_add_fusion.place, bf16[12,96,768]{2,1,0:T(8,128)(2,1)} %acts.3, bf16[12,96,384]{2,1,0:T(8,128)(2,1)} %cond.3, bf16[384,768]{1,0:T(8,128)(2,1)} %scale.2, bf16[384,768]{1,0:T(8,128)(2,1)} %shift.2, bf16[4,768,96]{2,1,0:T(8,128)(2,1)} %copy.20.w), custom_call_target="tpu_custom_call" | custom-call | bytes 27200000 | tf_op jit(solution)/shard_map/project/pallas_call | solution.py:84
  28.0 1.3 collective-permute-start.1
  29.3 9.5 %collective-permute-done.2 = bf16[384,768]{1,0:T(8,128)(2,1)S(1)} collective-permute-done((bf16[384,768]{1,0:T(8,128)(2,1)S(1)}, bf16[384,768]{1,0:T(8,128)(2,1)S(1)}, u32[]{:S(2)}, u32[]{:S(2)}) %collective-permute-start.2) | collective-permute-done | bytes 589856 | tf_op jit(solution)/shard_map/ppermute | solution.py:443
  38.9 0.0 collective-permute-done.1
  38.9 1.2 maximum_select_fusion
  40.1 0.0 all-gather.2.cloned.1.call-update
  40.2 1.0 copy-done.9
  41.2 0.1 broadcast_select_fusion
  41.3 0.8 fusion.2
  42.1 5.6 %collective-permute-start.7 = (bf16[192,1152]{1,0:T(8,128)(2,1)S(1)}, bf16[192,1152]{1,0:T(8,128)(2,1)S(1)}, u32[]{:S(2)}, u32[]{:S(2)}) collective-permute-start(bf16[192,1152]{1,0:T(8,128)(2,1)S(1)} %get-tuple-element.33.refs_1_), channel_id=1, source_target_pairs={{0,224},{32,0},{64,32},{96,64},{128,96},{160,128},{192,160},{224,1... | collective-permute-start | bytes 1327112 | tf_op jit(solution)/shard_map/ppermute | solution.py:475
  47.7 0.0 collective-permute-start.3
  47.7 7.9 %collective-permute-done.7.refs_2_ = bf16[192,1152]{1,0:T(8,128)(2,1)S(1)} collective-permute-done((bf16[192,1152]{1,0:T(8,128)(2,1)S(1)}, bf16[192,1152]{1,0:T(8,128)(2,1)S(1)}, u32[]{:S(2)}, u32[]{:S(2)}) %collective-permute-start.7) | collective-permute-done | bytes 442400 | tf_op jit(solution)/shard_map/ppermute | solution.py:475
  55.6 3.4 %collective-permute-start.8 = (bf16[192,1152]{1,0:T(8,128)(2,1)S(1)}, bf16[192,1152]{1,0:T(8,128)(2,1)}, u32[]{:S(2)}, u32[]{:S(2)}) collective-permute-start(bf16[192,1152]{1,0:T(8,128)(2,1)S(1)} %collective-permute-done.7.refs_2_), channel_id=1, source_target_pairs={{0,224},{32,0},{64,32},{96,64},{128,96},{160,128},{192,160},{224,1... | collective-permute-start | bytes 1327112 | tf_op jit(solution)/shard_map/ppermute | solution.py:475
  59.0 7.0 %collective-permute-done.8.refs_2_ = bf16[192,1152]{1,0:T(8,128)(2,1)} collective-permute-done((bf16[192,1152]{1,0:T(8,128)(2,1)S(1)}, bf16[192,1152]{1,0:T(8,128)(2,1)}, u32[]{:S(2)}, u32[]{:S(2)}) %collective-permute-start.8) | collective-permute-done | bytes 442400 | tf_op jit(solution)/shard_map/ppermute | solution.py:475
  66.0 3.5 %collective-permute-start.9 = (bf16[192,1152]{1,0:T(8,128)(2,1)}, bf16[192,1152]{1,0:T(8,128)(2,1)S(1)}, u32[]{:S(2)}, u32[]{:S(2)}) collective-permute-start(bf16[192,1152]{1,0:T(8,128)(2,1)} %collective-permute-done.8.refs_2_), channel_id=1, source_target_pairs={{0,224},{32,0},{64,32},{96,64},{128,96},{160,128},{192,160},{224,1... | collective-permute-start | bytes 1327112 | tf_op jit(solution)/shard_map/ppermute | solution.py:475
  69.5 0.0 collective-permute-done.4.refs_1_
  69.5 1.1 pad_maximum_fusion
  70.6 8.5 %all-to-all-start = ((bf16[16,96,192]{2,1,0:T(8,128)(2,1)}), bf16[16,96,192]{2,1,0:T(8,128)(2,1)S(1)}, u32[]{:S(2)}, u32[]{:S(2)}) async-start(bf16[16,96,192]{2,1,0:T(8,128)(2,1)} %pad_maximum_fusion), calls=%async_computation | async-start | bytes 1572864 | tf_op jit(solution)/shard_map/all_to_all | solution.py:462
  79.1 0.0 collective-permute-done.9.refs_2_
  79.2 3.0 %collective-permute-start.10 = (bf16[96,1152]{1,0:T(8,128)(2,1)S(1)}, bf16[96,1152]{1,0:T(8,128)(2,1)S(1)}, u32[]{:S(2)}, u32[]{:S(2)}) collective-permute-start(bf16[96,1152]{1,0:T(8,128)(2,1)S(1)} %slice.19), channel_id=1, source_target_pairs={{0,224},{32,0},{64,32},{96,64},{128,96},{160,128},{192,160},{224,1... | collective-permute-start | bytes 663560 | tf_op jit(solution)/shard_map/ppermute | solution.py:478
  82.2 0.3 collective-permute-start.6
  82.6 0.7 reshape.79.chain_a.chain_b.chain_q
  83.2 0.7 reshape.80.mask_a.mask_b
  83.9 0.7 stack.74.place
  84.6 10.4 %all-to-all-done = bf16[16,96,192]{2,1,0:T(8,128)(2,1)S(1)} async-done(((bf16[16,96,192]{2,1,0:T(8,128)(2,1)}), bf16[16,96,192]{2,1,0:T(8,128)(2,1)S(1)}, u32[]{:S(2)}, u32[]{:S(2)}) %all-to-all-start) | async-done | bytes 589856 | tf_op jit(solution)/shard_map/all_to_all | solution.py:462
  95.0 0.9 copy-done.1
  96.0 4.5 %assemble.1.refs_3_.refs_4_ = f32[4,192,384]{2,1,0:T(8,128)} custom-call(s32[11]{0:T(128)} %stack.74.place, bf16[8,2,96,192]{3,2,1,0:T(8,128)(2,1)} %bitcast.33, bf16[8,2,96,192]{3,2,1,0:T(8,128)(2,1)} %bitcast.34, s32[8,1,192]{2,1,0:T(1,128)} %reshape.79.chain_a.chain_b.chain_q, s32[8,1,192]{2,1,0:T(1,128)} %reshape.79.chain_a.chain_b.chain_q, ...), custom_call_target="tpu_custom_call" | custom-call | bytes 13600000 | tf_op jit(solution)/shard_map/assemble/pallas_call | solution.py:185
  100.5 5.4 %attend.3 = (f32[192,1152]{1,0:T(8,128)}, f32[3,192,128]{2,1,0:T(8,128)}) custom-call(bf16[192,1152]{1,0:T(8,128)(2,1)} %get-tuple-element.34.refs_0_, bf16[192,1152]{1,0:T(8,128)(2,1)} %copy-done.8, bf16[192,1152]{1,0:T(8,128)(2,1)} %copy-done.7, f32[4,192,384]{2,1,0:T(8,128)} %assemble.1.refs_3_.refs_4_), custom_call_target="tpu_custom_call" | custom-call | bytes 23800000 | tf_op jit(solution)/shard_map/attend/pallas_call | solution.py:293
  105.9 7.8 %attend.4 = (f32[192,1152]{1,0:T(8,128)}, f32[3,192,128]{2,1,0:T(8,128)}) custom-call(bf16[192,1152]{1,0:T(8,128)(2,1)} %get-tuple-element.34.refs_0_, bf16[192,1152]{1,0:T(8,128)(2,1)} %collective-permute-done.4.refs_1_, bf16[192,1152]{1,0:T(8,128)(2,1)} %collective-permute-done.8.refs_2_, f32[4,192,384]{2,1,0:T(8,128)} %assemble.1.refs_3_.refs_4_, ...), custom_call_target="tpu_custom_call" | custom-call | bytes 23800000 | tf_op jit(solution)/shard_map/attend/pallas_call | solution.py:293
  113.7 7.8 %attend.5 = (f32[192,1152]{1,0:T(8,128)}, f32[3,192,128]{2,1,0:T(8,128)}) custom-call(bf16[192,1152]{1,0:T(8,128)(2,1)} %get-tuple-element.34.refs_0_, bf16[192,1152]{1,0:T(8,128)(2,1)} %copy-done.5, bf16[192,1152]{1,0:T(8,128)(2,1)} %copy-done.4, f32[4,192,384]{2,1,0:T(8,128)} %assemble.1.refs_3_.refs_4_, f32[192,1152]{1,0:T(8,128)} %get-tuple-element.26.refs_4_, ...), custom_call_target="tpu_custom_call" | custom-call | bytes 23800000 | tf_op jit(solution)/shard_map/attend/pallas_call | solution.py:293
  121.5 0.7 copy-done.10
  122.2 0.1 copy-done.11
  122.3 8.5 %attend_last.1 = bf16[16,144,48]{2,1,0:T(8,128)(2,1)} custom-call(bf16[192,1152]{1,0:T(8,128)(2,1)} %get-tuple-element.34.refs_0_, bf16[192,1152]{1,0:T(8,128)(2,1)} %copy-done.2, bf16[96,1152]{1,0:T(8,128)(2,1)} %copy-done.11, bf16[96,1152]{1,0:T(8,128)(2,1)} %copy-done.10, f32[4,192,384]{2,1,0:T(8,128)} %assemble.1.refs_3_.refs_4_, ...), custom_call_target="tpu_custom_call" | custom-call | bytes 23800000 | tf_op jit(solution)/shard_map/attend_last/pallas_call | solution.py:293
  130.8 2.1 %copy.21 = bf16[16,144,48]{1,2,0:T(8,128)(2,1)} copy(bf16[16,144,48]{2,1,0:T(8,128)(2,1)} %attend_last.1) | data formatting | bytes 442368 | tf_op jit(solution)/shard_map/optimization_barrier | solution.py:481
  132.9 6.6 %all-to-all-start.1 = ((bf16[16,144,48]{1,2,0:T(8,128)(2,1)}), bf16[16,144,48]{1,2,0:T(8,128)(2,1)S(1)}, u32[]{:S(2)}, u32[]{:S(2)}) async-start(bf16[16,144,48]{1,2,0:T(8,128)(2,1)} %copy.21), calls=%async_computation.1 | async-start | bytes 786432 | tf_op jit(solution)/shard_map/all_to_all | solution.py:483
  139.5 4.3 %condition.1.mix = f32[4,144,768]{2,1,0:T(8,128)} custom-call(s32[3]{0:T(128)} %pad_add_fusion.place, bf16[12,96,384]{2,1,0:T(8,128)(2,1)} %cond.3, bf16[4,2,384,768]{3,2,1,0:T(8,128)(2,1)} %all-gather.2.cloned.1.call-done.gates.mine, bf16[384,768]{1,0:T(8,128)(2,1)} %scale.3, bf16[384,768]{1,0:T(8,128)(2,1)} %shift.3), custom_call_target="tpu_custom_call" | custom-call | bytes 13600000 | tf_op jit(solution)/shard_map/condition/pallas_call | solution.py:321
  143.8 5.6 %all-to-all-done.1 = bf16[16,144,48]{1,2,0:T(8,128)(2,1)S(1)} async-done(((bf16[16,144,48]{1,2,0:T(8,128)(2,1)}), bf16[16,144,48]{1,2,0:T(8,128)(2,1)S(1)}, u32[]{:S(2)}, u32[]{:S(2)}) %all-to-all-start.1) | async-done | bytes 221216 | tf_op jit(solution)/shard_map/all_to_all | solution.py:483
  149.4 1.1 copy.22.heads
  150.5 11.4 %transition.1 = bf16[8,144,96]{2,1,0:T(8,128)(2,1)} custom-call(s32[3]{0:T(128)} %pad_add_fusion.place, bf16[16,144,48]{2,1,0:T(8,128)(2,1)} %copy.22.heads, bf16[12,96,768]{2,1,0:T(8,128)(2,1)} %acts.3, f32[4,144,768]{2,1,0:T(8,128)} %condition.1.mix, bf16[768,768]{1,0:T(8,128)(2,1)} %w_out.1, ...), custom_call_target="tpu_custom_call" | custom-call | bytes 34000000 | tf_op jit(solution)/shard_map/transition/pallas_call | solution.py:380
  161.9 11.3 %all_to_all.15 = bf16[8,144,96]{2,1,0:T(8,128)(2,1)S(1)} all-to-all(bf16[8,144,96]{2,1,0:T(8,128)(2,1)} %transition.1), channel_id=1, replica_groups=mesh['z'=8,'core'=2,'xh'=2,'y'=4,'samp'=2] {'xh','y'}, dimensions={0} | all-to-all | bytes 442368 | tf_op jit(solution)/shard_map/all_to_all | solution.py:486
  173.2 0.7 copy.23
  (44 shorter events, 0.2 us)
Async XLA Ops:
  6.5 8.5 %copy-start = (bf16[2,768,192]{1,2,0:T(8,128)(2,1)S(1)}, bf16[2,768,192]{1,2,0:T(8,128)(2,1)}, u32[]{:S(2)}) copy-start(bf16[2,768,192]{1,2,0:T(8,128)(2,1)} %param.31) | copy-start | bytes 1769476
  6.5 124.3 %all-gather.2.cloned.1.call-start = ((), (), s32[]{:S(2)}) async-start(), calls=%async_computation.3 | async-start | bytes 5898240 | tf_op jit(solution)/shard_map/all_gather | solution.py:459
  6.5 8.6 %copy-start.14 = (bf16[192,768]{1,0:T(8,128)(2,1)S(1)}, bf16[192,768]{1,0:T(8,128)(2,1)}, u32[]{:S(2)}) copy-start(bf16[192,768]{1,0:T(8,128)(2,1)} %param.32) | copy-start | bytes 884740
  6.5 8.6 %copy-start.12 = (bf16[384,96]{0,1:T(8,128)(2,1)S(1)}, bf16[384,96]{0,1:T(8,128)(2,1)}, u32[]{:S(2)}) copy-start(bf16[384,96]{0,1:T(8,128)(2,1)} %param.33) | copy-start | bytes 221188
  6.5 8.6 %copy-start.13 = (bf16[384,96]{0,1:T(8,128)(2,1)S(1)}, bf16[384,96]{0,1:T(8,128)(2,1)}, u32[]{:S(2)}) copy-start(bf16[384,96]{0,1:T(8,128)(2,1)} %param.28) | copy-start | bytes 221188
  13.0 15.0 %collective-permute-start = (bf16[16,48,192]{2,1,0:T(8,128)(2,1)}, bf16[16,48,192]{2,1,0:T(8,128)(2,1)S(1)}, u32[]{:S(2)}, u32[]{:S(2)}) collective-permute-start(bf16[16,48,192]{2,1,0:T(8,128)(2,1)} %bitcast.35), channel_id=1, source_target_pairs={{0,1},{1,0},{2,3},{3,2},{4,5},{5,4},{6,7},{7,6},{8,9},{9,8},{10,11... | collective-permute-start | bytes 884744 | tf_op jit(solution)/shard_map/ppermute | solution.py:446
  15.1 2.7 %copy-start.6 = (bf16[4,768,96]{1,2,0:T(8,128)(2,1)S(1)}, bf16[4,768,96]{1,2,0:T(8,128)(2,1)}, u32[]{:S(2)}) copy-start(bf16[4,768,96]{1,2,0:T(8,128)(2,1)} %param.26) | copy-start | bytes 1769476
  15.3 23.6 %collective-permute-start.2 = (bf16[384,768]{1,0:T(8,128)(2,1)S(1)}, bf16[384,768]{1,0:T(8,128)(2,1)S(1)}, u32[]{:S(2)}, u32[]{:S(2)}) collective-permute-start(bf16[384,768]{1,0:T(8,128)(2,1)S(1)} %get-tuple-element.38), channel_id=1, source_target_pairs={{0,8},{8,0},{1,9},{9,1},{2,10},{10,2},{3,11},{11,3},{4,12},{12,4},... | collective-permute-start | bytes 1769480 | tf_op jit(solution)/shard_map/ppermute | solution.py:443
  28.0 10.9 %collective-permute-start.1 = (bf16[2,96,1152]{2,1,0:T(8,128)(2,1)}, bf16[2,96,1152]{2,1,0:T(8,128)(2,1)S(1)}, u32[]{:S(2)}, u32[]{:S(2)}) collective-permute-start(bf16[2,96,1152]{2,1,0:T(8,128)(2,1)} %get-tuple-element.21), channel_id=1, source_target_pairs={{0,16},{16,0},{1,17},{17,1},{2,18},{18,2},{3,19},{19,3},{4,20},{20... | collective-permute-start | bytes 1327112 | tf_op jit(solution)/shard_map/ppermute | solution.py:450
  40.1 1.0 copy-start.9
  41.2 28.3 %copy-start.3 = (bf16[768,192]{1,0:T(8,128)(2,1)S(1)}, bf16[768,192]{1,0:T(8,128)(2,1)}, u32[]{:S(2)}) copy-start(bf16[768,192]{1,0:T(8,128)(2,1)} %tile_bias.1) | copy-start | bytes 884740
  42.1 28.5 %copy-start.2 = (bf16[192,1152]{1,0:T(8,128)(2,1)}, bf16[192,1152]{1,0:T(8,128)(2,1)S(1)}, u32[]{:S(2)}) copy-start(bf16[192,1152]{1,0:T(8,128)(2,1)S(1)} %get-tuple-element.33.refs_1_) | copy-start | bytes 1327108
  42.1 13.5 %collective-permute-start.7 = (bf16[192,1152]{1,0:T(8,128)(2,1)S(1)}, bf16[192,1152]{1,0:T(8,128)(2,1)S(1)}, u32[]{:S(2)}, u32[]{:S(2)}) collective-permute-start(bf16[192,1152]{1,0:T(8,128)(2,1)S(1)} %get-tuple-element.33.refs_1_), channel_id=1, source_target_pairs={{0,224},{32,0},{64,32},{96,64},{128,96},{160,128},{192,160},{224,1... | collective-permute-start | bytes 1327112 | tf_op jit(solution)/shard_map/ppermute | solution.py:475
  47.7 11.3 %collective-permute-start.3 = (bf16[192,1152]{1,0:T(8,128)(2,1)S(1)}, bf16[192,1152]{1,0:T(8,128)(2,1)S(1)}, u32[]{:S(2)}, u32[]{:S(2)}) collective-permute-start(bf16[192,1152]{1,0:T(8,128)(2,1)S(1)} %get-tuple-element.33.refs_1_), channel_id=1, source_target_pairs={{0,32},{32,64},{64,96},{96,128},{128,160},{160,192},{192,224},{224... | collective-permute-start | bytes 1327112 | tf_op jit(solution)/shard_map/ppermute | solution.py:474
  55.6 15.0 %copy-start.7 = (bf16[192,1152]{1,0:T(8,128)(2,1)}, bf16[192,1152]{1,0:T(8,128)(2,1)S(1)}, u32[]{:S(2)}) copy-start(bf16[192,1152]{1,0:T(8,128)(2,1)S(1)} %collective-permute-done.7.refs_2_) | copy-start | bytes 1327108
  55.6 10.4 %collective-permute-start.8 = (bf16[192,1152]{1,0:T(8,128)(2,1)S(1)}, bf16[192,1152]{1,0:T(8,128)(2,1)}, u32[]{:S(2)}, u32[]{:S(2)}) collective-permute-start(bf16[192,1152]{1,0:T(8,128)(2,1)S(1)} %collective-permute-done.7.refs_2_), channel_id=1, source_target_pairs={{0,224},{32,0},{64,32},{96,64},{128,96},{160,128},{192,160},{224,1... | collective-permute-start | bytes 1327112 | tf_op jit(solution)/shard_map/ppermute | solution.py:475
  59.0 10.5 %copy-start.8 = (bf16[192,1152]{1,0:T(8,128)(2,1)}, bf16[192,1152]{1,0:T(8,128)(2,1)S(1)}, u32[]{:S(2)}) copy-start(bf16[192,1152]{1,0:T(8,128)(2,1)S(1)} %collective-permute-done.3.refs_1_) | copy-start | bytes 1327108
  59.0 10.5 %collective-permute-start.4 = (bf16[192,1152]{1,0:T(8,128)(2,1)S(1)}, bf16[192,1152]{1,0:T(8,128)(2,1)}, u32[]{:S(2)}, u32[]{:S(2)}) collective-permute-start(bf16[192,1152]{1,0:T(8,128)(2,1)S(1)} %collective-permute-done.3.refs_1_), channel_id=1, source_target_pairs={{0,32},{32,64},{64,96},{96,128},{128,160},{160,192},{192,224},{224... | collective-permute-start | bytes 1327112 | tf_op jit(solution)/shard_map/ppermute | solution.py:474
  66.0 13.1 %collective-permute-start.9 = (bf16[192,1152]{1,0:T(8,128)(2,1)}, bf16[192,1152]{1,0:T(8,128)(2,1)S(1)}, u32[]{:S(2)}, u32[]{:S(2)}) collective-permute-start(bf16[192,1152]{1,0:T(8,128)(2,1)} %collective-permute-done.8.refs_2_), channel_id=1, source_target_pairs={{0,224},{32,0},{64,32},{96,64},{128,96},{160,128},{192,160},{224,1... | collective-permute-start | bytes 1327112 | tf_op jit(solution)/shard_map/ppermute | solution.py:475
  69.5 12.7 %collective-permute-start.5 = (bf16[192,1152]{1,0:T(8,128)(2,1)}, bf16[192,1152]{1,0:T(8,128)(2,1)S(1)}, u32[]{:S(2)}, u32[]{:S(2)}) collective-permute-start(bf16[192,1152]{1,0:T(8,128)(2,1)} %collective-permute-done.4.refs_1_), channel_id=1, source_target_pairs={{0,32},{32,64},{64,96},{96,128},{128,160},{160,192},{192,224},{224... | collective-permute-start | bytes 1327112 | tf_op jit(solution)/shard_map/ppermute | solution.py:474
  70.6 12.0 %copy-start.15 = (s32[1536]{0:T(1024)S(1)}, s32[1536]{0:T(1024)}, u32[]{:S(2)}) copy-start(s32[1536]{0:T(1024)} %param.20) | copy-start | bytes 18436
  70.6 12.7 %copy-start.16 = (s32[1536]{0:T(1024)S(1)}, s32[1536]{0:T(1024)}, u32[]{:S(2)}) copy-start(s32[1536]{0:T(1024)} %param.21) | copy-start | bytes 18436
  70.6 24.4 %all-to-all-start = ((bf16[16,96,192]{2,1,0:T(8,128)(2,1)}), bf16[16,96,192]{2,1,0:T(8,128)(2,1)S(1)}, u32[]{:S(2)}, u32[]{:S(2)}) async-start(bf16[16,96,192]{2,1,0:T(8,128)(2,1)} %pad_maximum_fusion), calls=%async_computation | async-start | bytes 1572864 | tf_op jit(solution)/shard_map/all_to_all | solution.py:462
  79.1 21.3 %copy-start.4 = (bf16[192,1152]{1,0:T(8,128)(2,1)}, bf16[192,1152]{1,0:T(8,128)(2,1)S(1)}, u32[]{:S(2)}) copy-start(bf16[192,1152]{1,0:T(8,128)(2,1)S(1)} %collective-permute-done.9.refs_2_) | copy-start | bytes 1327108
  79.2 42.3 %collective-permute-start.10 = (bf16[96,1152]{1,0:T(8,128)(2,1)S(1)}, bf16[96,1152]{1,0:T(8,128)(2,1)S(1)}, u32[]{:S(2)}, u32[]{:S(2)}) collective-permute-start(bf16[96,1152]{1,0:T(8,128)(2,1)S(1)} %slice.19), channel_id=1, source_target_pairs={{0,224},{32,0},{64,32},{96,64},{128,96},{160,128},{192,160},{224,1... | collective-permute-start | bytes 663560 | tf_op jit(solution)/shard_map/ppermute | solution.py:478
  82.2 18.3 %copy-start.5 = (bf16[192,1152]{1,0:T(8,128)(2,1)}, bf16[192,1152]{1,0:T(8,128)(2,1)S(1)}, u32[]{:S(2)}) copy-start(bf16[192,1152]{1,0:T(8,128)(2,1)S(1)} %collective-permute-done.5.refs_1_) | copy-start | bytes 1327108
  82.2 39.3 %collective-permute-start.6 = (bf16[96,1152]{1,0:T(8,128)(2,1)S(1)}, bf16[96,1152]{1,0:T(8,128)(2,1)S(1)}, u32[]{:S(2)}, u32[]{:S(2)}) collective-permute-start(bf16[96,1152]{1,0:T(8,128)(2,1)S(1)} %slice.18), channel_id=1, source_target_pairs={{0,32},{32,64},{64,96},{96,128},{128,160},{160,192},{192,224},{224... | collective-permute-start | bytes 663560 | tf_op jit(solution)/shard_map/ppermute | solution.py:477
  95.0 0.9 copy-start.1
  121.5 0.7 copy-start.10
  121.5 0.8 copy-start.11
  130.8 19.7 %collective-permute-start.11 = (bf16[4,2,384,768]{3,2,1,0:T(8,128)(2,1)}, bf16[4,2,384,768]{3,2,1,0:T(8,128)(2,1)}, u32[]{:S(2)}, u32[]{:S(2)}) collective-permute-start(bf16[4,2,384,768]{3,2,1,0:T(8,128)(2,1)} %all-gather.2.cloned.1.call-done.gates.mine), channel_id=1, source_target_pairs={{0,16},{16,0},{1,17},{17,1},{2,18},{18,2},{3,19},{19,3},{4,20},{20... | collective-permute-start | bytes 14155784 | tf_op jit(solution)/shard_map/ppermute | solution.py:482
  132.9 16.5 %all-to-all-start.1 = ((bf16[16,144,48]{1,2,0:T(8,128)(2,1)}), bf16[16,144,48]{1,2,0:T(8,128)(2,1)S(1)}, u32[]{:S(2)}, u32[]{:S(2)}) async-start(bf16[16,144,48]{1,2,0:T(8,128)(2,1)} %copy.21), calls=%async_computation.1 | async-start | bytes 786432 | tf_op jit(solution)/shard_map/all_to_all | solution.py:483
Sparse Core Ops, SparseCore 0:
  40.3 65.2 all-gather.1

commit v2 on v1

v2 whole, which is shorter than its diff:
```python
import functools
import math

import jax
import jax.numpy as jnp
from jax import lax
from jax.experimental import pallas as pl
from jax.experimental.pallas import tpu as pltpu
from jax.sharding import Mesh, PartitionSpec as P

DH = 48
PIECE = 2 * DH
GROUP = 4
WIDE = GROUP * PIECE
EPS = 1e-05
LOG2E = math.log2(math.e)
MASKED = -1000000000.0
COL = ("xh", "y")
PLANE = ("xh", "y", "core")
VMEM = 56 * 1024 * 1024

WINDOW = 256

f32 = jnp.float32
bf16 = jnp.bfloat16


def normalize(values):
    mean = jnp.mean(values, axis=-1, keepdims=True)
    square = jnp.mean(values * values, axis=-1, keepdims=True)
    return (values - mean) * lax.rsqrt(square - mean * mean + EPS)


def sigmoid(values):
    return 0.5 * jnp.tanh(0.5 * values) + 0.5


def dot(left, right):
    return jnp.dot(left, right, preferred_element_type=f32)


def dot_t(left, right):
    return lax.dot_general(left, right, (((1,), (1,)), ((), ())), preferred_element_type=f32)


def params():
    return pltpu.CompilerParams(vmem_limit_bytes=VMEM)


def cost(micros):
    return pl.CostEstimate(flops=0, bytes_accessed=int(micros * 3_400_000), transcendentals=0)


def project_kernel(place, acts, cond, scale, shift, w, keep, send, wcat):
    first = place[0] == 0

    @pl.when(pl.program_id(0) == 0)
    def _():
        low = [w[n, :DH] for n in range(4)]
        high = [w[n, DH:] for n in range(4)]
        kept = [jnp.where(first, low[n], high[n]) for n in (1, 2, 0, 3)]
        sent = [jnp.where(first, high[n], low[n]) for n in (1, 2, 0, 3)]
        wcat[...] = jnp.concatenate(kept + sent, axis=0)

    rows = GROUP * acts.shape[1]
    x = acts[...].reshape(rows, acts.shape[2]).astype(f32)
    c = normalize(cond[...].reshape(rows, cond.shape[2]).astype(f32)).astype(bf16)
    a = (sigmoid(dot(c, scale[...])) * normalize(x) + dot(c, shift[...])).astype(bf16)
    y = dot_t(a, wcat[...])
    lane = lax.broadcasted_iota(jnp.int32, (1, WIDE), 1) % (2 * PIECE)
    is_query = (lane >= PIECE) & (lane < PIECE + DH)
    y = (y * jnp.where(is_query, LOG2E / math.sqrt(DH), 1.0)).astype(bf16)
    step = acts.shape[1]
    for n, out in enumerate((keep, send)):
        for part in range(2):
            at = (2 * n + part) * PIECE
            out[part] = jnp.concatenate(
                [y[j * step : (j + 1) * step, at : at + PIECE] for j in range(GROUP)], axis=1
            )


def project(core, acts, cond, scale, shift, w):
    samples, rows, width = acts.shape
    groups = samples // GROUP
    out = jax.ShapeDtypeStruct((2, rows, samples * PIECE), bf16)
    whole = lambda shape: pl.BlockSpec(shape, lambda g, p: (0,) * len(shape))
    return pl.pallas_call(
        project_kernel,
        grid_spec=pltpu.PrefetchScalarGridSpec(
            num_scalar_prefetch=1,
            grid=(groups,),
            in_specs=[
                pl.BlockSpec((GROUP, rows, width), lambda g, p: (g, 0, 0)),
                pl.BlockSpec((GROUP, rows, cond.shape[2]), lambda g, p: (g, 0, 0)),
                whole(scale.shape),
                whole(shift.shape),
                whole(w.shape),
            ],
            out_specs=[pl.BlockSpec((2, rows, WIDE), lambda g, p: (0, 0, g))] * 2,
            scratch_shapes=[pltpu.VMEM((WIDE, width), bf16)],
        ),
        out_shape=[out, out],
        compiler_params=params(),
        cost_estimate=cost(8),
        name="project",
    )(core, acts, cond, scale, shift, w)


def bias_kernel(pair, w, out, left, right):
    step = pl.program_id(0)
    heads = w.shape[0]
    rows = left.shape[0] // heads
    spare = jnp.zeros((heads, 256 - out.shape[2]), f32)
    for i in range(pair.shape[0]):
        x = normalize(pair[i].astype(f32)).astype(bf16)
        t = dot_t(w[...], x)
        at = pl.ds(step * pair.shape[0] + i, heads, stride=rows)
        left[at, :] = t[:, :128]
        right[at, :] = jnp.concatenate([t[:, 128:], spare], axis=1)

    @pl.when(step == pl.num_programs(0) - 1)
    def _():
        both = jnp.concatenate([left[...], right[...]], axis=1)
        both = both[:, : out.shape[2]].astype(bf16)
        out[0] = both
        out[1] = both


def tile_bias(pair, w_bias):
    rows, keys, width = pair.shape
    heads = w_bias.shape[1]
    block = 8
    flat = pl.pallas_call(
        bias_kernel,
        grid=(rows // block,),
        in_specs=[
            pl.BlockSpec((block, keys, width), lambda g: (g, 0, 0)),
            pl.BlockSpec((heads, width), lambda g: (0, 0)),
        ],
        out_specs=pl.BlockSpec((2, heads * rows, keys), lambda g: (0, 0, 0)),
        out_shape=jax.ShapeDtypeStruct((2, heads * rows, keys), bf16),
        scratch_shapes=[pltpu.VMEM((heads * rows, 128), f32)] * 2,
        compiler_params=params(),
        cost_estimate=cost(6),
        name="tile_bias",
    )(pair, w_bias.T)
    return flat.reshape(2 * heads, rows, keys)


def assemble_kernel(place, *refs):
    tiles, chains, masks = refs[:2], refs[2:4], refs[4:6]
    chain_q, cb, out = refs[6:]
    keys = out.shape[1]
    row = lax.broadcasted_iota(jnp.int32, (keys, keys), 0)
    col = lax.broadcasted_iota(jnp.int32, (keys, keys), 1)

    def upright(line):
        return jnp.sum(jnp.where(row == col, line.astype(f32), 0.0), axis=1, keepdims=True)

    query = place[8] * keys + col
    for n in range(2):
        tile = tiles[n]
        parts = [tile[half, 0, core] for core in range(2) for half in range(2)]
        bias = jnp.concatenate(parts, axis=0).astype(f32).T
        same = upright(chains[n][0]) == chain_q[0].astype(f32)
        bias = bias + jnp.where(same, cb[place[9]], 0.0)
        key = place[2 * pl.program_id(0) + n] * keys + row
        active = (upright(masks[n][0]) == 1.0) | (query == key)
        bias = jnp.where(active, bias * LOG2E, MASKED)
        out[n] = jnp.concatenate([bias, bias], axis=1)


def assemble(place, tiles, chain_id, residue_mask, chain_bias):
    halves, chunks, cores, rows, keys = tiles.shape
    tile = [
        pl.BlockSpec((halves, 1, cores, rows, keys), lambda n, p, m=m: (0, p[2 * n + m], 0, 0, 0))
        for m in range(2)
    ]
    line = [pl.BlockSpec((1, 1, keys), lambda n, p, m=m: (p[2 * n + m], 0, 0)) for m in range(2)]
    own = pl.BlockSpec((1, 1, keys), lambda n, p: (p[8], 0, 0))
    chain = chain_id.reshape(chunks, 1, keys)
    mask = residue_mask.reshape(chunks, 1, keys)
    return pl.pallas_call(
        assemble_kernel,
        grid_spec=pltpu.PrefetchScalarGridSpec(
            num_scalar_prefetch=1,
            grid=(chunks // 2,),
            in_specs=tile + line + line + [own, pl.BlockSpec(memory_space=pltpu.SMEM)],
            out_specs=pl.BlockSpec((2, keys, 2 * keys), lambda n, p: (n, 0, 0)),
        ),
        out_shape=jax.ShapeDtypeStruct((chunks, keys, 2 * keys), f32),
        compiler_params=params(),
        cost_estimate=cost(5),
        name="assemble",
    )(place, tiles, tiles, chain, chain, mask, mask, chain, chain_bias)


def attend_kernel(start, last, halves, chunks, *refs):
    qg_ref, refs = refs[0], refs[1:]
    key_refs, refs = refs[:halves], refs[halves:]
    bias_refs, refs = refs[:chunks], refs[chunks:]
    if not start:
        state, refs = refs[0], refs[1:]
    out = refs[0]
    rows = qg_ref.shape[0]
    bias = jnp.concatenate([ref[0] for ref in bias_refs], axis=0)
    lane = lax.broadcasted_iota(jnp.int32, (1, WINDOW), 1)
    wide = lax.broadcasted_iota(jnp.int32, (1, 2 * rows), 1)
    row = lax.broadcasted_iota(jnp.int32, (2 * DH, 1), 0)
    none = jnp.zeros((), bf16)
    size = rows // 4
    pieces = {}
    for pair in range(2 * qg_ref.shape[1] // WIDE):
        a = pair // 2 * WIDE + 128 * (pair % 2)
        base = 2 * PIECE * pair - a
        group, at = pair // 2, pair % 2
        keys = jnp.concatenate([ref[:, a : a + WINDOW] for ref in key_refs], axis=0)
        queries = qg_ref[:, a : a + WINDOW]

        def both(offset):
            ends = [base + offset, base + offset + PIECE]
            return jnp.concatenate(
                [jnp.where((lane >= n) & (lane < n + DH), queries, none) for n in ends], axis=0
            )

        s = dot_t(keys, both(0)) + bias
        top = jnp.max(s, axis=0, keepdims=True)
        if not start:
            top_old = state[group, at, DH : DH + 1]
            top = jnp.maximum(top, top_old)
            alpha = jnp.exp2(top_old - top)
        p = jnp.exp2(s - top)
        total = jnp.sum(p, axis=0, keepdims=True)
        source = base + DH + jnp.where(row < DH, row, row + PIECE - DH)
        select = jnp.where(lane == source, 1.0, 0.0).astype(bf16)
        values = dot_t(select, keys).astype(bf16)
        o = dot(values, p.astype(bf16))
        o = jnp.where(wide < rows, o[:DH], o[DH:])
        if not start:
            total = total + alpha * state[group, at, DH + 1 : DH + 2]
            o = o + alpha * state[group, at, :DH]
        if last:
            fold = (lane == base + DH + row[:DH]) | (lane == base + DH + PIECE + row[:DH])
            gate = dot_t(jnp.where(fold, 1.0, 0.0).astype(bf16), both(DH))
            o = (o / total * sigmoid(gate)).astype(bf16)
            for j in range(2):
                for quarter in range(4):
                    begin = j * rows + quarter * size
                    pieces[2 * pair + j, quarter] = o[:, begin : begin + size]
        else:
            out[group, at, :DH] = o
            out[group, at, DH:] = jnp.concatenate(
                [top, total, jnp.zeros((6, 2 * rows), f32)], axis=0
            )
    if last:
        for part in range(4):
            for quarter in range(4):
                core, half = quarter // 2, quarter % 2
                out[half * 8 + part * 2 + core] = jnp.concatenate(
                    [pieces[3 * part + n, quarter] for n in range(3)], axis=1
                )


def attend(qg, parts, bias, at, state, last):
    rows, width = qg.shape
    groups = width // WIDE
    lanes = lambda n: pl.BlockSpec((n, width if last else WIDE), lambda g: (0, g))
    state_shape = (groups, 2, DH + 8, 2 * rows)
    state_spec = pl.BlockSpec((groups if last else 1,) + state_shape[1:], lambda g: (g, 0, 0, 0))
    chunks = sum(part.shape[0] for part in parts) // bias.shape[1]
    in_specs = [lanes(rows)] + [lanes(part.shape[0]) for part in parts]
    in_specs += [
        pl.BlockSpec((1,) + bias.shape[1:], lambda g, n=n: (at + n, 0, 0)) for n in range(chunks)
    ]
    args = [qg, *parts] + [bias] * chunks
    if state is not None:
        in_specs += [state_spec]
        args += [state]
    if last:
        out_shape = jax.ShapeDtypeStruct((16, DH, 3 * rows // 4), bf16)
        out_specs = pl.BlockSpec(out_shape.shape, lambda g: (0, 0, 0))
    else:
        out_specs = state_spec
        out_shape = jax.ShapeDtypeStruct(state_shape, f32)
    return pl.pallas_call(
        functools.partial(attend_kernel, state is None, last, len(parts), chunks),
        grid=(1 if last else groups,),
        in_specs=in_specs,
        out_specs=out_specs,
        out_shape=out_shape,
        compiler_params=params(),
        cost_estimate=cost(3 + chunks),
        name="attend_last" if last else "attend",
    )(*args)


def condition_kernel(place, cond, gates, scale, shift, out):
    rows = cond.shape[0] * cond.shape[1]
    width = cond.shape[2]
    c = normalize(cond[...].reshape(rows, width).astype(f32)).astype(bf16)
    gate = jnp.concatenate([gates[n % 4, n // 4] for n in range(8)], axis=0)
    out[0] = sigmoid(dot_t(c, gate[:, :width]))
    out[1] = sigmoid(dot(c, scale[...]))
    out[2] = dot(c, shift[...])
    out[3] = sigmoid(dot_t(c, gate[:, width:]))


def condition(place, cond, gathered, scale, shift):
    samples, rows, width = cond.shape
    model = scale.shape[1]
    take, size, share = samples // 4, rows // 2, model // 8
    at = gathered.shape[2] // share - 1
    return pl.pallas_call(
        condition_kernel,
        grid_spec=pltpu.PrefetchScalarGridSpec(
            num_scalar_prefetch=1,
            grid=(1,),
            in_specs=[
                pl.BlockSpec((take, size, width), lambda g, p: (p[2], p[1], 0)),
                pl.BlockSpec((4, 2, share, model), lambda g, p: (0, 0, at, 0)),
                pl.BlockSpec(scale.shape, lambda g, p: (0, 0)),
                pl.BlockSpec(shift.shape, lambda g, p: (0, 0)),
            ],
            out_specs=pl.BlockSpec((4, take * size, model), lambda g, p: (0, 0, 0)),
        ),
        out_shape=jax.ShapeDtypeStruct((4, take * size, model), f32),
        compiler_params=params(),
        cost_estimate=cost(4),
        name="condition",
    )(place, cond, gathered, scale, shift)


def transition_kernel(place, heads, acts, mix, w_out, mine, other, out, stream, inputs, acc):
    step = pl.program_id(0)
    first = place[0] == 0
    rows = stream.shape[0]

    @pl.when(step == 0)
    def _():
        x = heads[...].reshape(w_out.shape[0], rows)
        attended = lax.dot_general(
            x, w_out[...], (((0,), (0,)), ((), ())), preferred_element_type=f32
        )
        s = acts[...].reshape(rows, acts.shape[2]).astype(f32) + mix[0] * attended
        stream[...] = s
        inputs[...] = (mix[1] * normalize(s) + mix[2]).astype(bf16)
        acc[...] = jnp.zeros(acc.shape, f32)

    half = mine.shape[2] // 2
    low = half + half // 2
    x = inputs[...]
    for n in range(mine.shape[1]):
        m, o = mine[0, n], other[0, n]
        a, b = dot_t(x, m[:half]), dot_t(x, o[:half])
        up, gate = jnp.where(first, a, b), jnp.where(first, b, a)
        hidden = (gate * sigmoid(gate) * up).astype(bf16)
        md, od = m[half:low], o[half:low]
        down = jnp.concatenate([jnp.where(first, md, od), jnp.where(first, od, md)], axis=0)
        acc[...] += dot(hidden, down)

    @pl.when(step == pl.num_programs(0) - 1)
    def _():
        result = (stream[...] + mix[3] * acc[...]).astype(bf16)
        share = out.shape[2]
        for n in range(out.shape[0]):
            out[n] = result[:, n * share : (n + 1) * share]


def transition(place, heads, acts, mix, w_out, mine, other):
    samples, rows, width = acts.shape
    take, size = samples // 4, rows // 2
    block = pl.BlockSpec((1,) + mine.shape[1:], lambda g, p: (g, 0, 0, 0))
    whole = lambda shape: pl.BlockSpec(shape, lambda g, p: (0,) * len(shape))
    return pl.pallas_call(
        transition_kernel,
        grid_spec=pltpu.PrefetchScalarGridSpec(
            num_scalar_prefetch=1,
            grid=(mine.shape[0],),
            in_specs=[
                whole(heads.shape),
                pl.BlockSpec((take, size, width), lambda g, p: (p[2], p[1], 0)),
                whole(mix.shape),
                whole(w_out.shape),
                block,
                block,
            ],
            out_specs=whole((8, take * size, width // 8)),
            scratch_shapes=[
                pltpu.VMEM((take * size, width), f32),
                pltpu.VMEM((take * size, width), bf16),
                pltpu.VMEM((take * size, width), f32),
            ],
        ),
        out_shape=jax.ShapeDtypeStruct((8, take * size, width // 8), bf16),
        compiler_params=params(),
        cost_estimate=cost(9),
        name="transition",
    )(place, heads, acts, mix, w_out, mine, other)


def per_device(
    acts,
    cond,
    pair,
    chain_id,
    residue_mask,
    w_bias,
    chain_bias,
    ada1_scale,
    ada1_shift,
    w_qkvg,
    w_out,
    out_gate1,
    ada2_scale,
    ada2_shift,
    w_up,
    w_down,
    out_gate2,
):
    z, core, xh, y, samp = (lax.axis_index(n) for n in ("z", "core", "xh", "y", "samp"))
    samples, rows, width = acts.shape
    swap = [(0, 1), (1, 0)]
    here = jnp.stack([core, xh, y]).astype(jnp.int32)

    half_down = w_down.shape[0] // 2
    pack = jnp.concatenate(
        [
            lax.dynamic_index_in_dim(w_up, core, 0, keepdims=False).T,
            lax.dynamic_slice_in_dim(w_down, core * half_down, half_down, 0),
            jnp.concatenate([out_gate1.T, out_gate2.T], axis=1),
        ],
        axis=0,
    )
    far = lax.ppermute(pack, "xh", swap)
    tile = tile_bias(pair, w_bias)
    keep, send = project(here, acts, cond, ada1_scale, ada1_shift, w_qkvg.swapaxes(1, 2))
    send, tile = lax.optimization_barrier((send, tile))
    got = lax.ppermute(send, "core", swap)
    got, far = lax.optimization_barrier((got, far))
    lower = core == 0
    chip = jnp.concatenate(
        [jnp.where(lower, keep, got), jnp.where(lower, got, keep)], axis=1
    )
    chunk, qg = chip[0], chip[1]

    packs = jnp.where(xh == 0, jnp.stack([pack, far]), jnp.stack([far, pack]))
    mine = lax.all_gather(packs, "y", axis=0)

    up_ring = [(i, (i + 1) % 8) for i in range(8)]
    down_ring = [(i, (i + 7) % 8) for i in range(8)]

    def around(right, left):
        return lax.ppermute(right, "z", up_ring), lax.ppermute(left, "z", down_ring)

    half = chunk.shape[0] // 2
    one = around(chunk, chunk)
    tiles = lax.all_to_all(tile, ("samp",) + PLANE, split_axis=0, concat_axis=0, tiled=True)
    tiles = tiles.reshape((2, 8, 2) + tiles.shape[1:])
    two = around(*one)
    (two, tiles) = lax.optimization_barrier((two, tiles))
    order = [z + 7, z + 1, z + 6, z + 2, z + 5, z + 3, z, z + 4]
    place = jnp.stack([n % 8 for n in order] + [z, core]).astype(jnp.int32)
    bias = assemble(place, tiles, chain_id, residue_mask, chain_bias)
    three = around(*two)
    state = attend(qg, [*one, *two], bias, 0, None, False)
    state, three = lax.optimization_barrier((state, three))
    four = around(three[0][:half], three[1][half:])
    state = attend(qg, [*three, chunk], bias, 4, state, False)
    heads = attend(qg, [*four], bias, 7, state, True)

    heads, mine = lax.optimization_barrier((heads, mine))
    other = lax.ppermute(mine, "core", swap)
    heads = lax.all_to_all(heads, PLANE, split_axis=0, concat_axis=0, tiled=True)
    mix = condition(here, cond, mine, ada2_scale, ada2_shift)
    out = transition(here, heads, acts, mix, w_out, mine, other)
    out = lax.all_to_all(out, COL, split_axis=0, concat_axis=0, tiled=True)
    out = out.reshape(2, 4, samples // 4, rows // 2, width // 8)
    return out.transpose(1, 2, 0, 3, 4).reshape(samples, rows, width // 8)


def solution(mesh):
    fine = Mesh(mesh.devices.reshape(8, 2, 2, 4, 2), ("z", "core", "xh", "y", "samp"))
    row = ("z", "core")
    in_specs = (
        P("samp", row, None),
        P("samp", row, None),
        P(row + ("samp",), COL, None),
        P(),
        P(),
        P(),
        P(COL),
        P(),
        P(),
        P(None, None, COL),
        P(),
        P(None, COL),
        P(),
        P(),
        P(None, None, COL),
        P(COL, None),
        P(None, COL),
    )
    return jax.shard_map(
        per_device,
        mesh=fine,
        in_specs=in_specs,
        out_specs=P("samp", row, COL),
        check_vma=False,
    )
```

time: 182 us -> 142 us (0.78)
  waiting for transfers between devices: 40.5 us -> 23.5 us
  Pallas kernels: 64.6 us -> 49.4 us
  starting transfers between devices: 36.8 us -> 31.5 us
  local copies, waits for them, and re-layouts: 10 us -> 7.06 us
    pallas_call x4 -> x3, Pallas kernels: 29.5 us -> 16.7 us  [attend(): pl.pallas_call(functools.partial(attend_kernel, state is None, last, len(...]
    ppermute x1, waiting for transfers between devices: 9.54 us -> 0.01 us  [per_device(): far = lax.ppermute(pack, 'xh', swap)]
    ppermute x9 -> x8, waiting for transfers between devices: 14.9 us -> 7 us  [the longest x4 3.75 us: around(): lax.ppermute(left, 'z', down_ring)]
    ppermute x9 -> x8, starting transfers between devices: 17.8 us -> 14.4 us  [the longest x4 14.3 us: around(): lax.ppermute(left, 'z', down_ring)]
    all_to_all x1, starting transfers between devices: 8.53 us -> 5.86 us  [per_device(): lax.all_to_all(tile, ('samp',) + PLANE, split_axis=0, concat_axis=0, tile...]
    all_to_all x1, waiting for transfers between devices: 10.4 us -> 7.82 us  [per_device(): lax.all_to_all(tile, ('samp',) + PLANE, split_axis=0, concat_axis=0, tile...]
    optimization_barrier x1 -> x0, local copies, waits for them, and re-layouts: 2.15 us -> none  [per_device(): heads, mine = lax.optimization_barrier((heads, mine))]
    ppermute x1, starting transfers between devices: 0.01 us -> 2.03 us  [per_device(): other = lax.ppermute(mine, 'core', swap)]
  transfers between devices with their start and end apart: 15 -> 14, of which waited for: 5 -> 7; matrix products, arithmetic and copies ran while one was open for 5% -> 3% of each run, Pallas kernels for 26% -> 29%
where the time goes in v2:
time: 142 us; the launch traced here: 140 us
  Pallas kernels  49.4 us (35%)
  starting transfers between devices  31.5 us (22%)
  waiting for transfers between devices  23.5 us (17%)
  between operations  13.5 us (10%)
  blocking collectives  11.3 us (8%)
  local copies, waits for them, and re-layouts  7.06 us (5%)
  other arithmetic  3.9 us (3%)
    pallas_call x3, Pallas kernels, attend(): pl.pallas_call(functools.partial(attend_kernel, state is None, last, len(...  16.7 us
    ppermute x4, starting transfers between devices, around(): lax.ppermute(left, 'z', down_ring)  14.3 us
    all_to_all x1, blocking collectives, per_device(): out = lax.all_to_all(out, COL, split_axis=0, concat_axis=0, tiled=True)  11.3 us
    pallas_call x1, Pallas kernels, transition(): pl.pallas_call(transition_kernel, grid_spec=pltpu.PrefetchScalarGridSpec(...  9.39 us
    all_to_all x1, waiting for transfers between devices, per_device(): lax.all_to_all(tile, ('samp',) + PLANE, split_axis=0, concat_axis=0, tile...  7.82 us
    pallas_call x1, Pallas kernels, project(): pl.pallas_call(project_kernel, grid_spec=pltpu.PrefetchScalarGridSpec(num...  7.12 us
    pallas_call x1, Pallas kernels, tile_bias(): pl.pallas_call(bias_kernel, grid=(rows // block,), in_specs=[pl.BlockSpec...  6.56 us
    all_to_all x1, starting transfers between devices, per_device(): lax.all_to_all(tile, ('samp',) + PLANE, split_axis=0, concat_axis=0, tile...  5.86 us
  transfers between devices with their start and end apart: 14, of which 7 were waited for; matrix products, arithmetic and copies ran while one was open for 3% of the time, Pallas kernels for 29%

profile of v2, /device:TPU:1, one launch (start us, length us, event | category | flops | bytes accessed | tf_op | source)
XLA Modules:
  0.0 140.2 jit_solution(14652806100849211057)
XLA Ops:
  6.5 1.0 constant_dynamic-slice_fusion
  7.5 0.1 copy-done
  7.7 1.0 fusion.3
  8.7 3.7 %collective-permute-start.1 = (bf16[384,768]{1,0:T(8,128)(2,1)S(1)}, bf16[384,768]{1,0:T(8,128)(2,1)S(1)}, u32[]{:S(2)}, u32[]{:S(2)}) collective-permute-start(bf16[384,768]{1,0:T(8,128)(2,1)S(1)} %get-tuple-element.38), channel_id=1, source_target_pairs={{0,8},{8,0},{1,9},{9,1},{2,10},{10,2},{3,11},{11,3},{4,12},{12,4},... | collective-permute-start | bytes 1769480 | tf_op jit(solution)/shard_map/ppermute | solution.py:434
  12.4 6.6 %tile_bias.1 = bf16[2,768,192]{2,1,0:T(8,128)(2,1)} custom-call(bf16[48,192,128]{2,1,0:T(8,128)(2,1)} %pair.1, bf16[16,128]{1,0:T(8,128)(2,1)} %bitcast.40), custom_call_target="tpu_custom_call" | custom-call | bytes 20400000 | tf_op jit(solution)/shard_map/tile_bias/pallas_call | solution.py:133
  18.9 0.7 pad_add_fusion.place
  19.6 7.1 %project.1 = (bf16[2,96,1152]{2,1,0:T(8,128)(2,1)}, bf16[2,96,1152]{2,1,0:T(8,128)(2,1)}) custom-call(s32[3]{0:T(128)} %pad_add_fusion.place, bf16[12,96,768]{2,1,0:T(8,128)(2,1)} %acts.3, bf16[12,96,384]{2,1,0:T(8,128)(2,1)} %cond.3, bf16[384,768]{1,0:T(8,128)(2,1)} %scale.2, bf16[384,768]{1,0:T(8,128)(2,1)} %shift.2, bf16[4,96,768]{2,1,0:T(8,128)(2,1)} %bitcast.36), custom_call_target="tpu_custom_call" | custom-call | bytes 27200000 | tf_op jit(solution)/shard_map/project/pallas_call | solution.py:87
  26.7 1.0 collective-permute-start
  27.7 1.6 %collective-permute-done = bf16[2,96,1152]{2,1,0:T(8,128)(2,1)S(1)} collective-permute-done((bf16[2,96,1152]{2,1,0:T(8,128)(2,1)}, bf16[2,96,1152]{2,1,0:T(8,128)(2,1)S(1)}, u32[]{:S(2)}, u32[]{:S(2)}) %collective-permute-start) | collective-permute-done | bytes 442400 | tf_op jit(solution)/shard_map/ppermute | solution.py:438
  29.3 1.3 maximum_select_fusion
  30.6 0.0 all-gather.2.cloned.1.call-update
  30.6 1.0 copy-done.6
  31.6 0.1 broadcast_select_fusion
  31.7 0.8 fusion.2
  32.6 5.6 %collective-permute-start.3 = (bf16[192,1152]{1,0:T(8,128)(2,1)S(1)}, bf16[192,1152]{1,0:T(8,128)(2,1)S(1)}, u32[]{:S(2)}, u32[]{:S(2)}) collective-permute-start(bf16[192,1152]{1,0:T(8,128)(2,1)S(1)} %get-tuple-element.33.refs_3_), channel_id=1, source_target_pairs={{0,224},{32,0},{64,32},{96,64},{128,96},{160,128},{192,160},{224,1... | collective-permute-start | bytes 1327112 | tf_op jit(solution)/shard_map/ppermute | solution.py:453
  38.1 5.9 %all-to-all-start = ((bf16[32,48,192]{2,1,0:T(8,128)(2,1)}), bf16[32,48,192]{2,1,0:T(8,128)(2,1)S(1)}, u32[]{:S(2)}, u32[]{:S(2)}) async-start(bf16[32,48,192]{2,1,0:T(8,128)(2,1)} %bitcast.5), calls=%async_computation | async-start | bytes 1572864 | tf_op jit(solution)/shard_map/all_to_all | solution.py:457
  44.0 3.3 %collective-permute-done.3.refs_2_ = bf16[192,1152]{1,0:T(8,128)(2,1)S(1)} collective-permute-done((bf16[192,1152]{1,0:T(8,128)(2,1)S(1)}, bf16[192,1152]{1,0:T(8,128)(2,1)S(1)}, u32[]{:S(2)}, u32[]{:S(2)}) %collective-permute-start.3) | collective-permute-done | bytes 442400 | tf_op jit(solution)/shard_map/ppermute | solution.py:453
  47.3 3.4 %collective-permute-start.5 = (bf16[192,1152]{1,0:T(8,128)(2,1)S(1)}, bf16[192,1152]{1,0:T(8,128)(2,1)S(1)}, u32[]{:S(2)}, u32[]{:S(2)}) collective-permute-start(bf16[192,1152]{1,0:T(8,128)(2,1)S(1)} %collective-permute-done.3.refs_2_), channel_id=1, source_target_pairs={{0,224},{32,0},{64,32},{96,64},{128,96},{160,128},{192,160},{224,1... | collective-permute-start | bytes 1327112 | tf_op jit(solution)/shard_map/ppermute | solution.py:453
  50.7 0.0 collective-permute-start.4
  50.7 7.8 %all-to-all-done = bf16[32,48,192]{2,1,0:T(8,128)(2,1)S(1)} async-done(((bf16[32,48,192]{2,1,0:T(8,128)(2,1)}), bf16[32,48,192]{2,1,0:T(8,128)(2,1)S(1)}, u32[]{:S(2)}, u32[]{:S(2)}) %all-to-all-start) | async-done | bytes 589856 | tf_op jit(solution)/shard_map/all_to_all | solution.py:457
  58.6 0.4 collective-permute-done.5.refs_4_
  59.0 3.2 %collective-permute-done.4.refs_3_ = bf16[192,1152]{1,0:T(8,128)(2,1)} collective-permute-done((bf16[192,1152]{1,0:T(8,128)(2,1)S(1)}, bf16[192,1152]{1,0:T(8,128)(2,1)}, u32[]{:S(2)}, u32[]{:S(2)}) %collective-permute-start.4) | collective-permute-done | bytes 442400 | tf_op jit(solution)/shard_map/ppermute | solution.py:453
  62.2 0.0 collective-permute-start.6
  62.2 2.7 %collective-permute-start.7 = (bf16[192,1152]{1,0:T(8,128)(2,1)}, bf16[192,1152]{1,0:T(8,128)(2,1)S(1)}, u32[]{:S(2)}, u32[]{:S(2)}) collective-permute-start(bf16[192,1152]{1,0:T(8,128)(2,1)} %copy-done.9), channel_id=1, source_target_pairs={{0,224},{32,0},{64,32},{96,64},{128,96},{160,128},{192,160},{224,1... | collective-permute-start | bytes 1327112 | tf_op jit(solution)/shard_map/ppermute | solution.py:453
  64.9 0.7 reshape.79.refs_2_.refs_3_.refs_6_
  65.6 0.7 reshape.80.refs_4_.refs_5_
  66.3 0.7 stack.70.place
  66.9 5.3 %assemble.1.refs_5_.refs_6_.refs_7_.refs_8_.refs_4_.refs_3_ = f32[8,192,384]{2,1,0:T(8,128)} custom-call(s32[10]{0:T(128)} %stack.70.place, bf16[2,8,2,48,192]{4,3,2,1,0:T(8,128)(2,1)} %bitcast.33, bf16[2,8,2,48,192]{4,3,2,1,0:T(8,128)(2,1)} %bitcast.34, s32[8,1,192]{2,1,0:T(1,128)} %reshape.79.refs_2_.refs_3_.refs_6_, ...), custom_call_target="tpu_custom_call" | custom-call | bytes 17000000 | tf_op jit(solution)/shard_map/assemble/pallas_call | solution.py:183
  72.2 6.5 %attend.2.refs_7_ = f32[3,2,56,384]{3,2,1,0:T(8,128)} custom-call(bf16[192,1152]{1,0:T(8,128)(2,1)} %get-tuple-element.34.refs_0_, bf16[192,1152]{1,0:T(8,128)(2,1)} %copy-done.8, bf16[192,1152]{1,0:T(8,128)(2,1)} %copy-done.7, bf16[192,1152]{1,0:T(8,128)(2,1)} %collective-permute-done.4.refs_3_, bf16[192,1152]{1,0:T(8,128)(2,1)} %copy-done.9, ...), custom_call_target="tpu_custom_call" | custom-call | bytes 23800000 | tf_op jit(solution)/shard_map/attend/pallas_call | solution.py:285
  78.7 0.0 collective-permute-done.6.refs_1_
  78.7 0.0 collective-permute-done.7.refs_2_
  78.8 0.1 collective-permute-start.8
  78.9 2.7 %collective-permute-start.9 = (bf16[96,1152]{1,0:T(8,128)(2,1)S(1)}, bf16[96,1152]{1,0:T(8,128)(2,1)S(1)}, u32[]{:S(2)}, u32[]{:S(2)}) collective-permute-start(bf16[96,1152]{1,0:T(8,128)(2,1)S(1)} %slice.15), channel_id=1, source_target_pairs={{0,224},{32,0},{64,32},{96,64},{128,96},{160,128},{192,160},{224,1... | collective-permute-start | bytes 663560 | tf_op jit(solution)/shard_map/ppermute | solution.py:453
  81.6 5.8 %attend.3.refs_4_ = f32[3,2,56,384]{3,2,1,0:T(8,128)} custom-call(bf16[192,1152]{1,0:T(8,128)(2,1)} %get-tuple-element.34.refs_0_, bf16[192,1152]{1,0:T(8,128)(2,1)} %copy-done.4, bf16[192,1152]{1,0:T(8,128)(2,1)} %copy-done.5, bf16[192,1152]{1,0:T(8,128)(2,1)} %copy-done.2, f32[8,192,384]{2,1,0:T(8,128)} %assemble.1.refs_5_.refs_6_.refs_7_.refs_8_.refs_4_.refs_3_, ...), custom_call_target="tpu_custom_call" | custom-call | bytes 20400000 | tf_op jit(solution)/shard_map/attend/pallas_call | solution.py:285
  87.4 0.0 collective-permute-done.9.refs_2_
  87.4 0.7 copy-done.10
  88.1 0.7 copy-done.11
  88.8 4.4 %attend_last.1 = bf16[16,48,144]{2,1,0:T(8,128)(2,1)} custom-call(bf16[192,1152]{1,0:T(8,128)(2,1)} %get-tuple-element.34.refs_0_, bf16[96,1152]{1,0:T(8,128)(2,1)} %copy-done.10, bf16[96,1152]{1,0:T(8,128)(2,1)} %copy-done.11, f32[8,192,384]{2,1,0:T(8,128)} %assemble.1.refs_5_.refs_6_.refs_7_.refs_8_.refs_4_.refs_3_, f32[3,2,56,384]{3,2,1,0:T(8,128)} %attend.3.refs_4_), custom_call_target="tpu_custom_call" | custom-call | bytes 13600000 | tf_op jit(solution)/shard_map/attend_last/pallas_call | solution.py:285
  93.2 1.4 %all-gather.2.cloned.1.call-done.gates.mine = bf16[4,2,384,768]{3,2,1,0:T(8,128)(2,1)} async-done(((bf16[1,2,384,768]{3,2,1,0:T(8,128)(2,1)}), bf16[4,2,384,768]{3,2,1,0:T(8,128)(2,1)}) %all-gather.2.cloned.1.call-update) | async-done | bytes 4718608 | tf_op jit(solution)/shard_map/all_gather | solution.py:447
  94.6 2.0 %collective-permute-start.10 = (bf16[4,2,384,768]{3,2,1,0:T(8,128)(2,1)}, bf16[4,2,384,768]{3,2,1,0:T(8,128)(2,1)}, u32[]{:S(2)}, u32[]{:S(2)}) collective-permute-start(bf16[4,2,384,768]{3,2,1,0:T(8,128)(2,1)} %all-gather.2.cloned.1.call-done.gates.mine), channel_id=1, source_target_pairs={{0,16},{16,0},{1,17},{17,1},{2,18},{18,2},{3,19},{19,3},{4,20},{20... | collective-permute-start | bytes 14155784 | tf_op jit(solution)/shard_map/ppermute | solution.py:472
  96.7 4.6 %all-to-all-start.1 = ((bf16[16,48,144]{2,1,0:T(8,128)(2,1)}), bf16[16,48,144]{2,1,0:T(8,128)(2,1)S(1)}, u32[]{:S(2)}, u32[]{:S(2)}) async-start(bf16[16,48,144]{2,1,0:T(8,128)(2,1)} %attend_last.1), calls=%async_computation.1 | async-start | bytes 786432 | tf_op jit(solution)/shard_map/all_to_all | solution.py:473
  101.3 4.3 %condition.1.mix = f32[4,144,768]{2,1,0:T(8,128)} custom-call(s32[3]{0:T(128)} %pad_add_fusion.place, bf16[12,96,384]{2,1,0:T(8,128)(2,1)} %cond.3, bf16[4,2,384,768]{3,2,1,0:T(8,128)(2,1)} %all-gather.2.cloned.1.call-done.gates.mine, bf16[384,768]{1,0:T(8,128)(2,1)} %scale.3, bf16[384,768]{1,0:T(8,128)(2,1)} %shift.3), custom_call_target="tpu_custom_call" | custom-call | bytes 13600000 | tf_op jit(solution)/shard_map/condition/pallas_call | solution.py:313
  105.6 5.6 %all-to-all-done.1.heads = bf16[16,48,144]{2,1,0:T(8,128)(2,1)S(1)} async-done(((bf16[16,48,144]{2,1,0:T(8,128)(2,1)}), bf16[16,48,144]{2,1,0:T(8,128)(2,1)S(1)}, u32[]{:S(2)}, u32[]{:S(2)}) %all-to-all-start.1) | async-done | bytes 221216 | tf_op jit(solution)/shard_map/all_to_all | solution.py:473
  111.2 0.0 collective-permute-done.10.other
  111.2 0.7 copy-done.3
  111.9 9.4 %transition.1 = bf16[8,144,96]{2,1,0:T(8,128)(2,1)} custom-call(s32[3]{0:T(128)} %pad_add_fusion.place, bf16[16,48,144]{2,1,0:T(8,128)(2,1)} %copy-done.3, bf16[12,96,768]{2,1,0:T(8,128)(2,1)} %acts.3, f32[4,144,768]{2,1,0:T(8,128)} %condition.1.mix, bf16[768,768]{1,0:T(8,128)(2,1)} %w_out.1, ...), custom_call_target="tpu_custom_call" | custom-call | bytes 30600000 | tf_op jit(solution)/shard_map/transition/pallas_call | solution.py:374
  121.3 11.3 %all_to_all.15 = bf16[8,144,96]{2,1,0:T(8,128)(2,1)S(1)} all-to-all(bf16[8,144,96]{2,1,0:T(8,128)(2,1)} %transition.1), channel_id=1, replica_groups=mesh['z'=8,'core'=2,'xh'=2,'y'=4,'samp'=2] {'xh','y'}, dimensions={0} | all-to-all | bytes 442368 | tf_op jit(solution)/shard_map/all_to_all | solution.py:476
  132.7 0.7 copy.19
  (31 shorter events, 0.1 us)
Async XLA Ops:
  6.5 1.1 copy-start
  6.5 88.1 %all-gather.2.cloned.1.call-start = ((), (), s32[]{:S(2)}) async-start(), calls=%async_computation.3 | async-start | bytes 5898240 | tf_op jit(solution)/shard_map/all_gather | solution.py:447
  8.7 20.6 %collective-permute-start.1 = (bf16[384,768]{1,0:T(8,128)(2,1)S(1)}, bf16[384,768]{1,0:T(8,128)(2,1)S(1)}, u32[]{:S(2)}, u32[]{:S(2)}) collective-permute-start(bf16[384,768]{1,0:T(8,128)(2,1)S(1)} %get-tuple-element.38), channel_id=1, source_target_pairs={{0,8},{8,0},{1,9},{9,1},{2,10},{10,2},{3,11},{11,3},{4,12},{12,4},... | collective-permute-start | bytes 1769480 | tf_op jit(solution)/shard_map/ppermute | solution.py:434
  26.7 2.6 %collective-permute-start = (bf16[2,96,1152]{2,1,0:T(8,128)(2,1)}, bf16[2,96,1152]{2,1,0:T(8,128)(2,1)S(1)}, u32[]{:S(2)}, u32[]{:S(2)}) collective-permute-start(bf16[2,96,1152]{2,1,0:T(8,128)(2,1)} %get-tuple-element.21), channel_id=1, source_target_pairs={{0,16},{16,0},{1,17},{17,1},{2,18},{18,2},{3,19},{19,3},{4,20},{20... | collective-permute-start | bytes 1327112 | tf_op jit(solution)/shard_map/ppermute | solution.py:438
  30.6 1.0 copy-start.6
  32.5 39.7 %copy-start.2 = (bf16[192,1152]{1,0:T(8,128)(2,1)}, bf16[192,1152]{1,0:T(8,128)(2,1)S(1)}, u32[]{:S(2)}) copy-start(bf16[192,1152]{1,0:T(8,128)(2,1)S(1)} %get-tuple-element.33.refs_3_) | copy-start | bytes 1327108
  32.5 32.4 %copy-start.12 = (s32[1536]{0:T(1024)S(1)}, s32[1536]{0:T(1024)}, u32[]{:S(2)}) copy-start(s32[1536]{0:T(1024)} %param.20) | copy-start | bytes 18436
  32.6 33.0 %copy-start.13 = (s32[1536]{0:T(1024)S(1)}, s32[1536]{0:T(1024)}, u32[]{:S(2)}) copy-start(s32[1536]{0:T(1024)} %param.21) | copy-start | bytes 18436
  32.6 14.8 %collective-permute-start.3 = (bf16[192,1152]{1,0:T(8,128)(2,1)S(1)}, bf16[192,1152]{1,0:T(8,128)(2,1)S(1)}, u32[]{:S(2)}, u32[]{:S(2)}) collective-permute-start(bf16[192,1152]{1,0:T(8,128)(2,1)S(1)} %get-tuple-element.33.refs_3_), channel_id=1, source_target_pairs={{0,224},{32,0},{64,32},{96,64},{128,96},{160,128},{192,160},{224,1... | collective-permute-start | bytes 1327112 | tf_op jit(solution)/shard_map/ppermute | solution.py:453
  38.1 12.6 %collective-permute-start.2 = (bf16[192,1152]{1,0:T(8,128)(2,1)S(1)}, bf16[192,1152]{1,0:T(8,128)(2,1)S(1)}, u32[]{:S(2)}, u32[]{:S(2)}) collective-permute-start(bf16[192,1152]{1,0:T(8,128)(2,1)S(1)} %get-tuple-element.33.refs_3_), channel_id=1, source_target_pairs={{0,32},{32,64},{64,96},{96,128},{128,160},{160,192},{192,224},{224... | collective-permute-start | bytes 1327112 | tf_op jit(solution)/shard_map/ppermute | solution.py:453
  38.1 20.4 %all-to-all-start = ((bf16[32,48,192]{2,1,0:T(8,128)(2,1)}), bf16[32,48,192]{2,1,0:T(8,128)(2,1)S(1)}, u32[]{:S(2)}, u32[]{:S(2)}) async-start(bf16[32,48,192]{2,1,0:T(8,128)(2,1)} %bitcast.5), calls=%async_computation | async-start | bytes 1572864 | tf_op jit(solution)/shard_map/all_to_all | solution.py:457
  47.3 24.9 %copy-start.7 = (bf16[192,1152]{1,0:T(8,128)(2,1)}, bf16[192,1152]{1,0:T(8,128)(2,1)S(1)}, u32[]{:S(2)}) copy-start(bf16[192,1152]{1,0:T(8,128)(2,1)S(1)} %collective-permute-done.3.refs_2_) | copy-start | bytes 1327108
  47.3 11.7 %collective-permute-start.5 = (bf16[192,1152]{1,0:T(8,128)(2,1)S(1)}, bf16[192,1152]{1,0:T(8,128)(2,1)S(1)}, u32[]{:S(2)}, u32[]{:S(2)}) collective-permute-start(bf16[192,1152]{1,0:T(8,128)(2,1)S(1)} %collective-permute-done.3.refs_2_), channel_id=1, source_target_pairs={{0,224},{32,0},{64,32},{96,64},{128,96},{160,128},{192,160},{224,1... | collective-permute-start | bytes 1327112 | tf_op jit(solution)/shard_map/ppermute | solution.py:453
  50.7 11.5 %copy-start.8 = (bf16[192,1152]{1,0:T(8,128)(2,1)}, bf16[192,1152]{1,0:T(8,128)(2,1)S(1)}, u32[]{:S(2)}) copy-start(bf16[192,1152]{1,0:T(8,128)(2,1)S(1)} %collective-permute-done.2.refs_1_) | copy-start | bytes 1327108
  50.7 11.5 %collective-permute-start.4 = (bf16[192,1152]{1,0:T(8,128)(2,1)S(1)}, bf16[192,1152]{1,0:T(8,128)(2,1)}, u32[]{:S(2)}, u32[]{:S(2)}) collective-permute-start(bf16[192,1152]{1,0:T(8,128)(2,1)S(1)} %collective-permute-done.2.refs_1_), channel_id=1, source_target_pairs={{0,32},{32,64},{64,96},{96,128},{128,160},{160,192},{192,224},{224... | collective-permute-start | bytes 1327112 | tf_op jit(solution)/shard_map/ppermute | solution.py:453
  58.6 8.4 %copy-start.1 = (bf16[32,48,192]{2,1,0:T(8,128)(2,1)}, bf16[32,48,192]{2,1,0:T(8,128)(2,1)S(1)}, u32[]{:S(2)}) copy-start(bf16[32,48,192]{2,1,0:T(8,128)(2,1)S(1)} %all-to-all-done) | copy-start | bytes 1769476
  59.0 3.2 %copy-start.9 = (bf16[192,1152]{1,0:T(8,128)(2,1)}, bf16[192,1152]{1,0:T(8,128)(2,1)S(1)}, u32[]{:S(2)}) copy-start(bf16[192,1152]{1,0:T(8,128)(2,1)S(1)} %collective-permute-done.5.refs_4_) | copy-start | bytes 1327108
  62.2 16.5 %collective-permute-start.6 = (bf16[192,1152]{1,0:T(8,128)(2,1)}, bf16[192,1152]{1,0:T(8,128)(2,1)S(1)}, u32[]{:S(2)}, u32[]{:S(2)}) collective-permute-start(bf16[192,1152]{1,0:T(8,128)(2,1)} %collective-permute-done.4.refs_3_), channel_id=1, source_target_pairs={{0,32},{32,64},{64,96},{96,128},{128,160},{160,192},{192,224},{224... | collective-permute-start | bytes 1327112 | tf_op jit(solution)/shard_map/ppermute | solution.py:453
  62.2 16.5 %collective-permute-start.7 = (bf16[192,1152]{1,0:T(8,128)(2,1)}, bf16[192,1152]{1,0:T(8,128)(2,1)S(1)}, u32[]{:S(2)}, u32[]{:S(2)}) collective-permute-start(bf16[192,1152]{1,0:T(8,128)(2,1)} %copy-done.9), channel_id=1, source_target_pairs={{0,224},{32,0},{64,32},{96,64},{128,96},{160,128},{192,160},{224,1... | collective-permute-start | bytes 1327112 | tf_op jit(solution)/shard_map/ppermute | solution.py:453
  78.7 2.8 %copy-start.4 = (bf16[192,1152]{1,0:T(8,128)(2,1)}, bf16[192,1152]{1,0:T(8,128)(2,1)S(1)}, u32[]{:S(2)}) copy-start(bf16[192,1152]{1,0:T(8,128)(2,1)S(1)} %collective-permute-done.6.refs_1_) | copy-start | bytes 1327108
  78.7 2.8 %copy-start.5 = (bf16[192,1152]{1,0:T(8,128)(2,1)}, bf16[192,1152]{1,0:T(8,128)(2,1)S(1)}, u32[]{:S(2)}) copy-start(bf16[192,1152]{1,0:T(8,128)(2,1)S(1)} %collective-permute-done.7.refs_2_) | copy-start | bytes 1327108
  78.8 8.6 %collective-permute-start.8 = (bf16[96,1152]{1,0:T(8,128)(2,1)S(1)}, bf16[96,1152]{1,0:T(8,128)(2,1)S(1)}, u32[]{:S(2)}, u32[]{:S(2)}) collective-permute-start(bf16[96,1152]{1,0:T(8,128)(2,1)S(1)} %slice.14), channel_id=1, source_target_pairs={{0,32},{32,64},{64,96},{96,128},{128,160},{160,192},{192,224},{224... | collective-permute-start | bytes 663560 | tf_op jit(solution)/shard_map/ppermute | solution.py:453
  78.9 8.5 %collective-permute-start.9 = (bf16[96,1152]{1,0:T(8,128)(2,1)S(1)}, bf16[96,1152]{1,0:T(8,128)(2,1)S(1)}, u32[]{:S(2)}, u32[]{:S(2)}) collective-permute-start(bf16[96,1152]{1,0:T(8,128)(2,1)S(1)} %slice.15), channel_id=1, source_target_pairs={{0,224},{32,0},{64,32},{96,64},{128,96},{160,128},{192,160},{224,1... | collective-permute-start | bytes 663560 | tf_op jit(solution)/shard_map/ppermute | solution.py:453
  87.4 0.7 copy-start.10
  88.1 0.7 copy-start.11
  94.6 16.6 %collective-permute-start.10 = (bf16[4,2,384,768]{3,2,1,0:T(8,128)(2,1)}, bf16[4,2,384,768]{3,2,1,0:T(8,128)(2,1)}, u32[]{:S(2)}, u32[]{:S(2)}) collective-permute-start(bf16[4,2,384,768]{3,2,1,0:T(8,128)(2,1)} %all-gather.2.cloned.1.call-done.gates.mine), channel_id=1, source_target_pairs={{0,16},{16,0},{1,17},{17,1},{2,18},{18,2},{3,19},{19,3},{4,20},{20... | collective-permute-start | bytes 14155784 | tf_op jit(solution)/shard_map/ppermute | solution.py:472
  96.7 14.5 %all-to-all-start.1 = ((bf16[16,48,144]{2,1,0:T(8,128)(2,1)}), bf16[16,48,144]{2,1,0:T(8,128)(2,1)S(1)}, u32[]{:S(2)}, u32[]{:S(2)}) async-start(bf16[16,48,144]{2,1,0:T(8,128)(2,1)} %attend_last.1), calls=%async_computation.1 | async-start | bytes 786432 | tf_op jit(solution)/shard_map/all_to_all | solution.py:473
  111.2 0.7 copy-start.3
Sparse Core Ops, SparseCore 0:
  30.7 63.8 all-gather.1

commit v3 on v2

v3 whole, which is shorter than its diff:
```python
import functools
import math

import jax
import jax.numpy as jnp
from jax import lax
from jax.experimental import pallas as pl
from jax.experimental.pallas import tpu as pltpu
from jax.sharding import Mesh, PartitionSpec as P

DH = 48
PIECE = 2 * DH
GROUP = 4
WIDE = GROUP * PIECE
EPS = 1e-05
LOG2E = math.log2(math.e)
MASKED = -1000000000.0
COL = ("xh", "y")
PLANE = ("xh", "y", "core")
VMEM = 14 * 1024 * 1024

WINDOW = 256

f32 = jnp.float32
bf16 = jnp.bfloat16


def normalize(values):
    mean = jnp.mean(values, axis=-1, keepdims=True)
    square = jnp.mean(values * values, axis=-1, keepdims=True)
    return (values - mean) * lax.rsqrt(square - mean * mean + EPS)


def sigmoid(values):
    return 0.5 * jnp.tanh(0.5 * values) + 0.5


def dot(left, right):
    return jnp.dot(left, right, preferred_element_type=f32)


def dot_t(left, right):
    return lax.dot_general(left, right, (((1,), (1,)), ((), ())), preferred_element_type=f32)


def params(limit=VMEM):
    return pltpu.CompilerParams(vmem_limit_bytes=limit)


def cost(micros):
    return pl.CostEstimate(flops=0, bytes_accessed=int(micros * 3_400_000), transcendentals=0)


def project_kernel(place, acts, cond, scale, shift, w, stay, send, wcat):
    first = place[0] == 0

    @pl.when(pl.program_id(0) == 0)
    def _():
        low = [w[n, :DH] for n in range(4)]
        high = [w[n, DH:] for n in range(4)]
        kept = [jnp.where(first, low[n], high[n]) for n in (1, 2, 0, 3)]
        sent = [jnp.where(first, high[n], low[n]) for n in (1, 2, 0, 3)]
        wcat[...] = jnp.concatenate(kept + sent, axis=0)

    rows = GROUP * acts.shape[1]
    x = acts[...].reshape(rows, acts.shape[2]).astype(f32)
    c = normalize(cond[...].reshape(rows, cond.shape[2]).astype(f32)).astype(bf16)
    a = (sigmoid(dot(c, scale[...])) * normalize(x) + dot(c, shift[...])).astype(bf16)
    y = dot_t(a, wcat[...])
    lane = lax.broadcasted_iota(jnp.int32, (1, WIDE), 1) % (2 * PIECE)
    is_query = (lane >= PIECE) & (lane < PIECE + DH)
    y = (y * jnp.where(is_query, LOG2E / math.sqrt(DH), 1.0)).astype(bf16)
    step = acts.shape[1]
    for n, out in enumerate((send.at[0], stay, send.at[1], send.at[2])):
        at = n * PIECE
        out[...] = jnp.concatenate(
            [y[j * step : (j + 1) * step, at : at + PIECE] for j in range(GROUP)], axis=1
        )


def project(core, acts, cond, scale, shift, w):
    samples, rows, width = acts.shape
    groups = samples // GROUP
    one = jax.ShapeDtypeStruct((rows, samples * PIECE), bf16)
    three = jax.ShapeDtypeStruct((3,) + one.shape, bf16)
    whole = lambda shape: pl.BlockSpec(shape, lambda g, p: (0,) * len(shape))
    return pl.pallas_call(
        project_kernel,
        grid_spec=pltpu.PrefetchScalarGridSpec(
            num_scalar_prefetch=1,
            grid=(groups,),
            in_specs=[
                pl.BlockSpec((GROUP, rows, width), lambda g, p: (g, 0, 0)),
                pl.BlockSpec((GROUP, rows, cond.shape[2]), lambda g, p: (g, 0, 0)),
                whole(scale.shape),
                whole(shift.shape),
                whole(w.shape),
            ],
            out_specs=[
                pl.BlockSpec((rows, WIDE), lambda g, p: (0, g)),
                pl.BlockSpec((3, rows, WIDE), lambda g, p: (0, 0, g)),
            ],
            scratch_shapes=[pltpu.VMEM((WIDE, width), bf16)],
        ),
        out_shape=[one, three],
        compiler_params=params(56 * 1024 * 1024),
        cost_estimate=cost(8),
        name="project",
    )(core, acts, cond, scale, shift, w)


def bias_kernel(pair, w, out, left, right):
    step = pl.program_id(0)
    heads = w.shape[0]
    rows, keys = left.shape[0] // heads, pair.shape[1]
    spare = jnp.zeros((heads, 256 - keys), f32)
    for i in range(pair.shape[0]):
        x = normalize(pair[i].astype(f32)).astype(bf16)
        t = dot_t(w[...], x)
        at = pl.ds(step * pair.shape[0] + i, heads, stride=rows)
        left[at, :] = t[:, :128]
        right[at, :] = jnp.concatenate([t[:, 128:], spare], axis=1)

    @pl.when(step == pl.num_programs(0) - 1)
    def _():
        for h in range(heads):
            rest = right[h * rows : (h + 1) * rows]
            rest = jnp.concatenate([rest[: rows // 2, :64], rest[rows // 2 :, :64]], axis=1)
            tile = jnp.concatenate([left[h * rows : (h + 1) * rows], rest], axis=0).astype(bf16)
            out[h] = tile


def tile_bias(pair, w_bias):
    rows, keys, width = pair.shape
    heads = w_bias.shape[1]
    block = 8
    shape = (heads, rows * keys // 128, 128)
    return pl.pallas_call(
        bias_kernel,
        grid=(rows // block,),
        in_specs=[
            pl.BlockSpec((block, keys, width), lambda g: (g, 0, 0)),
            pl.BlockSpec((heads, width), lambda g: (0, 0)),
        ],
        out_specs=pl.BlockSpec(shape, lambda g: (0, 0, 0)),
        out_shape=jax.ShapeDtypeStruct(shape, bf16),
        scratch_shapes=[pltpu.VMEM((heads * rows, 128), f32)] * 2,
        compiler_params=params(),
        cost_estimate=cost(6),
        name="tile_bias",
    )(pair, w_bias.T)


def assemble_kernel(place, *refs):
    tiles, chains, masks = refs[:2], refs[2:4], refs[4:6]
    chain_q, cb, out = refs[6:]
    keys = out.shape[1]
    row = lax.broadcasted_iota(jnp.int32, (keys, keys), 0)
    col = lax.broadcasted_iota(jnp.int32, (keys, keys), 1)

    def upright(line):
        return jnp.sum(jnp.where(row == col, line.astype(f32), 0.0), axis=1, keepdims=True)

    query = place[8] * keys + col
    low = place[10] == 0
    for n in range(2):
        tile = tiles[n]
        parts = []
        for core in range(2):
            own, theirs = tile[0, core, 0].astype(f32), tile[0, core, 1].astype(f32)
            parts += [jnp.where(low, own, theirs), jnp.where(low, theirs, own)]
        rows = keys // 4
        first = jnp.concatenate([part[:rows] for part in parts], axis=0)
        rest = []
        for part in parts:
            rest += [part[rows:, :64], part[rows:, 64:]]
        bias = jnp.concatenate([first, jnp.concatenate(rest, axis=0)], axis=1).T
        same = upright(chains[n][0]) == chain_q[0].astype(f32)
        bias = bias + jnp.where(same, cb[place[9]], 0.0)
        key = place[2 * pl.program_id(0) + n] * keys + row
        active = (upright(masks[n][0]) == 1.0) | (query == key)
        bias = jnp.where(active, bias * LOG2E, MASKED)
        out[n] = jnp.concatenate([bias, bias], axis=1)


def assemble(place, tiles, chain_id, residue_mask, chain_bias):
    chunks, cores, halves, rows, lanes = tiles.shape
    keys = chain_id.shape[0] // chunks
    tile = [
        pl.BlockSpec((1, cores, halves, rows, lanes), lambda n, p, m=m: (p[2 * n + m], 0, 0, 0, 0))
        for m in range(2)
    ]
    line = [pl.BlockSpec((1, 1, keys), lambda n, p, m=m: (p[2 * n + m], 0, 0)) for m in range(2)]
    own = pl.BlockSpec((1, 1, keys), lambda n, p: (p[8], 0, 0))
    chain = chain_id.reshape(chunks, 1, keys)
    mask = residue_mask.reshape(chunks, 1, keys)
    return pl.pallas_call(
        assemble_kernel,
        grid_spec=pltpu.PrefetchScalarGridSpec(
            num_scalar_prefetch=1,
            grid=(chunks // 2,),
            in_specs=tile + line + line + [own, pl.BlockSpec(memory_space=pltpu.SMEM)],
            out_specs=pl.BlockSpec((2, keys, 2 * keys), lambda n, p: (n, 0, 0)),
        ),
        out_shape=jax.ShapeDtypeStruct((chunks, keys, 2 * keys), f32),
        compiler_params=params(),
        cost_estimate=cost(5),
        name="assemble",
    )(place, tiles, tiles, chain, chain, mask, mask, chain, chain_bias)


def attend_kernel(start, last, picks, begin, chunks, *refs):
    qg_ref, refs = refs[0], refs[1:]
    key_refs, refs = refs[: len(picks)], refs[len(picks) :]
    key_refs = [ref if n is None else ref.at[n] for ref, n in zip(key_refs, picks)]
    bias_ref, refs = refs[0], refs[1:]
    if not start:
        state, refs = refs[0], refs[1:]
    out = refs[0]
    rows = qg_ref.shape[0]
    bias = bias_ref[begin : begin + chunks].reshape(chunks * bias_ref.shape[1], 2 * rows)
    lane = lax.broadcasted_iota(jnp.int32, (1, WINDOW), 1)
    wide = lax.broadcasted_iota(jnp.int32, (1, 2 * rows), 1)
    row = lax.broadcasted_iota(jnp.int32, (2 * DH, 1), 0)
    none = jnp.zeros((), bf16)
    size = rows // 4
    pieces = {}
    for pair in range(2 * qg_ref.shape[1] // WIDE):
        a = pair // 2 * WIDE + 128 * (pair % 2)
        base = 2 * PIECE * pair - a
        group, at = pair // 2, pair % 2
        keys = jnp.concatenate([ref[:, a : a + WINDOW] for ref in key_refs], axis=0)
        queries = qg_ref[:, a : a + WINDOW]

        def both(offset):
            ends = [base + offset, base + offset + PIECE]
            return jnp.concatenate(
                [jnp.where((lane >= n) & (lane < n + DH), queries, none) for n in ends], axis=0
            )

        s = dot_t(keys, both(0)) + bias
        top = jnp.max(s, axis=0, keepdims=True)
        if not start:
            top_old = state[group, at, DH : DH + 1]
            top = jnp.maximum(top, top_old)
            alpha = jnp.exp2(top_old - top)
        p = jnp.exp2(s - top)
        total = jnp.sum(p, axis=0, keepdims=True)
        source = base + DH + jnp.where(row < DH, row, row + PIECE - DH)
        select = jnp.where(lane == source, 1.0, 0.0).astype(bf16)
        values = dot_t(select, keys).astype(bf16)
        o = dot(values, p.astype(bf16))
        o = jnp.where(wide < rows, o[:DH], o[DH:])
        if not start:
            total = total + alpha * state[group, at, DH + 1 : DH + 2]
            o = o + alpha * state[group, at, :DH]
        if last:
            fold = (lane == base + DH + row[:DH]) | (lane == base + DH + PIECE + row[:DH])
            gate = dot_t(jnp.where(fold, 1.0, 0.0).astype(bf16), both(DH))
            o = (o / total * sigmoid(gate)).astype(bf16)
            for j in range(2):
                for quarter in range(4):
                    first = j * rows + quarter * size
                    pieces[2 * pair + j, quarter] = o[:, first : first + size]
        else:
            out[group, at, :DH] = o
            out[group, at, DH:] = jnp.concatenate(
                [top, total, jnp.zeros((6, 2 * rows), f32)], axis=0
            )
    if last:
        for part in range(4):
            for quarter in range(4):
                core, half = quarter // 2, quarter % 2
                out[half * 8 + part * 2 + core] = jnp.concatenate(
                    [pieces[3 * part + n, quarter] for n in range(3)], axis=1
                )


def attend(qg, parts, bias, begin, state, last):
    rows, width = qg.shape
    parts, picks = zip(*parts)
    chunks = len(parts)
    args = [qg, *parts, bias] + ([] if state is None else [state])
    if last:
        out_shape = jax.ShapeDtypeStruct((16, DH, 3 * rows // 4), bf16)
    else:
        out_shape = jax.ShapeDtypeStruct((width // WIDE, 2, DH + 8, 2 * rows), f32)
    return pl.pallas_call(
        functools.partial(attend_kernel, state is None, last, picks, begin, chunks),
        in_specs=[pl.BlockSpec(memory_space=pltpu.VMEM)] * len(args),
        out_specs=pl.BlockSpec(memory_space=pltpu.VMEM),
        out_shape=out_shape,
        compiler_params=params(),
        cost_estimate=cost(2 + chunks),
        name="attend_last" if last else "attend",
    )(*args)


def condition_kernel(place, cond, *refs):
    blocks = refs[:8]
    scale, shift, out, slots, gates, sems = refs[8:]
    width = cond.shape[1]
    share = gates.shape[1]
    copies = [
        pltpu.make_async_copy(blocks[n].at[pl.ds(4 * share, share)], slots.at[n], sems.at[n])
        for n in range(8)
    ]
    for copy in copies:
        copy.start()
    c = normalize(cond[...].astype(f32)).astype(bf16)
    out[1] = sigmoid(dot(c, scale[...]))
    out[2] = dot(c, shift[...])
    for n in range(8):
        copies[n].wait()
        gates[place[1 + n]] = slots[n]
    gate = gates[...].reshape(8 * share, 2 * width)
    out[0] = sigmoid(dot_t(c, gate[:, :width]))
    out[3] = sigmoid(dot_t(c, gate[:, width:]))


def in_vmem(count):
    return [pl.BlockSpec(memory_space=pltpu.VMEM)] * count


def condition(place, cond, weights, scale, shift):
    model = scale.shape[1]
    return pl.pallas_call(
        condition_kernel,
        in_specs=[pl.BlockSpec(memory_space=pltpu.SMEM)]
        + in_vmem(1)
        + [pl.BlockSpec(memory_space=pltpu.HBM)] * len(weights)
        + in_vmem(2),
        out_specs=pl.BlockSpec(memory_space=pltpu.VMEM),
        out_shape=jax.ShapeDtypeStruct((4, cond.shape[0], model), f32),
        scratch_shapes=[
            pltpu.VMEM((8, model // 8, model), bf16),
            pltpu.VMEM((8, model // 8, model), bf16),
            pltpu.SemaphoreType.DMA((8,)),
        ],
        compiler_params=params(58 * 1024 * 1024),
        cost_estimate=cost(4),
        name="condition",
    )(place, cond, *weights, scale, shift)


def transition_kernel(heads, acts, mix, w_out, *refs):
    out, ups, downs, sems = refs[16:]
    units = downs.shape[1]
    copies = []
    for n in range(8):
        up = refs[n].at[pl.ds(0, 2 * units)]
        copies.append(
            (
                pltpu.make_async_copy(up, ups.at[n], sems.at[0, n]),
                pltpu.make_async_copy(refs[8 + n], downs.at[n], sems.at[1, n]),
            )
        )
    for up_copy, down_copy in copies:
        up_copy.start()
        down_copy.start()
    rows = acts.shape[0]
    x = heads[...].reshape(w_out.shape[0], rows)
    attended = lax.dot_general(
        x, w_out[...], (((0,), (0,)), ((), ())), preferred_element_type=f32
    )
    stream = acts[...].astype(f32) + mix[0] * attended
    x = (mix[1] * normalize(stream) + mix[2]).astype(bf16)
    acc = jnp.zeros(stream.shape, f32)
    for n in range(8):
        copies[n][0].wait()
        both = dot_t(x, ups[n])
        up, gate = both[:, :units], both[:, units:]
        hidden = (gate * sigmoid(gate) * up).astype(bf16)
        copies[n][1].wait()
        acc = acc + dot(hidden, downs[n])
    result = (stream + mix[3] * acc).astype(bf16)
    share = out.shape[2]
    for n in range(out.shape[0]):
        out[n] = result[:, n * share : (n + 1) * share]


def transition(heads, acts, mix, w_out, ups, downs):
    rows, width = acts.shape
    units = downs[0].shape[0]
    return pl.pallas_call(
        transition_kernel,
        in_specs=in_vmem(4) + [pl.BlockSpec(memory_space=pltpu.HBM)] * 16,
        out_specs=pl.BlockSpec(memory_space=pltpu.VMEM),
        out_shape=jax.ShapeDtypeStruct((8, rows, width // 8), bf16),
        scratch_shapes=[
            pltpu.VMEM((8, 2 * units, width), bf16),
            pltpu.VMEM((8, units, width), bf16),
            pltpu.SemaphoreType.DMA((2, 8)),
        ],
        compiler_params=params(58 * 1024 * 1024),
        cost_estimate=cost(8),
        name="transition",
    )(heads, acts, mix, w_out, *ups, *downs)


def per_device(
    acts,
    cond,
    pair,
    chain_id,
    residue_mask,
    w_bias,
    chain_bias,
    ada1_scale,
    ada1_shift,
    w_qkvg,
    w_out,
    out_gate1,
    ada2_scale,
    ada2_shift,
    w_up,
    w_down,
    out_gate2,
):
    z, core, xh, y, samp = (lax.axis_index(n) for n in ("z", "core", "xh", "y", "samp"))
    samples, rows, width = acts.shape
    swap = [(0, 1), (1, 0)]
    lower = core == 0
    turn = jnp.where(lower, 1, 3)

    def around(array):
        up = [(2 * n, 2 * ((n + 1) % 8)) for n in range(8)]
        down = [(2 * n + 1, 2 * ((n + 7) % 8) + 1) for n in range(8)]
        return lax.ppermute(array, ("z", "core"), up + down)

    def around_y(array):
        up = [(n, (n + 1) % 4) for n in range(4)]
        down = [(4 + n, 4 + (n + 3) % 4) for n in range(4)]
        return lax.ppermute(array, ("core", "y"), up + down)

    def far_side(array):
        return lax.ppermute(array, ("xh", "samp"), [(0, 3), (3, 0), (1, 2), (2, 1)])

    def cross(array):
        return lax.ppermute(array, "core", swap)

    w_down_y = around_y(w_down)
    down_far = far_side(w_down)

    back, ahead = (y + 4 - turn) % 4, (y + turn) % 4
    owners = [4 * x + n for n in (y, back, ahead) for x in (xh, 1 - xh)]
    opposite = (y + 2) % 4
    owners += [4 * jnp.where(lower, xh, 1 - xh) + opposite]
    owners += [4 * jnp.where(lower, 1 - xh, xh) + opposite]
    here = jnp.stack([core] + owners).astype(jnp.int32)

    stay, send = project(here, acts, cond, ada1_scale, ada1_shift, w_qkvg.swapaxes(1, 2))
    send, w_down_y, down_far = lax.optimization_barrier((send, w_down_y, down_far))
    got = cross(send)

    def in_order(own, theirs):
        return jnp.concatenate(
            [jnp.where(lower, own, theirs), jnp.where(lower, theirs, own)], axis=0
        )

    chunk = jnp.stack([in_order(send[0], got[1]), in_order(send[1], got[0])])
    one = around(chunk)
    w_bias, w_up, chunk = lax.optimization_barrier((w_bias, w_up, chunk))
    up = jnp.concatenate(
        [
            w_up.swapaxes(1, 2).reshape(-1, width),
            jnp.concatenate([out_gate1.T, out_gate2.T], axis=1),
        ],
        axis=0,
    )
    part = up.shape[0] // 2
    up_part = far_side(lax.dynamic_slice_in_dim(up, core * part, part, 0))
    up_y = around_y(up)
    down_far_y = around_y(down_far)
    tile = tile_bias(pair, w_bias)
    tile_other = lax.ppermute(tile, "samp", swap)
    one, up_part, up_y, down_far_y, tile_other = lax.optimization_barrier(
        (one, up_part, up_y, down_far_y, tile_other)
    )
    up_far = in_order(up_part, cross(up_part))
    tiles = jnp.stack([tile, tile_other], axis=1)
    tiles = lax.all_to_all(tiles, PLANE, split_axis=0, concat_axis=0, tiled=True)
    tiles = tiles.reshape((8, 2) + tiles.shape[1:])
    two = around(one)
    one_x = cross(one)
    qg = in_order(stay, got[2])
    two, up_far, tiles = lax.optimization_barrier((two, up_far, tiles))
    side = jnp.where(lower, 1, 7)
    order = [z] + [n for s in (1, 2, 3) for n in (z + 8 * 3 - s * side, z + s * side)] + [z + 4]
    place = jnp.stack([n % 8 for n in order] + [z, core, samp]).astype(jnp.int32)
    bias = assemble(place, tiles, chain_id, residue_mask, chain_bias)
    three = around(two)
    two_x = cross(two)
    up_far_y = around_y(up_far)
    down_last = around_y(jnp.where(lower, w_down_y, down_far_y))
    parts = [(chunk, 0), (one, 0), (one_x, 1), (two, 0), (two_x, 1)]
    state = attend(qg, parts, bias, 0, None, False)
    three, state, up_far_y, down_last = lax.optimization_barrier(
        (three, state, up_far_y, down_last)
    )
    four = around(three[0])
    up_last = around_y(jnp.where(lower, up_y, up_far_y))
    three_x = cross(three)
    state = attend(qg, [(three, 0), (three_x, 1)], bias, 5, state, False)
    heads = attend(qg, [(four, None)], bias, 7, state, True)
    heads, up_last = lax.optimization_barrier((heads, up_last))

    def all_blocks(own, far, own_y, far_y, last):
        return [own, far, own_y, far_y, cross(own_y), cross(far_y), last, cross(last)]

    ups = all_blocks(up, up_far, up_y, up_far_y, up_last)
    heads = lax.all_to_all(heads, PLANE, split_axis=0, concat_axis=0, tiled=True)

    def rows_of(array):
        take, size = samples // 4, rows // 2
        at = (y * take, xh * size, 0)
        return lax.dynamic_slice(array, at, (take, size, array.shape[2])).reshape(
            take * size, array.shape[2]
        )

    mix = condition(here, rows_of(cond), ups, ada2_scale, ada2_shift)
    downs = all_blocks(w_down, down_far, w_down_y, down_far_y, down_last)
    out = transition(heads, rows_of(acts), mix, w_out, ups, downs)
    out = lax.all_to_all(out, COL, split_axis=0, concat_axis=0, tiled=True)
    out = out.reshape(2, 4, samples // 4, rows // 2, width // 8)
    return out.transpose(1, 2, 0, 3, 4).reshape(samples, rows, width // 8)


def solution(mesh):
    fine = Mesh(mesh.devices.reshape(8, 2, 2, 4, 2), ("z", "core", "xh", "y", "samp"))
    row = ("z", "core")
    in_specs = (
        P("samp", row, None),
        P("samp", row, None),
        P(row + ("samp",), COL, None),
        P(),
        P(),
        P(),
        P(COL),
        P(),
        P(),
        P(None, None, COL),
        P(),
        P(None, COL),
        P(),
        P(),
        P(None, None, COL),
        P(COL, None),
        P(None, COL),
    )
    return jax.shard_map(
        per_device,
        mesh=fine,
        in_specs=in_specs,
        out_specs=P("samp", row, COL),
        check_vma=False,
    )
```

time: 142 us -> 132 us (0.930)
  between operations: 13.5 us -> 0.33 us
  Pallas kernels: 49.4 us -> 40.1 us
  starting transfers between devices: 31.5 us -> 37.2 us
  other arithmetic: 3.9 us -> 6.95 us
  blocking collectives: 11.3 us -> 14.2 us
  local copies, waits for them, and re-layouts: 7.06 us -> 9.4 us
    ppermute x11 -> x24, starting transfers between devices: 21.1 us -> 29.2 us  [the longest x4 11.8 us: around(): return lax.ppermute(array, ('z', 'core'), up + down)]
    pallas_call x5, Pallas kernels: 30.4 us -> 24.6 us  [the longest x3 11.1 us: attend(): pl.pallas_call(functools.partial(attend_kernel, state is None, last, pick...]
    all_to_all x1, waiting for transfers between devices: 5.57 us -> 1.04 us  [per_device(): lax.all_to_all(heads, PLANE, split_axis=0, concat_axis=0, tiled=True)]
    select_n x2 -> x5, other arithmetic: 1.39 us -> 5.7 us  [the longest x3 3.5 us: in_order(): jnp.where(lower, own, theirs)]
    ppermute x11 -> x24, waiting for transfers between devices: 8.63 us -> 12.5 us  [the longest x6 5.87 us: around_y(): return lax.ppermute(array, ('core', 'y'), up + down)]
    all_to_all x1, blocking collectives: 11.3 us -> 14.2 us  [per_device(): out = lax.all_to_all(out, COL, split_axis=0, concat_axis=0, tiled=True)]
    pallas_call x1, Pallas kernels: 6.56 us -> 3.88 us  [tile_bias(): pl.pallas_call(bias_kernel, grid=(rows // block,), in_specs=[pl.BlockSpec...]
    dynamic_slice x1 -> x3, local copies, waits for them, and re-layouts: 0.98 us -> 3.22 us  [the longest x2 3.19 us: rows_of(): lax.dynamic_slice(array, at, (take, size, array.shape[2]))]
  transfers between devices with their start and end apart: 14 -> 26, of which waited for: 7 -> 8; matrix products, arithmetic and copies ran while one was open for 3% -> 7% of each run, Pallas kernels for 29% -> 24%
where the time goes in v3:
time: 132 us; the launch traced here: 131 us
  Pallas kernels  40.1 us (30%)
  starting transfers between devices  37.2 us (28%)
  waiting for transfers between devices  22.8 us (17%)
  blocking collectives  14.2 us (11%)
  local copies, waits for them, and re-layouts  9.4 us (7%)
  other arithmetic  6.95 us (5%)
    all_to_all x1, blocking collectives, per_device(): out = lax.all_to_all(out, COL, split_axis=0, concat_axis=0, tiled=True)  14.2 us
    ppermute x4, starting transfers between devices, around(): return lax.ppermute(array, ('z', 'core'), up + down)  11.8 us
    pallas_call x3, Pallas kernels, attend(): pl.pallas_call(functools.partial(attend_kernel, state is None, last, pick...  11.1 us
    all_to_all x1, waiting for transfers between devices, per_device(): lax.all_to_all(tiles, PLANE, split_axis=0, concat_axis=0, tiled=True)  9.34 us
    pallas_call x1, Pallas kernels, transition(): pl.pallas_call(transition_kernel, in_specs=in_vmem(4) + [pl.BlockSpec(mem...  9.05 us
    pallas_call x1, Pallas kernels, project(): pl.pallas_call(project_kernel, grid_spec=pltpu.PrefetchScalarGridSpec(num...  7.11 us
    ppermute x6, starting transfers between devices, around_y(): return lax.ppermute(array, ('core', 'y'), up + down)  7.04 us
    ppermute x6, waiting for transfers between devices, around_y(): return lax.ppermute(array, ('core', 'y'), up + down)  5.87 us
  transfers between devices with their start and end apart: 26, of which 8 were waited for; matrix products, arithmetic and copies ran while one was open for 7% of the time, Pallas kernels for 24%

profile of v3, /device:TPU:1, one launch (start us, length us, event | category | flops | bytes accessed | tf_op | source)
XLA Modules:
  0.0 131.0 jit_solution(4173774342296857437)
XLA Ops:
  0.0 3.6 %collective-permute-start = (bf16[192,768]{1,0:T(8,128)(2,1)}, bf16[192,768]{1,0:T(8,128)(2,1)}, u32[]{:S(2)}, u32[]{:S(2)}) collective-permute-start(bf16[192,768]{1,0:T(8,128)(2,1)} %refs_8_.3), channel_id=1, source_target_pairs={{0,2},{2,4},{4,6},{6,0},{16,22},{18,16},{20,18},{22,20},{1,3},{3,5... | collective-permute-start | bytes 884744 | tf_op jit(solution)/shard_map/ppermute | solution.py:434
  3.6 2.5 %collective-permute-start.1 = (bf16[192,768]{1,0:T(8,128)(2,1)}, bf16[192,768]{1,0:T(8,128)(2,1)S(1)}, u32[]{:S(2)}, u32[]{:S(2)}) collective-permute-start(bf16[192,768]{1,0:T(8,128)(2,1)} %refs_8_.3), channel_id=1, source_target_pairs={{0,9},{9,0},{1,8},{8,1},{2,11},{11,2},{3,10},{10,3},{4,13},{13,4},... | collective-permute-start | bytes 884744 | tf_op jit(solution)/shard_map/ppermute | solution.py:437
  6.0 0.7 stack.91.place
  6.7 7.1 %project.1 = (bf16[96,1152]{1,0:T(8,128)(2,1)}, bf16[3,96,1152]{2,1,0:T(8,128)(2,1)}) custom-call(s32[9]{0:T(128)} %stack.91.place, bf16[12,96,768]{2,1,0:T(8,128)(2,1)} %acts.1, bf16[12,96,384]{2,1,0:T(8,128)(2,1)} %cond.1, bf16[384,768]{1,0:T(8,128)(2,1)} %scale.1, bf16[384,768]{1,0:T(8,128)(2,1)} %shift.1, bf16[4,96,768]{2,1,0:T(8,128)(2,1)} %bitcast.61), custom_call_target="tpu_custom_call" | custom-call | bytes 27200000 | tf_op jit(solution)/shard_map/project/pallas_call | solution.py:87
  13.9 0.5 collective-permute-start.2
  14.4 1.9 %collective-permute-done.2 = bf16[3,96,1152]{2,1,0:T(8,128)(2,1)S(1)} collective-permute-done((bf16[3,96,1152]{2,1,0:T(8,128)(2,1)}, bf16[3,96,1152]{2,1,0:T(8,128)(2,1)S(1)}, u32[]{:S(2)}, u32[]{:S(2)}) %collective-permute-start.2) | collective-permute-done | bytes 663584 | tf_op jit(solution)/shard_map/ppermute | solution.py:440
  16.4 1.4 %select_bitcast_fusion.3 = (bf16[96,1152]{1,0:T(8,128)(2,1)S(1)}, bf16[96,1152]{1,0:T(8,128)(2,1)S(1)}, bf16[96,1152]{1,0:T(8,128)(2,1)S(1)}, bf16[96,1152]{1,0:T(8,128)(2,1)S(1)}) fusion(pred[]{:T(512)S(6)} %eq.15, bf16[3,96,1152]{2,1,0:T(8,128)(2,1)S(1)} %collective-permute-done.2, bf16[3,96,1152]{2,1,0:T(8,128)(2,1)} %get-tuple-element.29), kind=kLoop, calls=%fused_computation.16 | loop fusion | flops 442368 | bytes 1769473 | tf_op jit(solution)/shard_map/jit(_where)/select_n | solution.py:458
  18.0 5.6 %collective-permute-start.3 = (bf16[2,192,1152]{2,1,0:T(8,128)(2,1)S(1)}, bf16[2,192,1152]{2,1,0:T(8,128)(2,1)S(1)}, u32[]{:S(2)}, u32[]{:S(2)}) collective-permute-start(bf16[2,192,1152]{2,1,0:T(8,128)(2,1)S(1)} %pad_maximum_fusion.refs_1_), channel_id=1, source_target_pairs={{0,32},{32,64},{64,96},{96,128},{128,160},{160,192},{192,224},{224... | collective-permute-start | bytes 2654216 | tf_op jit(solution)/shard_map/ppermute | solution.py:429
  23.6 0.8 collective-permute-start.5
  24.5 2.3 %collective-permute-start.4 = (bf16[240,768]{1,0:T(8,128)(2,1)S(1)}, bf16[240,768]{1,0:T(8,128)(2,1)}, u32[]{:S(2)}, u32[]{:S(2)}) collective-permute-start(bf16[240,768]{1,0:T(8,128)(2,1)S(1)} %constant_dynamic-slice_fusion.2), channel_id=1, source_target_pairs={{0,9},{9,0},{1,8},{8,1},{2,11},{11,2},{3,10},{10,3},{4,13},{13,4},... | collective-permute-start | bytes 1105928 | tf_op jit(solution)/shard_map/ppermute | solution.py:437
  27.0 1.7 %copy-done = bf16[48,192,128]{2,1,0:T(8,128)(2,1)S(1)} copy-done((bf16[48,192,128]{2,1,0:T(8,128)(2,1)S(1)}, bf16[48,192,128]{2,1,0:T(8,128)(2,1)}, u32[]{:S(2)}) %copy-start) | copy-done | bytes 2359320
  28.7 3.9 %tile_bias.1 = bf16[16,72,128]{2,1,0:T(8,128)(2,1)S(1)} custom-call(bf16[48,192,128]{2,1,0:T(8,128)(2,1)S(1)} %copy-done, bf16[16,128]{1,0:T(8,128)(2,1)S(1)} %bitcast.58), custom_call_target="tpu_custom_call" | custom-call | bytes 20400000 | tf_op jit(solution)/shard_map/tile_bias/pallas_call | solution.py:138
  32.7 4.6 %collective-permute-done.6.refs_11_ = bf16[192,768]{1,0:T(8,128)(2,1)} collective-permute-done((bf16[192,768]{1,0:T(8,128)(2,1)S(1)}, bf16[192,768]{1,0:T(8,128)(2,1)}, u32[]{:S(2)}, u32[]{:S(2)}) %collective-permute-start.6) | collective-permute-done | bytes 294944 | tf_op jit(solution)/shard_map/ppermute | solution.py:434
  37.3 1.5 %collective-permute-done.7 = bf16[16,72,128]{2,1,0:T(8,128)(2,1)S(1)} collective-permute-done((bf16[16,72,128]{2,1,0:T(8,128)(2,1)S(1)}, bf16[16,72,128]{2,1,0:T(8,128)(2,1)S(1)}, u32[]{:S(2)}, u32[]{:S(2)}) %collective-permute-start.7) | collective-permute-done | bytes 294944 | tf_op jit(solution)/shard_map/ppermute | solution.py:476
  38.8 2.7 %collective-permute-start.8 = (bf16[2,192,1152]{2,1,0:T(8,128)(2,1)S(1)}, bf16[2,192,1152]{2,1,0:T(8,128)(2,1)S(1)}, u32[]{:S(2)}, u32[]{:S(2)}) collective-permute-start(bf16[2,192,1152]{2,1,0:T(8,128)(2,1)S(1)} %collective-permute-done.3.refs_2_), channel_id=1, source_target_pairs={{0,32},{32,64},{64,96},{96,128},{128,160},{160,192},{192,224},{224... | collective-permute-start | bytes 2654216 | tf_op jit(solution)/shard_map/ppermute | solution.py:429
  41.6 0.9 copy.20
  42.4 3.9 %all-to-all-start = ((bf16[16,2,72,128]{3,2,1,0:T(8,128)(2,1)}), bf16[16,2,72,128]{3,2,1,0:T(8,128)(2,1)S(1)}, u32[]{:S(2)}, u32[]{:S(2)}) async-start(bf16[16,2,72,128]{3,2,1,0:T(8,128)(2,1)} %copy.20), calls=%async_computation | async-start | bytes 1179648 | tf_op jit(solution)/shard_map/all_to_all | solution.py:482
  46.6 0.3 collective-permute-start.11
  46.9 1.2 broadcast_select_fusion.2
  48.1 0.9 pad_maximum_fusion.1.refs_1_
  49.0 9.3 %all-to-all-done = bf16[16,2,72,128]{3,2,1,0:T(8,128)(2,1)S(1)} async-done(((bf16[16,2,72,128]{3,2,1,0:T(8,128)(2,1)}), bf16[16,2,72,128]{3,2,1,0:T(8,128)(2,1)S(1)}, u32[]{:S(2)}, u32[]{:S(2)}) %all-to-all-start) | async-done | bytes 589856 | tf_op jit(solution)/shard_map/all_to_all | solution.py:482
  58.4 1.2 collective-permute-start.12
  59.5 1.9 %collective-permute-start.10 = (bf16[2,192,1152]{2,1,0:T(8,128)(2,1)S(1)}, bf16[2,192,1152]{2,1,0:T(8,128)(2,1)S(1)}, u32[]{:S(2)}, u32[]{:S(2)}) collective-permute-start(bf16[2,192,1152]{2,1,0:T(8,128)(2,1)S(1)} %collective-permute-done.8.refs_4_), channel_id=1, source_target_pairs={{0,32},{32,64},{64,96},{96,128},{128,160},{160,192},{192,224},{224... | collective-permute-start | bytes 2654216 | tf_op jit(solution)/shard_map/ppermute | solution.py:429
  61.4 0.7 collective-permute-start.13
  62.1 1.0 broadcast_select_fusion.3
  63.2 1.0 broadcast_select_fusion.5
  64.3 4.5 %assemble.1.refs_6_.refs_3_.refs_2_ = f32[8,192,384]{2,1,0:T(8,128)S(1)} custom-call(s32[11]{0:T(128)S(1)} %stack.108.place, bf16[8,2,2,72,128]{4,3,2,1,0:T(8,128)(2,1)S(1)} %bitcast.55, bf16[8,2,2,72,128]{4,3,2,1,0:T(8,128)(2,1)S(1)} %bitcast.56, s32[8,1,192]{2,1,0:T(1,128)S(1)} %reshape.34.refs_2_.refs_3_.refs_6_, ...), custom_call_target="tpu_custom_call" | custom-call | bytes 17000000 | tf_op jit(solution)/shard_map/assemble/pallas_call | solution.py:197
  68.8 5.5 %attend.2.refs_4_ = f32[3,2,56,384]{3,2,1,0:T(8,128)S(1)} custom-call(bf16[192,1152]{1,0:T(8,128)(2,1)S(1)} %pad_maximum_fusion.3.refs_0_, bf16[2,192,1152]{2,1,0:T(8,128)(2,1)S(1)} %pad_maximum_fusion.refs_1_, bf16[2,192,1152]{2,1,0:T(8,128)(2,1)S(1)} %collective-permute-done.3.refs_2_, bf16[2,192,1152]{2,1,0:T(8,128)(2,1)} %collective-permute-done.11.refs_3_, ...), custom_call_target="tpu_custom_call" | custom-call | bytes 23800000 | tf_op jit(solution)/shard_map/attend/pallas_call | solution.py:288
  74.3 1.2 collective-permute-done.14.refs_14_
  75.5 1.2 broadcast_select_fusion
  76.7 1.7 %collective-permute-start.17 = (bf16[480,768]{1,0:T(8,128)(2,1)S(1)}, bf16[480,768]{1,0:T(8,128)(2,1)S(1)}, u32[]{:S(2)}, u32[]{:S(2)}) collective-permute-start(bf16[480,768]{1,0:T(8,128)(2,1)S(1)} %broadcast_select_fusion), channel_id=1, source_target_pairs={{0,2},{2,4},{4,6},{6,0},{16,22},{18,16},{20,18},{22,20},{1,3},{3,5... | collective-permute-start | bytes 2211848 | tf_op jit(solution)/shard_map/ppermute | solution.py:434
  78.4 1.7 %collective-permute-start.15 = (bf16[192,1152]{1,0:T(8,128)(2,1)S(1)}, bf16[192,1152]{1,0:T(8,128)(2,1)S(1)}, u32[]{:S(2)}, u32[]{:S(2)}) collective-permute-start(bf16[192,1152]{1,0:T(8,128)(2,1)S(1)} %slice_bitcast_fusion), channel_id=1, source_target_pairs={{0,32},{32,64},{64,96},{96,128},{128,160},{160,192},{192,224},{224... | collective-permute-start | bytes 1327112 | tf_op jit(solution)/shard_map/ppermute | solution.py:429
  80.2 0.5 collective-permute-start.18
  80.8 2.6 %attend.3.refs_3_ = f32[3,2,56,384]{3,2,1,0:T(8,128)S(1)} custom-call(bf16[192,1152]{1,0:T(8,128)(2,1)S(1)} %pad_maximum_fusion.3.refs_0_, bf16[2,192,1152]{2,1,0:T(8,128)(2,1)S(1)} %collective-permute-done.10.refs_1_, bf16[2,192,1152]{2,1,0:T(8,128)(2,1)S(1)} %collective-permute-done.16.refs_2_, f32[8,192,384]{2,1,0:T(8,128)S(1)} %assemble.1.refs_6_.refs_3_.refs_2_, ...), custom_call_target="tpu_custom_call" | custom-call | bytes 13600000 | tf_op jit(solution)/shard_map/attend/pallas_call | solution.py:288
  83.4 2.9 %collective-permute-done.15.refs_1_ = bf16[192,1152]{1,0:T(8,128)(2,1)S(1)} collective-permute-done((bf16[192,1152]{1,0:T(8,128)(2,1)S(1)}, bf16[192,1152]{1,0:T(8,128)(2,1)S(1)}, u32[]{:S(2)}, u32[]{:S(2)}) %collective-permute-start.15) | collective-permute-done | bytes 442400 | tf_op jit(solution)/shard_map/ppermute | solution.py:429
  86.3 3.0 %attend_last.1 = bf16[16,48,144]{2,1,0:T(8,128)(2,1)} custom-call(bf16[192,1152]{1,0:T(8,128)(2,1)S(1)} %pad_maximum_fusion.3.refs_0_, bf16[192,1152]{1,0:T(8,128)(2,1)S(1)} %collective-permute-done.15.refs_1_, f32[8,192,384]{2,1,0:T(8,128)S(1)} %assemble.1.refs_6_.refs_3_.refs_2_, f32[3,2,56,384]{3,2,1,0:T(8,128)S(1)} %attend.3.refs_3_), custom_call_target="tpu_custom_call" | custom-call | bytes 10200000 | tf_op jit(solution)/shard_map/attend_last/pallas_call | solution.py:288
  89.4 2.2 %collective-permute-start.20 = (bf16[480,768]{1,0:T(8,128)(2,1)S(1)}, bf16[480,768]{1,0:T(8,128)(2,1)S(1)}, u32[]{:S(2)}, u32[]{:S(2)}) collective-permute-start(bf16[480,768]{1,0:T(8,128)(2,1)S(1)} %collective-permute-done.17.refs_6_), channel_id=1, source_target_pairs={{0,16},{16,0},{1,17},{17,1},{2,18},{18,2},{3,19},{19,3},{4,20},{20... | collective-permute-start | bytes 2211848 | tf_op jit(solution)/shard_map/ppermute | solution.py:440
  91.7 0.4 collective-permute-start.22
  92.2 4.1 %all-to-all-start.1 = ((bf16[16,48,144]{2,1,0:T(8,128)(2,1)}), bf16[16,48,144]{2,1,0:T(8,128)(2,1)S(1)}, u32[]{:S(2)}, u32[]{:S(2)}) async-start(bf16[16,48,144]{2,1,0:T(8,128)(2,1)} %attend_last.1), calls=%async_computation.1 | async-start | bytes 786432 | tf_op jit(solution)/shard_map/all_to_all | solution.py:512
  96.3 1.6 %constant_dynamic-slice_fusion = bf16[3,48,384]{2,1,0:T(8,128)(2,1)} fusion(bf16[12,96,384]{2,1,0:T(8,128)(2,1)} %cond.1, s32[]{:T(128)S(6)} %select_n.176, s32[]{:T(128)S(6)} %select_n.177), kind=kLoop, calls=%fused_computation.19 | loop fusion | bytes 221192 | tf_op jit(solution)/shard_map/dynamic_slice | solution.py:517
  97.8 1.6 %constant_dynamic-slice_fusion.1 = bf16[3,48,768]{2,1,0:T(8,128)(2,1)} fusion(bf16[12,96,768]{2,1,0:T(8,128)(2,1)} %acts.1, s32[]{:T(128)S(6)} %select_n.176, s32[]{:T(128)S(6)} %select_n.177), kind=kLoop, calls=%fused_computation.20 | loop fusion | bytes 442376 | tf_op jit(solution)/shard_map/dynamic_slice | solution.py:517
  99.5 0.8 copy-done.6
  100.6 4.5 %condition.1.mix = f32[4,144,768]{2,1,0:T(8,128)} custom-call(s32[9]{0:T(128)} %stack.91.place, bf16[144,384]{1,0:T(8,128)(2,1)} %bitcast.63, bf16[480,768]{1,0:T(8,128)(2,1)} %copy-done.3, bf16[480,768]{1,0:T(8,128)(2,1)} %pad_maximum_fusion.1.refs_1_, bf16[480,768]{1,0:T(8,128)(2,1)} %collective-permute-done.5.refs_2_, ...), custom_call_target="tpu_custom_call" | custom-call | bytes 13600000 | tf_op jit(solution)/shard_map/condition/pallas_call | solution.py:327
  105.1 1.0 all-to-all-done.1.heads
  106.2 0.8 copy-done.8
  107.0 9.1 %transition.1 = bf16[8,144,96]{2,1,0:T(8,128)(2,1)} custom-call(bf16[16,48,144]{2,1,0:T(8,128)(2,1)} %copy-done.8, bf16[144,768]{1,0:T(8,128)(2,1)} %bitcast.60, f32[4,144,768]{2,1,0:T(8,128)} %condition.1.mix, bf16[768,768]{1,0:T(8,128)(2,1)} %w_out.1, bf16[480,768]{1,0:T(8,128)(2,1)} %copy-done.3, bf16[480,768]{1,0:T(8,128)(2,1)} %pad_maximum_fusion.1.refs_1_, ...), custom_call_target="tpu_custom_call" | custom-call | bytes 27200000 | tf_op jit(solution)/shard_map/transition/pallas_call | solution.py:385
  116.0 14.2 %all_to_all.15 = bf16[8,144,96]{2,1,0:T(8,128)(2,1)S(1)} all-to-all(bf16[8,144,96]{2,1,0:T(8,128)(2,1)} %transition.1), channel_id=1, replica_groups=mesh['z'=8,'core'=2,'xh'=2,'y'=4,'samp'=2] {'xh','y'}, dimensions={0} | all-to-all | bytes 442368 | tf_op jit(solution)/shard_map/all_to_all | solution.py:524
  130.3 0.7 copy.21
  (68 shorter events, 1.8 us)
Async XLA Ops:
  0.0 13.8 %collective-permute-start = (bf16[192,768]{1,0:T(8,128)(2,1)}, bf16[192,768]{1,0:T(8,128)(2,1)}, u32[]{:S(2)}, u32[]{:S(2)}) collective-permute-start(bf16[192,768]{1,0:T(8,128)(2,1)} %refs_8_.3), channel_id=1, source_target_pairs={{0,2},{2,4},{4,6},{6,0},{16,22},{18,16},{20,18},{22,20},{1,3},{3,5... | collective-permute-start | bytes 884744 | tf_op jit(solution)/shard_map/ppermute | solution.py:434
  3.6 10.3 %collective-permute-start.1 = (bf16[192,768]{1,0:T(8,128)(2,1)}, bf16[192,768]{1,0:T(8,128)(2,1)S(1)}, u32[]{:S(2)}, u32[]{:S(2)}) collective-permute-start(bf16[192,768]{1,0:T(8,128)(2,1)} %refs_8_.3), channel_id=1, source_target_pairs={{0,9},{9,0},{1,8},{8,1},{2,11},{11,2},{3,10},{10,3},{4,13},{13,4},... | collective-permute-start | bytes 884744 | tf_op jit(solution)/shard_map/ppermute | solution.py:437
  13.9 13.0 %copy-start.11 = (bf16[192,768]{1,0:T(8,128)(2,1)}, bf16[192,768]{1,0:T(8,128)(2,1)S(1)}, u32[]{:S(2)}) copy-start(bf16[192,768]{1,0:T(8,128)(2,1)S(1)} %collective-permute-done.1.refs_9_) | copy-start | bytes 884740
  13.9 2.5 %collective-permute-start.2 = (bf16[3,96,1152]{2,1,0:T(8,128)(2,1)}, bf16[3,96,1152]{2,1,0:T(8,128)(2,1)S(1)}, u32[]{:S(2)}, u32[]{:S(2)}) collective-permute-start(bf16[3,96,1152]{2,1,0:T(8,128)(2,1)} %get-tuple-element.29), channel_id=1, source_target_pairs={{0,16},{16,0},{1,17},{17,1},{2,18},{18,2},{3,19},{19,3},{4,20},{20... | collective-permute-start | bytes 1990664 | tf_op jit(solution)/shard_map/ppermute | solution.py:440
  16.4 1.4 %copy-start.9 = (bf16[3,96,1152]{2,1,0:T(8,128)(2,1)}, bf16[3,96,1152]{2,1,0:T(8,128)(2,1)S(1)}, u32[]{:S(2)}) copy-start(bf16[3,96,1152]{2,1,0:T(8,128)(2,1)S(1)} %collective-permute-done.2) | copy-start | bytes 1990660
  17.7 5.8 %copy-start.10 = (bf16[2,768,192]{1,2,0:T(8,128)(2,1)S(1)}, bf16[2,768,192]{1,2,0:T(8,128)(2,1)}, u32[]{:S(2)}) copy-start(bf16[2,768,192]{1,2,0:T(8,128)(2,1)} %param.31) | copy-start | bytes 1769476
  17.8 5.8 %copy-start.13 = (bf16[384,96]{0,1:T(8,128)(2,1)S(1)}, bf16[384,96]{0,1:T(8,128)(2,1)}, u32[]{:S(2)}) copy-start(bf16[384,96]{0,1:T(8,128)(2,1)} %param.33) | copy-start | bytes 221188
  17.8 5.8 %copy-start.14 = (bf16[384,96]{0,1:T(8,128)(2,1)S(1)}, bf16[384,96]{0,1:T(8,128)(2,1)}, u32[]{:S(2)}) copy-start(bf16[384,96]{0,1:T(8,128)(2,1)} %param.28) | copy-start | bytes 221188
  18.0 9.1 %copy-start.1 = (bf16[128,16]{0,1:T(8,128)(2,1)S(1)}, bf16[128,16]{0,1:T(8,128)(2,1)}, u32[]{:S(2)}) copy-start(bf16[128,16]{0,1:T(8,128)(2,1)} %param.22) | copy-start | bytes 12292
  18.0 20.8 %collective-permute-start.3 = (bf16[2,192,1152]{2,1,0:T(8,128)(2,1)S(1)}, bf16[2,192,1152]{2,1,0:T(8,128)(2,1)S(1)}, u32[]{:S(2)}, u32[]{:S(2)}) collective-permute-start(bf16[2,192,1152]{2,1,0:T(8,128)(2,1)S(1)} %pad_maximum_fusion.refs_1_), channel_id=1, source_target_pairs={{0,32},{32,64},{64,96},{96,128},{128,160},{160,192},{192,224},{224... | collective-permute-start | bytes 2654216 | tf_op jit(solution)/shard_map/ppermute | solution.py:429
  23.6 8.9 %copy-start.3 = (bf16[480,768]{1,0:T(8,128)(2,1)}, bf16[480,768]{1,0:T(8,128)(2,1)S(1)}, u32[]{:S(2)}) copy-start(bf16[480,768]{1,0:T(8,128)(2,1)S(1)} %maximum_maximum_fusion.refs_0_) | copy-start | bytes 2211844
  23.6 15.2 %collective-permute-start.5 = (bf16[480,768]{1,0:T(8,128)(2,1)S(1)}, bf16[480,768]{1,0:T(8,128)(2,1)}, u32[]{:S(2)}, u32[]{:S(2)}) collective-permute-start(bf16[480,768]{1,0:T(8,128)(2,1)S(1)} %maximum_maximum_fusion.refs_0_), channel_id=1, source_target_pairs={{0,2},{2,4},{4,6},{6,0},{16,22},{18,16},{20,18},{22,20},{1,3},{3,5... | collective-permute-start | bytes 2211848 | tf_op jit(solution)/shard_map/ppermute | solution.py:434
  24.5 14.3 %collective-permute-start.4 = (bf16[240,768]{1,0:T(8,128)(2,1)S(1)}, bf16[240,768]{1,0:T(8,128)(2,1)}, u32[]{:S(2)}, u32[]{:S(2)}) collective-permute-start(bf16[240,768]{1,0:T(8,128)(2,1)S(1)} %constant_dynamic-slice_fusion.2), channel_id=1, source_target_pairs={{0,9},{9,0},{1,8},{8,1},{2,11},{11,2},{3,10},{10,3},{4,13},{13,4},... | collective-permute-start | bytes 1105928 | tf_op jit(solution)/shard_map/ppermute | solution.py:437
  26.8 10.5 %collective-permute-start.6 = (bf16[192,768]{1,0:T(8,128)(2,1)S(1)}, bf16[192,768]{1,0:T(8,128)(2,1)}, u32[]{:S(2)}, u32[]{:S(2)}) collective-permute-start(bf16[192,768]{1,0:T(8,128)(2,1)S(1)} %collective-permute-done.1.refs_9_), channel_id=1, source_target_pairs={{0,2},{2,4},{4,6},{6,0},{16,22},{18,16},{20,18},{22,20},{1,3},{3,5... | collective-permute-start | bytes 884744 | tf_op jit(solution)/shard_map/ppermute | solution.py:434
  27.0 1.7 %copy-start = (bf16[48,192,128]{2,1,0:T(8,128)(2,1)S(1)}, bf16[48,192,128]{2,1,0:T(8,128)(2,1)}, u32[]{:S(2)}) copy-start(bf16[48,192,128]{2,1,0:T(8,128)(2,1)} %pair.1) | copy-start | bytes 7077892
  32.6 6.2 %collective-permute-start.7 = (bf16[16,72,128]{2,1,0:T(8,128)(2,1)S(1)}, bf16[16,72,128]{2,1,0:T(8,128)(2,1)S(1)}, u32[]{:S(2)}, u32[]{:S(2)}) collective-permute-start(bf16[16,72,128]{2,1,0:T(8,128)(2,1)S(1)} %tile_bias.1), channel_id=1, source_target_pairs={{0,1},{1,0},{2,3},{3,2},{4,5},{5,4},{6,7},{7,6},{8,9},{9,8},{10,11... | collective-permute-start | bytes 884744 | tf_op jit(solution)/shard_map/ppermute | solution.py:476
  38.8 19.6 %collective-permute-start.8 = (bf16[2,192,1152]{2,1,0:T(8,128)(2,1)S(1)}, bf16[2,192,1152]{2,1,0:T(8,128)(2,1)S(1)}, u32[]{:S(2)}, u32[]{:S(2)}) collective-permute-start(bf16[2,192,1152]{2,1,0:T(8,128)(2,1)S(1)} %collective-permute-done.3.refs_2_), channel_id=1, source_target_pairs={{0,32},{32,64},{64,96},{96,128},{128,160},{160,192},{192,224},{224... | collective-permute-start | bytes 2654216 | tf_op jit(solution)/shard_map/ppermute | solution.py:429
  41.5 5.5 %collective-permute-start.9 = (bf16[240,768]{1,0:T(8,128)(2,1)}, bf16[240,768]{1,0:T(8,128)(2,1)}, u32[]{:S(2)}, u32[]{:S(2)}) collective-permute-start(bf16[240,768]{1,0:T(8,128)(2,1)} %collective-permute-done.4), channel_id=1, source_target_pairs={{0,16},{16,0},{1,17},{17,1},{2,18},{18,2},{3,19},{19,3},{4,20},{20... | collective-permute-start | bytes 1105928 | tf_op jit(solution)/shard_map/ppermute | solution.py:440
  41.5 4.8 %copy-start.15 = (s32[1536]{0:T(1024)S(1)}, s32[1536]{0:T(1024)}, u32[]{:S(2)}) copy-start(s32[1536]{0:T(1024)} %param.20) | copy-start | bytes 18436
  41.5 4.9 %copy-start.16 = (s32[1536]{0:T(1024)S(1)}, s32[1536]{0:T(1024)}, u32[]{:S(2)}) copy-start(s32[1536]{0:T(1024)} %param.21) | copy-start | bytes 18436
  42.4 16.0 %all-to-all-start = ((bf16[16,2,72,128]{3,2,1,0:T(8,128)(2,1)}), bf16[16,2,72,128]{3,2,1,0:T(8,128)(2,1)S(1)}, u32[]{:S(2)}, u32[]{:S(2)}) async-start(bf16[16,2,72,128]{3,2,1,0:T(8,128)(2,1)} %copy.20), calls=%async_computation | async-start | bytes 1179648 | tf_op jit(solution)/shard_map/all_to_all | solution.py:482
  46.6 22.2 %collective-permute-start.11 = (bf16[2,192,1152]{2,1,0:T(8,128)(2,1)S(1)}, bf16[2,192,1152]{2,1,0:T(8,128)(2,1)}, u32[]{:S(2)}, u32[]{:S(2)}) collective-permute-start(bf16[2,192,1152]{2,1,0:T(8,128)(2,1)S(1)} %collective-permute-done.3.refs_2_), channel_id=1, source_target_pairs={{0,16},{16,0},{1,17},{17,1},{2,18},{18,2},{3,19},{19,3},{4,20},{20... | collective-permute-start | bytes 2654216 | tf_op jit(solution)/shard_map/ppermute | solution.py:440
  48.1 15.1 %copy-start.12 = (bf16[96,1152]{1,0:T(8,128)(2,1)S(1)}, bf16[96,1152]{1,0:T(8,128)(2,1)}, u32[]{:S(2)}) copy-start(bf16[96,1152]{1,0:T(8,128)(2,1)} %get-tuple-element.27) | copy-start | bytes 663556
  49.0 15.2 %copy-start.2 = (f32[2]{0:T(128)S(1)}, f32[2]{0:T(128)}, u32[]{:S(2)}) copy-start(f32[2]{0:T(128)} %refs_7_.1) | copy-start | bytes 28
  58.4 10.4 %collective-permute-start.12 = (bf16[2,192,1152]{2,1,0:T(8,128)(2,1)S(1)}, bf16[2,192,1152]{2,1,0:T(8,128)(2,1)S(1)}, u32[]{:S(2)}, u32[]{:S(2)}) collective-permute-start(bf16[2,192,1152]{2,1,0:T(8,128)(2,1)S(1)} %collective-permute-done.8.refs_4_), channel_id=1, source_target_pairs={{0,16},{16,0},{1,17},{17,1},{2,18},{18,2},{3,19},{19,3},{4,20},{20... | collective-permute-start | bytes 2654216 | tf_op jit(solution)/shard_map/ppermute | solution.py:440
  59.5 16.0 %collective-permute-start.10 = (bf16[2,192,1152]{2,1,0:T(8,128)(2,1)S(1)}, bf16[2,192,1152]{2,1,0:T(8,128)(2,1)S(1)}, u32[]{:S(2)}, u32[]{:S(2)}) collective-permute-start(bf16[2,192,1152]{2,1,0:T(8,128)(2,1)S(1)} %collective-permute-done.8.refs_4_), channel_id=1, source_target_pairs={{0,32},{32,64},{64,96},{96,128},{128,160},{160,192},{192,224},{224... | collective-permute-start | bytes 2654216 | tf_op jit(solution)/shard_map/ppermute | solution.py:429
  61.4 14.1 %collective-permute-start.13 = (bf16[480,768]{1,0:T(8,128)(2,1)}, bf16[480,768]{1,0:T(8,128)(2,1)}, u32[]{:S(2)}, u32[]{:S(2)}) collective-permute-start(bf16[480,768]{1,0:T(8,128)(2,1)} %pad_maximum_fusion.1.refs_1_), channel_id=1, source_target_pairs={{0,2},{2,4},{4,6},{6,0},{16,22},{18,16},{20,18},{22,20},{1,3},{3,5... | collective-permute-start | bytes 2211848 | tf_op jit(solution)/shard_map/ppermute | solution.py:434
  63.1 12.4 %collective-permute-start.14 = (bf16[192,768]{1,0:T(8,128)(2,1)S(1)}, bf16[192,768]{1,0:T(8,128)(2,1)}, u32[]{:S(2)}, u32[]{:S(2)}) collective-permute-start(bf16[192,768]{1,0:T(8,128)(2,1)S(1)} %broadcast_select_fusion.3), channel_id=1, source_target_pairs={{0,2},{2,4},{4,6},{6,0},{16,22},{18,16},{20,18},{22,20},{1,3},{3,5... | collective-permute-start | bytes 884744 | tf_op jit(solution)/shard_map/ppermute | solution.py:434
  76.7 12.7 %collective-permute-start.17 = (bf16[480,768]{1,0:T(8,128)(2,1)S(1)}, bf16[480,768]{1,0:T(8,128)(2,1)S(1)}, u32[]{:S(2)}, u32[]{:S(2)}) collective-permute-start(bf16[480,768]{1,0:T(8,128)(2,1)S(1)} %broadcast_select_fusion), channel_id=1, source_target_pairs={{0,2},{2,4},{4,6},{6,0},{16,22},{18,16},{20,18},{22,20},{1,3},{3,5... | collective-permute-start | bytes 2211848 | tf_op jit(solution)/shard_map/ppermute | solution.py:434
  78.4 2.4 %collective-permute-start.16 = (bf16[2,192,1152]{2,1,0:T(8,128)(2,1)S(1)}, bf16[2,192,1152]{2,1,0:T(8,128)(2,1)S(1)}, u32[]{:S(2)}, u32[]{:S(2)}) collective-permute-start(bf16[2,192,1152]{2,1,0:T(8,128)(2,1)S(1)} %collective-permute-done.10.refs_1_), channel_id=1, source_target_pairs={{0,16},{16,0},{1,17},{17,1},{2,18},{18,2},{3,19},{19,3},{4,20},{20... | collective-permute-start | bytes 2654216 | tf_op jit(solution)/shard_map/ppermute | solution.py:440
  78.4 7.9 %collective-permute-start.15 = (bf16[192,1152]{1,0:T(8,128)(2,1)S(1)}, bf16[192,1152]{1,0:T(8,128)(2,1)S(1)}, u32[]{:S(2)}, u32[]{:S(2)}) collective-permute-start(bf16[192,1152]{1,0:T(8,128)(2,1)S(1)} %slice_bitcast_fusion), channel_id=1, source_target_pairs={{0,32},{32,64},{64,96},{96,128},{128,160},{160,192},{192,224},{224... | collective-permute-start | bytes 1327112 | tf_op jit(solution)/shard_map/ppermute | solution.py:429
  80.2 11.9 %collective-permute-start.18 = (bf16[480,768]{1,0:T(8,128)(2,1)}, bf16[480,768]{1,0:T(8,128)(2,1)S(1)}, u32[]{:S(2)}, u32[]{:S(2)}) collective-permute-start(bf16[480,768]{1,0:T(8,128)(2,1)} %collective-permute-done.5.refs_2_), channel_id=1, source_target_pairs={{0,16},{16,0},{1,17},{17,1},{2,18},{18,2},{3,19},{19,3},{4,20},{20... | collective-permute-start | bytes 2211848 | tf_op jit(solution)/shard_map/ppermute | solution.py:440
  80.6 18.8 %collective-permute-start.19 = (bf16[480,768]{1,0:T(8,128)(2,1)}, bf16[480,768]{1,0:T(8,128)(2,1)S(1)}, u32[]{:S(2)}, u32[]{:S(2)}) collective-permute-start(bf16[480,768]{1,0:T(8,128)(2,1)} %collective-permute-done.13.refs_3_), channel_id=1, source_target_pairs={{0,16},{16,0},{1,17},{17,1},{2,18},{18,2},{3,19},{19,3},{4,20},{20... | collective-permute-start | bytes 2211848 | tf_op jit(solution)/shard_map/ppermute | solution.py:440
  89.4 10.1 %copy-start.4 = (bf16[480,768]{1,0:T(8,128)(2,1)}, bf16[480,768]{1,0:T(8,128)(2,1)S(1)}, u32[]{:S(2)}) copy-start(bf16[480,768]{1,0:T(8,128)(2,1)S(1)} %collective-permute-done.17.refs_6_) | copy-start | bytes 2211844
  89.4 10.1 %collective-permute-start.20 = (bf16[480,768]{1,0:T(8,128)(2,1)S(1)}, bf16[480,768]{1,0:T(8,128)(2,1)S(1)}, u32[]{:S(2)}, u32[]{:S(2)}) collective-permute-start(bf16[480,768]{1,0:T(8,128)(2,1)S(1)} %collective-permute-done.17.refs_6_), channel_id=1, source_target_pairs={{0,16},{16,0},{1,17},{17,1},{2,18},{18,2},{3,19},{19,3},{4,20},{20... | collective-permute-start | bytes 2211848 | tf_op jit(solution)/shard_map/ppermute | solution.py:440
  91.6 13.5 %collective-permute-start.21 = (bf16[192,768]{1,0:T(8,128)(2,1)}, bf16[192,768]{1,0:T(8,128)(2,1)}, u32[]{:S(2)}, u32[]{:S(2)}) collective-permute-start(bf16[192,768]{1,0:T(8,128)(2,1)} %collective-permute-done.refs_10_), channel_id=1, source_target_pairs={{0,16},{16,0},{1,17},{17,1},{2,18},{18,2},{3,19},{19,3},{4,20},{20... | collective-permute-start | bytes 884744 | tf_op jit(solution)/shard_map/ppermute | solution.py:440
  91.7 13.4 %collective-permute-start.22 = (bf16[192,768]{1,0:T(8,128)(2,1)}, bf16[192,768]{1,0:T(8,128)(2,1)}, u32[]{:S(2)}, u32[]{:S(2)}) collective-permute-start(bf16[192,768]{1,0:T(8,128)(2,1)} %collective-permute-done.6.refs_11_), channel_id=1, source_target_pairs={{0,16},{16,0},{1,17},{17,1},{2,18},{18,2},{3,19},{19,3},{4,20},{20... | collective-permute-start | bytes 884744 | tf_op jit(solution)/shard_map/ppermute | solution.py:440
  92.1 7.4 %copy-start.5 = (bf16[480,768]{1,0:T(8,128)(2,1)}, bf16[480,768]{1,0:T(8,128)(2,1)S(1)}, u32[]{:S(2)}) copy-start(bf16[480,768]{1,0:T(8,128)(2,1)S(1)} %collective-permute-done.18.refs_4_) | copy-start | bytes 2211844
  92.1 13.0 %collective-permute-start.23 = (bf16[192,768]{1,0:T(8,128)(2,1)}, bf16[192,768]{1,0:T(8,128)(2,1)}, u32[]{:S(2)}, u32[]{:S(2)}) collective-permute-start(bf16[192,768]{1,0:T(8,128)(2,1)} %collective-permute-done.14.refs_14_), channel_id=1, source_target_pairs={{0,16},{16,0},{1,17},{17,1},{2,18},{18,2},{3,19},{19,3},{4,20},{20... | collective-permute-start | bytes 884744 | tf_op jit(solution)/shard_map/ppermute | solution.py:440
  92.2 14.0 %all-to-all-start.1 = ((bf16[16,48,144]{2,1,0:T(8,128)(2,1)}), bf16[16,48,144]{2,1,0:T(8,128)(2,1)S(1)}, u32[]{:S(2)}, u32[]{:S(2)}) async-start(bf16[16,48,144]{2,1,0:T(8,128)(2,1)} %attend_last.1), calls=%async_computation.1 | async-start | bytes 786432 | tf_op jit(solution)/shard_map/all_to_all | solution.py:512
  99.5 0.9 copy-start.6
  99.5 1.1 copy-start.7
  106.2 0.8 copy-start.8

commit v4 on v3

--- a/solution.py
+++ b/solution.py
@@ -484,7 +484,8 @@
     two = around(one)
     one_x = cross(one)
     qg = in_order(stay, got[2])
-    two, up_far, tiles = lax.optimization_barrier((two, up_far, tiles))
+    two, up_far = lax.optimization_barrier((two, up_far))
+    up_far, tiles = lax.optimization_barrier((up_far, tiles))
     side = jnp.where(lower, 1, 7)
     order = [z] + [n for s in (1, 2, 3) for n in (z + 8 * 3 - s * side, z + s * side)] + [z + 4]
     place = jnp.stack([n % 8 for n in order] + [z, core, samp]).astype(jnp.int32)
@@ -495,9 +496,7 @@
     down_last = around_y(jnp.where(lower, w_down_y, down_far_y))
     parts = [(chunk, 0), (one, 0), (one_x, 1), (two, 0), (two_x, 1)]
     state = attend(qg, parts, bias, 0, None, False)
-    three, state, up_far_y, down_last = lax.optimization_barrier(
-        (three, state, up_far_y, down_last)
-    )
+    state, up_far_y, down_last = lax.optimization_barrier((state, up_far_y, down_last))
     four = around(three[0])
     up_last = around_y(jnp.where(lower, up_y, up_far_y))
     three_x = cross(three)

time: 132 us -> 131 us (level)
    ppermute x4, waiting for transfers between devices: 2.94 us -> 5.4 us  [around(): return lax.ppermute(array, ('z', 'core'), up + down)]
    all_to_all x1, waiting for transfers between devices: 9.34 us -> 6.91 us  [per_device(): lax.all_to_all(tiles, PLANE, split_axis=0, concat_axis=0, tiled=True)]
  transfers between devices with their start and end apart: 26 -> 26, of which waited for: 8 -> 7; matrix products, arithmetic and copies ran while one was open for 7% -> 8% of each run, Pallas kernels for 24% -> 24%
where the time goes in v4:
time: 131 us; the launch traced here: 130 us
  Pallas kernels  40.1 us (31%)
  starting transfers between devices  37.5 us (29%)
  waiting for transfers between devices  21.5 us (16%)
  blocking collectives  14.2 us (11%)
  local copies, waits for them, and re-layouts  9.4 us (7%)
  other arithmetic  6.95 us (5%)
    all_to_all x1, blocking collectives, per_device(): out = lax.all_to_all(out, COL, split_axis=0, concat_axis=0, tiled=True)  14.2 us
    ppermute x4, starting transfers between devices, around(): return lax.ppermute(array, ('z', 'core'), up + down)  12.2 us
    pallas_call x3, Pallas kernels, attend(): pl.pallas_call(functools.partial(attend_kernel, state is None, last, pick...  11.1 us
    pallas_call x1, Pallas kernels, transition(): pl.pallas_call(transition_kernel, in_specs=in_vmem(4) + [pl.BlockSpec(mem...  9.06 us
    pallas_call x1, Pallas kernels, project(): pl.pallas_call(project_kernel, grid_spec=pltpu.PrefetchScalarGridSpec(num...  7.11 us
    all_to_all x1, waiting for transfers between devices, per_device(): lax.all_to_all(tiles, PLANE, split_axis=0, concat_axis=0, tiled=True)  6.91 us
    ppermute x6, starting transfers between devices, around_y(): return lax.ppermute(array, ('core', 'y'), up + down)  6.44 us
    ppermute x4, waiting for transfers between devices, around(): return lax.ppermute(array, ('z', 'core'), up + down)  5.4 us
  transfers between devices with their start and end apart: 26, of which 7 were waited for; matrix products, arithmetic and copies ran while one was open for 8% of the time, Pallas kernels for 24%

profile of v4, /device:TPU:1, one launch (start us, length us, event | category | flops | bytes accessed | tf_op | source)
XLA Modules:
  0.0 130.0 jit_solution(247870568241791061)
XLA Ops:
  0.0 3.6 %collective-permute-start = (bf16[192,768]{1,0:T(8,128)(2,1)}, bf16[192,768]{1,0:T(8,128)(2,1)}, u32[]{:S(2)}, u32[]{:S(2)}) collective-permute-start(bf16[192,768]{1,0:T(8,128)(2,1)} %refs_8_.3), channel_id=1, source_target_pairs={{0,2},{2,4},{4,6},{6,0},{16,22},{18,16},{20,18},{22,20},{1,3},{3,5... | collective-permute-start | bytes 884744 | tf_op jit(solution)/shard_map/ppermute | solution.py:434
  3.6 2.5 %collective-permute-start.1 = (bf16[192,768]{1,0:T(8,128)(2,1)}, bf16[192,768]{1,0:T(8,128)(2,1)S(1)}, u32[]{:S(2)}, u32[]{:S(2)}) collective-permute-start(bf16[192,768]{1,0:T(8,128)(2,1)} %refs_8_.3), channel_id=1, source_target_pairs={{0,9},{9,0},{1,8},{8,1},{2,11},{11,2},{3,10},{10,3},{4,13},{13,4},... | collective-permute-start | bytes 884744 | tf_op jit(solution)/shard_map/ppermute | solution.py:437
  6.0 0.7 stack.91.place
  6.7 7.1 %project.1 = (bf16[96,1152]{1,0:T(8,128)(2,1)}, bf16[3,96,1152]{2,1,0:T(8,128)(2,1)}) custom-call(s32[9]{0:T(128)} %stack.91.place, bf16[12,96,768]{2,1,0:T(8,128)(2,1)} %acts.1, bf16[12,96,384]{2,1,0:T(8,128)(2,1)} %cond.1, bf16[384,768]{1,0:T(8,128)(2,1)} %scale.1, bf16[384,768]{1,0:T(8,128)(2,1)} %shift.1, bf16[4,96,768]{2,1,0:T(8,128)(2,1)} %bitcast.61), custom_call_target="tpu_custom_call" | custom-call | bytes 27200000 | tf_op jit(solution)/shard_map/project/pallas_call | solution.py:87
  13.9 0.5 collective-permute-start.2
  14.4 1.9 %collective-permute-done.2 = bf16[3,96,1152]{2,1,0:T(8,128)(2,1)S(1)} collective-permute-done((bf16[3,96,1152]{2,1,0:T(8,128)(2,1)}, bf16[3,96,1152]{2,1,0:T(8,128)(2,1)S(1)}, u32[]{:S(2)}, u32[]{:S(2)}) %collective-permute-start.2) | collective-permute-done | bytes 663584 | tf_op jit(solution)/shard_map/ppermute | solution.py:440
  16.4 1.4 %select_bitcast_fusion.3 = (bf16[96,1152]{1,0:T(8,128)(2,1)S(1)}, bf16[96,1152]{1,0:T(8,128)(2,1)S(1)}, bf16[96,1152]{1,0:T(8,128)(2,1)S(1)}, bf16[96,1152]{1,0:T(8,128)(2,1)S(1)}) fusion(pred[]{:T(512)S(6)} %eq.15, bf16[3,96,1152]{2,1,0:T(8,128)(2,1)S(1)} %collective-permute-done.2, bf16[3,96,1152]{2,1,0:T(8,128)(2,1)} %get-tuple-element.29), kind=kLoop, calls=%fused_computation.16 | loop fusion | flops 442368 | bytes 1769473 | tf_op jit(solution)/shard_map/jit(_where)/select_n | solution.py:458
  18.0 5.6 %collective-permute-start.3 = (bf16[2,192,1152]{2,1,0:T(8,128)(2,1)S(1)}, bf16[2,192,1152]{2,1,0:T(8,128)(2,1)S(1)}, u32[]{:S(2)}, u32[]{:S(2)}) collective-permute-start(bf16[2,192,1152]{2,1,0:T(8,128)(2,1)S(1)} %pad_maximum_fusion.refs_1_), channel_id=1, source_target_pairs={{0,32},{32,64},{64,96},{96,128},{128,160},{160,192},{192,224},{224... | collective-permute-start | bytes 2654216 | tf_op jit(solution)/shard_map/ppermute | solution.py:429
  23.6 0.8 collective-permute-start.5
  24.5 2.3 %collective-permute-start.4 = (bf16[240,768]{1,0:T(8,128)(2,1)S(1)}, bf16[240,768]{1,0:T(8,128)(2,1)}, u32[]{:S(2)}, u32[]{:S(2)}) collective-permute-start(bf16[240,768]{1,0:T(8,128)(2,1)S(1)} %constant_dynamic-slice_fusion.2), channel_id=1, source_target_pairs={{0,9},{9,0},{1,8},{8,1},{2,11},{11,2},{3,10},{10,3},{4,13},{13,4},... | collective-permute-start | bytes 1105928 | tf_op jit(solution)/shard_map/ppermute | solution.py:437
  27.0 1.7 %copy-done = bf16[48,192,128]{2,1,0:T(8,128)(2,1)S(1)} copy-done((bf16[48,192,128]{2,1,0:T(8,128)(2,1)S(1)}, bf16[48,192,128]{2,1,0:T(8,128)(2,1)}, u32[]{:S(2)}) %copy-start) | copy-done | bytes 2359320
  28.7 3.9 %tile_bias.1 = bf16[16,72,128]{2,1,0:T(8,128)(2,1)S(1)} custom-call(bf16[48,192,128]{2,1,0:T(8,128)(2,1)S(1)} %copy-done, bf16[16,128]{1,0:T(8,128)(2,1)S(1)} %bitcast.58), custom_call_target="tpu_custom_call" | custom-call | bytes 20400000 | tf_op jit(solution)/shard_map/tile_bias/pallas_call | solution.py:138
  32.7 4.6 %collective-permute-done.6.refs_11_ = bf16[192,768]{1,0:T(8,128)(2,1)} collective-permute-done((bf16[192,768]{1,0:T(8,128)(2,1)S(1)}, bf16[192,768]{1,0:T(8,128)(2,1)}, u32[]{:S(2)}, u32[]{:S(2)}) %collective-permute-start.6) | collective-permute-done | bytes 294944 | tf_op jit(solution)/shard_map/ppermute | solution.py:434
  37.3 1.5 %collective-permute-done.7 = bf16[16,72,128]{2,1,0:T(8,128)(2,1)S(1)} collective-permute-done((bf16[16,72,128]{2,1,0:T(8,128)(2,1)S(1)}, bf16[16,72,128]{2,1,0:T(8,128)(2,1)S(1)}, u32[]{:S(2)}, u32[]{:S(2)}) %collective-permute-start.7) | collective-permute-done | bytes 294944 | tf_op jit(solution)/shard_map/ppermute | solution.py:476
  38.8 2.7 %collective-permute-start.8 = (bf16[2,192,1152]{2,1,0:T(8,128)(2,1)S(1)}, bf16[2,192,1152]{2,1,0:T(8,128)(2,1)S(1)}, u32[]{:S(2)}, u32[]{:S(2)}) collective-permute-start(bf16[2,192,1152]{2,1,0:T(8,128)(2,1)S(1)} %collective-permute-done.3.refs_2_), channel_id=1, source_target_pairs={{0,32},{32,64},{64,96},{96,128},{128,160},{160,192},{192,224},{224... | collective-permute-start | bytes 2654216 | tf_op jit(solution)/shard_map/ppermute | solution.py:429
  41.6 0.9 copy.20
  42.4 3.9 %all-to-all-start = ((bf16[16,2,72,128]{3,2,1,0:T(8,128)(2,1)}), bf16[16,2,72,128]{3,2,1,0:T(8,128)(2,1)S(1)}, u32[]{:S(2)}, u32[]{:S(2)}) async-start(bf16[16,2,72,128]{3,2,1,0:T(8,128)(2,1)} %copy.20), calls=%async_computation | async-start | bytes 1179648 | tf_op jit(solution)/shard_map/all_to_all | solution.py:482
  46.9 1.2 broadcast_select_fusion.2
  48.1 0.9 pad_maximum_fusion.1.refs_1_
  49.0 2.4 %collective-permute-done.8.refs_4_ = bf16[2,192,1152]{2,1,0:T(8,128)(2,1)S(1)} collective-permute-done((bf16[2,192,1152]{2,1,0:T(8,128)(2,1)S(1)}, bf16[2,192,1152]{2,1,0:T(8,128)(2,1)S(1)}, u32[]{:S(2)}, u32[]{:S(2)}) %collective-permute-start.8) | collective-permute-done | bytes 884768 | tf_op jit(solution)/shard_map/ppermute | solution.py:429
  51.5 6.9 %all-to-all-done = bf16[16,2,72,128]{3,2,1,0:T(8,128)(2,1)S(1)} async-done(((bf16[16,2,72,128]{3,2,1,0:T(8,128)(2,1)}), bf16[16,2,72,128]{3,2,1,0:T(8,128)(2,1)S(1)}, u32[]{:S(2)}, u32[]{:S(2)}) %all-to-all-start) | async-done | bytes 589856 | tf_op jit(solution)/shard_map/all_to_all | solution.py:482
  58.4 1.2 collective-permute-start.14
  59.5 0.7 collective-permute-start.15
  60.2 1.0 broadcast_select_fusion.3
  61.5 2.0 %collective-permute-start.10 = (bf16[2,192,1152]{2,1,0:T(8,128)(2,1)S(1)}, bf16[2,192,1152]{2,1,0:T(8,128)(2,1)S(1)}, u32[]{:S(2)}, u32[]{:S(2)}) collective-permute-start(bf16[2,192,1152]{2,1,0:T(8,128)(2,1)S(1)} %collective-permute-done.8.refs_4_), channel_id=1, source_target_pairs={{0,32},{32,64},{64,96},{96,128},{128,160},{160,192},{192,224},{224... | collective-permute-start | bytes 2654216 | tf_op jit(solution)/shard_map/ppermute | solution.py:429
  63.5 1.0 broadcast_select_fusion.5
  64.5 4.5 %assemble.1.refs_6_.refs_3_.refs_2_ = f32[8,192,384]{2,1,0:T(8,128)S(1)} custom-call(s32[11]{0:T(128)S(1)} %stack.105.place, bf16[8,2,2,72,128]{4,3,2,1,0:T(8,128)(2,1)S(1)} %bitcast.55, bf16[8,2,2,72,128]{4,3,2,1,0:T(8,128)(2,1)S(1)} %bitcast.56, s32[8,1,192]{2,1,0:T(1,128)S(1)} %reshape.34.refs_2_.refs_3_.refs_6_, ...), custom_call_target="tpu_custom_call" | custom-call | bytes 17000000 | tf_op jit(solution)/shard_map/assemble/pallas_call | solution.py:197
  69.0 5.5 %attend.2.refs_4_ = f32[3,2,56,384]{3,2,1,0:T(8,128)S(1)} custom-call(bf16[192,1152]{1,0:T(8,128)(2,1)S(1)} %pad_maximum_fusion.3.refs_0_, bf16[2,192,1152]{2,1,0:T(8,128)(2,1)S(1)} %pad_maximum_fusion.refs_1_, bf16[2,192,1152]{2,1,0:T(8,128)(2,1)S(1)} %collective-permute-done.3.refs_2_, bf16[2,192,1152]{2,1,0:T(8,128)(2,1)} %collective-permute-done.13.refs_3_, ...), custom_call_target="tpu_custom_call" | custom-call | bytes 23800000 | tf_op jit(solution)/shard_map/attend/pallas_call | solution.py:288
  74.5 1.2 broadcast_select_fusion
  75.7 0.9 collective-permute-start.17
  76.7 0.4 collective-permute-start.12
  77.1 1.9 %collective-permute-start.11 = (bf16[192,1152]{1,0:T(8,128)(2,1)S(1)}, bf16[192,1152]{1,0:T(8,128)(2,1)S(1)}, u32[]{:S(2)}, u32[]{:S(2)}) collective-permute-start(bf16[192,1152]{1,0:T(8,128)(2,1)S(1)} %slice_bitcast_fusion), channel_id=1, source_target_pairs={{0,32},{32,64},{64,96},{96,128},{128,160},{160,192},{192,224},{224... | collective-permute-start | bytes 1327112 | tf_op jit(solution)/shard_map/ppermute | solution.py:429
  79.1 0.3 collective-permute-start.18
  79.6 2.6 %attend.3.refs_3_ = f32[3,2,56,384]{3,2,1,0:T(8,128)S(1)} custom-call(bf16[192,1152]{1,0:T(8,128)(2,1)S(1)} %pad_maximum_fusion.3.refs_0_, bf16[2,192,1152]{2,1,0:T(8,128)(2,1)S(1)} %collective-permute-done.10.refs_1_, bf16[2,192,1152]{2,1,0:T(8,128)(2,1)S(1)} %collective-permute-done.12.refs_2_, f32[8,192,384]{2,1,0:T(8,128)S(1)} %assemble.1.refs_6_.refs_3_.refs_2_, ...), custom_call_target="tpu_custom_call" | custom-call | bytes 13600000 | tf_op jit(solution)/shard_map/attend/pallas_call | solution.py:288
  82.1 3.0 %collective-permute-done.11.refs_1_ = bf16[192,1152]{1,0:T(8,128)(2,1)S(1)} collective-permute-done((bf16[192,1152]{1,0:T(8,128)(2,1)S(1)}, bf16[192,1152]{1,0:T(8,128)(2,1)S(1)}, u32[]{:S(2)}, u32[]{:S(2)}) %collective-permute-start.11) | collective-permute-done | bytes 442400 | tf_op jit(solution)/shard_map/ppermute | solution.py:429
  85.1 3.0 %attend_last.1 = bf16[16,48,144]{2,1,0:T(8,128)(2,1)} custom-call(bf16[192,1152]{1,0:T(8,128)(2,1)S(1)} %pad_maximum_fusion.3.refs_0_, bf16[192,1152]{1,0:T(8,128)(2,1)S(1)} %collective-permute-done.11.refs_1_, f32[8,192,384]{2,1,0:T(8,128)S(1)} %assemble.1.refs_6_.refs_3_.refs_2_, f32[3,2,56,384]{3,2,1,0:T(8,128)S(1)} %attend.3.refs_3_), custom_call_target="tpu_custom_call" | custom-call | bytes 10200000 | tf_op jit(solution)/shard_map/attend_last/pallas_call | solution.py:288
  88.2 1.7 %collective-permute-start.20 = (bf16[480,768]{1,0:T(8,128)(2,1)S(1)}, bf16[480,768]{1,0:T(8,128)(2,1)S(1)}, u32[]{:S(2)}, u32[]{:S(2)}) collective-permute-start(bf16[480,768]{1,0:T(8,128)(2,1)S(1)} %collective-permute-done.17.refs_6_), channel_id=1, source_target_pairs={{0,16},{16,0},{1,17},{17,1},{2,18},{18,2},{3,19},{19,3},{4,20},{20... | collective-permute-start | bytes 2211848 | tf_op jit(solution)/shard_map/ppermute | solution.py:440
  90.0 0.4 collective-permute-start.22
  90.5 4.8 %all-to-all-start.1 = ((bf16[16,48,144]{2,1,0:T(8,128)(2,1)}), bf16[16,48,144]{2,1,0:T(8,128)(2,1)S(1)}, u32[]{:S(2)}, u32[]{:S(2)}) async-start(bf16[16,48,144]{2,1,0:T(8,128)(2,1)} %attend_last.1), calls=%async_computation.1 | async-start | bytes 786432 | tf_op jit(solution)/shard_map/all_to_all | solution.py:511
  95.3 1.6 %constant_dynamic-slice_fusion = bf16[3,48,384]{2,1,0:T(8,128)(2,1)} fusion(bf16[12,96,384]{2,1,0:T(8,128)(2,1)} %cond.1, s32[]{:T(128)S(6)} %select_n.176, s32[]{:T(128)S(6)} %select_n.177), kind=kLoop, calls=%fused_computation.19 | loop fusion | bytes 221192 | tf_op jit(solution)/shard_map/dynamic_slice | solution.py:516
  96.8 1.6 %constant_dynamic-slice_fusion.1 = bf16[3,48,768]{2,1,0:T(8,128)(2,1)} fusion(bf16[12,96,768]{2,1,0:T(8,128)(2,1)} %acts.1, s32[]{:T(128)S(6)} %select_n.176, s32[]{:T(128)S(6)} %select_n.177), kind=kLoop, calls=%fused_computation.20 | loop fusion | bytes 442376 | tf_op jit(solution)/shard_map/dynamic_slice | solution.py:516
  98.5 0.8 copy-done.6
  99.6 4.5 %condition.1.mix = f32[4,144,768]{2,1,0:T(8,128)} custom-call(s32[9]{0:T(128)} %stack.91.place, bf16[144,384]{1,0:T(8,128)(2,1)} %bitcast.63, bf16[480,768]{1,0:T(8,128)(2,1)} %copy-done.3, bf16[480,768]{1,0:T(8,128)(2,1)} %pad_maximum_fusion.1.refs_1_, bf16[480,768]{1,0:T(8,128)(2,1)} %collective-permute-done.5.refs_2_, ...), custom_call_target="tpu_custom_call" | custom-call | bytes 13600000 | tf_op jit(solution)/shard_map/condition/pallas_call | solution.py:327
  104.1 1.0 all-to-all-done.1.heads
  105.2 0.8 copy-done.8
  106.0 9.1 %transition.1 = bf16[8,144,96]{2,1,0:T(8,128)(2,1)} custom-call(bf16[16,48,144]{2,1,0:T(8,128)(2,1)} %copy-done.8, bf16[144,768]{1,0:T(8,128)(2,1)} %bitcast.60, f32[4,144,768]{2,1,0:T(8,128)} %condition.1.mix, bf16[768,768]{1,0:T(8,128)(2,1)} %w_out.1, bf16[480,768]{1,0:T(8,128)(2,1)} %copy-done.3, bf16[480,768]{1,0:T(8,128)(2,1)} %pad_maximum_fusion.1.refs_1_, ...), custom_call_target="tpu_custom_call" | custom-call | bytes 27200000 | tf_op jit(solution)/shard_map/transition/pallas_call | solution.py:385
  115.0 14.2 %all_to_all.15 = bf16[8,144,96]{2,1,0:T(8,128)(2,1)S(1)} all-to-all(bf16[8,144,96]{2,1,0:T(8,128)(2,1)} %transition.1), channel_id=1, replica_groups=mesh['z'=8,'core'=2,'xh'=2,'y'=4,'samp'=2] {'xh','y'}, dimensions={0} | all-to-all | bytes 442368 | tf_op jit(solution)/shard_map/all_to_all | solution.py:523
  129.3 0.7 copy.21
  (68 shorter events, 2.3 us)
Async XLA Ops:
  0.0 13.8 %collective-permute-start = (bf16[192,768]{1,0:T(8,128)(2,1)}, bf16[192,768]{1,0:T(8,128)(2,1)}, u32[]{:S(2)}, u32[]{:S(2)}) collective-permute-start(bf16[192,768]{1,0:T(8,128)(2,1)} %refs_8_.3), channel_id=1, source_target_pairs={{0,2},{2,4},{4,6},{6,0},{16,22},{18,16},{20,18},{22,20},{1,3},{3,5... | collective-permute-start | bytes 884744 | tf_op jit(solution)/shard_map/ppermute | solution.py:434
  3.6 10.3 %collective-permute-start.1 = (bf16[192,768]{1,0:T(8,128)(2,1)}, bf16[192,768]{1,0:T(8,128)(2,1)S(1)}, u32[]{:S(2)}, u32[]{:S(2)}) collective-permute-start(bf16[192,768]{1,0:T(8,128)(2,1)} %refs_8_.3), channel_id=1, source_target_pairs={{0,9},{9,0},{1,8},{8,1},{2,11},{11,2},{3,10},{10,3},{4,13},{13,4},... | collective-permute-start | bytes 884744 | tf_op jit(solution)/shard_map/ppermute | solution.py:437
  13.9 13.0 %copy-start.11 = (bf16[192,768]{1,0:T(8,128)(2,1)}, bf16[192,768]{1,0:T(8,128)(2,1)S(1)}, u32[]{:S(2)}) copy-start(bf16[192,768]{1,0:T(8,128)(2,1)S(1)} %collective-permute-done.1.refs_9_) | copy-start | bytes 884740
  13.9 2.5 %collective-permute-start.2 = (bf16[3,96,1152]{2,1,0:T(8,128)(2,1)}, bf16[3,96,1152]{2,1,0:T(8,128)(2,1)S(1)}, u32[]{:S(2)}, u32[]{:S(2)}) collective-permute-start(bf16[3,96,1152]{2,1,0:T(8,128)(2,1)} %get-tuple-element.29), channel_id=1, source_target_pairs={{0,16},{16,0},{1,17},{17,1},{2,18},{18,2},{3,19},{19,3},{4,20},{20... | collective-permute-start | bytes 1990664 | tf_op jit(solution)/shard_map/ppermute | solution.py:440
  16.4 1.4 %copy-start.9 = (bf16[3,96,1152]{2,1,0:T(8,128)(2,1)}, bf16[3,96,1152]{2,1,0:T(8,128)(2,1)S(1)}, u32[]{:S(2)}) copy-start(bf16[3,96,1152]{2,1,0:T(8,128)(2,1)S(1)} %collective-permute-done.2) | copy-start | bytes 1990660
  17.7 5.8 %copy-start.10 = (bf16[2,768,192]{1,2,0:T(8,128)(2,1)S(1)}, bf16[2,768,192]{1,2,0:T(8,128)(2,1)}, u32[]{:S(2)}) copy-start(bf16[2,768,192]{1,2,0:T(8,128)(2,1)} %param.31) | copy-start | bytes 1769476
  17.8 5.8 %copy-start.13 = (bf16[384,96]{0,1:T(8,128)(2,1)S(1)}, bf16[384,96]{0,1:T(8,128)(2,1)}, u32[]{:S(2)}) copy-start(bf16[384,96]{0,1:T(8,128)(2,1)} %param.33) | copy-start | bytes 221188
  17.8 5.8 %copy-start.14 = (bf16[384,96]{0,1:T(8,128)(2,1)S(1)}, bf16[384,96]{0,1:T(8,128)(2,1)}, u32[]{:S(2)}) copy-start(bf16[384,96]{0,1:T(8,128)(2,1)} %param.28) | copy-start | bytes 221188
  18.0 9.1 %copy-start.1 = (bf16[128,16]{0,1:T(8,128)(2,1)S(1)}, bf16[128,16]{0,1:T(8,128)(2,1)}, u32[]{:S(2)}) copy-start(bf16[128,16]{0,1:T(8,128)(2,1)} %param.22) | copy-start | bytes 12292
  18.0 20.8 %collective-permute-start.3 = (bf16[2,192,1152]{2,1,0:T(8,128)(2,1)S(1)}, bf16[2,192,1152]{2,1,0:T(8,128)(2,1)S(1)}, u32[]{:S(2)}, u32[]{:S(2)}) collective-permute-start(bf16[2,192,1152]{2,1,0:T(8,128)(2,1)S(1)} %pad_maximum_fusion.refs_1_), channel_id=1, source_target_pairs={{0,32},{32,64},{64,96},{96,128},{128,160},{160,192},{192,224},{224... | collective-permute-start | bytes 2654216 | tf_op jit(solution)/shard_map/ppermute | solution.py:429
  23.6 8.9 %copy-start.3 = (bf16[480,768]{1,0:T(8,128)(2,1)}, bf16[480,768]{1,0:T(8,128)(2,1)S(1)}, u32[]{:S(2)}) copy-start(bf16[480,768]{1,0:T(8,128)(2,1)S(1)} %maximum_maximum_fusion.refs_0_) | copy-start | bytes 2211844
  23.6 15.2 %collective-permute-start.5 = (bf16[480,768]{1,0:T(8,128)(2,1)S(1)}, bf16[480,768]{1,0:T(8,128)(2,1)}, u32[]{:S(2)}, u32[]{:S(2)}) collective-permute-start(bf16[480,768]{1,0:T(8,128)(2,1)S(1)} %maximum_maximum_fusion.refs_0_), channel_id=1, source_target_pairs={{0,2},{2,4},{4,6},{6,0},{16,22},{18,16},{20,18},{22,20},{1,3},{3,5... | collective-permute-start | bytes 2211848 | tf_op jit(solution)/shard_map/ppermute | solution.py:434
  24.5 14.3 %collective-permute-start.4 = (bf16[240,768]{1,0:T(8,128)(2,1)S(1)}, bf16[240,768]{1,0:T(8,128)(2,1)}, u32[]{:S(2)}, u32[]{:S(2)}) collective-permute-start(bf16[240,768]{1,0:T(8,128)(2,1)S(1)} %constant_dynamic-slice_fusion.2), channel_id=1, source_target_pairs={{0,9},{9,0},{1,8},{8,1},{2,11},{11,2},{3,10},{10,3},{4,13},{13,4},... | collective-permute-start | bytes 1105928 | tf_op jit(solution)/shard_map/ppermute | solution.py:437
  26.8 10.5 %collective-permute-start.6 = (bf16[192,768]{1,0:T(8,128)(2,1)S(1)}, bf16[192,768]{1,0:T(8,128)(2,1)}, u32[]{:S(2)}, u32[]{:S(2)}) collective-permute-start(bf16[192,768]{1,0:T(8,128)(2,1)S(1)} %collective-permute-done.1.refs_9_), channel_id=1, source_target_pairs={{0,2},{2,4},{4,6},{6,0},{16,22},{18,16},{20,18},{22,20},{1,3},{3,5... | collective-permute-start | bytes 884744 | tf_op jit(solution)/shard_map/ppermute | solution.py:434
  27.0 1.7 %copy-start = (bf16[48,192,128]{2,1,0:T(8,128)(2,1)S(1)}, bf16[48,192,128]{2,1,0:T(8,128)(2,1)}, u32[]{:S(2)}) copy-start(bf16[48,192,128]{2,1,0:T(8,128)(2,1)} %pair.1) | copy-start | bytes 7077892
  32.6 6.2 %collective-permute-start.7 = (bf16[16,72,128]{2,1,0:T(8,128)(2,1)S(1)}, bf16[16,72,128]{2,1,0:T(8,128)(2,1)S(1)}, u32[]{:S(2)}, u32[]{:S(2)}) collective-permute-start(bf16[16,72,128]{2,1,0:T(8,128)(2,1)S(1)} %tile_bias.1), channel_id=1, source_target_pairs={{0,1},{1,0},{2,3},{3,2},{4,5},{5,4},{6,7},{7,6},{8,9},{9,8},{10,11... | collective-permute-start | bytes 884744 | tf_op jit(solution)/shard_map/ppermute | solution.py:476
  38.8 12.6 %collective-permute-start.8 = (bf16[2,192,1152]{2,1,0:T(8,128)(2,1)S(1)}, bf16[2,192,1152]{2,1,0:T(8,128)(2,1)S(1)}, u32[]{:S(2)}, u32[]{:S(2)}) collective-permute-start(bf16[2,192,1152]{2,1,0:T(8,128)(2,1)S(1)} %collective-permute-done.3.refs_2_), channel_id=1, source_target_pairs={{0,32},{32,64},{64,96},{96,128},{128,160},{160,192},{192,224},{224... | collective-permute-start | bytes 2654216 | tf_op jit(solution)/shard_map/ppermute | solution.py:429
  41.5 5.5 %collective-permute-start.9 = (bf16[240,768]{1,0:T(8,128)(2,1)}, bf16[240,768]{1,0:T(8,128)(2,1)}, u32[]{:S(2)}, u32[]{:S(2)}) collective-permute-start(bf16[240,768]{1,0:T(8,128)(2,1)} %collective-permute-done.4), channel_id=1, source_target_pairs={{0,16},{16,0},{1,17},{17,1},{2,18},{18,2},{3,19},{19,3},{4,20},{20... | collective-permute-start | bytes 1105928 | tf_op jit(solution)/shard_map/ppermute | solution.py:440
  41.5 4.8 %copy-start.15 = (s32[1536]{0:T(1024)S(1)}, s32[1536]{0:T(1024)}, u32[]{:S(2)}) copy-start(s32[1536]{0:T(1024)} %param.20) | copy-start | bytes 18436
  41.5 4.9 %copy-start.16 = (s32[1536]{0:T(1024)S(1)}, s32[1536]{0:T(1024)}, u32[]{:S(2)}) copy-start(s32[1536]{0:T(1024)} %param.21) | copy-start | bytes 18436
  42.4 16.0 %all-to-all-start = ((bf16[16,2,72,128]{3,2,1,0:T(8,128)(2,1)}), bf16[16,2,72,128]{3,2,1,0:T(8,128)(2,1)S(1)}, u32[]{:S(2)}, u32[]{:S(2)}) async-start(bf16[16,2,72,128]{3,2,1,0:T(8,128)(2,1)} %copy.20), calls=%async_computation | async-start | bytes 1179648 | tf_op jit(solution)/shard_map/all_to_all | solution.py:482
  46.6 22.4 %collective-permute-start.13 = (bf16[2,192,1152]{2,1,0:T(8,128)(2,1)S(1)}, bf16[2,192,1152]{2,1,0:T(8,128)(2,1)}, u32[]{:S(2)}, u32[]{:S(2)}) collective-permute-start(bf16[2,192,1152]{2,1,0:T(8,128)(2,1)S(1)} %collective-permute-done.3.refs_2_), channel_id=1, source_target_pairs={{0,16},{16,0},{1,17},{17,1},{2,18},{18,2},{3,19},{19,3},{4,20},{20... | collective-permute-start | bytes 2654216 | tf_op jit(solution)/shard_map/ppermute | solution.py:440
  48.1 15.4 %copy-start.12 = (bf16[96,1152]{1,0:T(8,128)(2,1)S(1)}, bf16[96,1152]{1,0:T(8,128)(2,1)}, u32[]{:S(2)}) copy-start(bf16[96,1152]{1,0:T(8,128)(2,1)} %get-tuple-element.27) | copy-start | bytes 663556
  49.0 15.5 %copy-start.2 = (f32[2]{0:T(128)S(1)}, f32[2]{0:T(128)}, u32[]{:S(2)}) copy-start(f32[2]{0:T(128)} %refs_7_.1) | copy-start | bytes 28
  58.4 10.6 %collective-permute-start.14 = (bf16[2,192,1152]{2,1,0:T(8,128)(2,1)S(1)}, bf16[2,192,1152]{2,1,0:T(8,128)(2,1)S(1)}, u32[]{:S(2)}, u32[]{:S(2)}) collective-permute-start(bf16[2,192,1152]{2,1,0:T(8,128)(2,1)S(1)} %collective-permute-done.8.refs_4_), channel_id=1, source_target_pairs={{0,16},{16,0},{1,17},{17,1},{2,18},{18,2},{3,19},{19,3},{4,20},{20... | collective-permute-start | bytes 2654216 | tf_op jit(solution)/shard_map/ppermute | solution.py:440
  59.5 15.0 %collective-permute-start.15 = (bf16[480,768]{1,0:T(8,128)(2,1)}, bf16[480,768]{1,0:T(8,128)(2,1)}, u32[]{:S(2)}, u32[]{:S(2)}) collective-permute-start(bf16[480,768]{1,0:T(8,128)(2,1)} %pad_maximum_fusion.1.refs_1_), channel_id=1, source_target_pairs={{0,2},{2,4},{4,6},{6,0},{16,22},{18,16},{20,18},{22,20},{1,3},{3,5... | collective-permute-start | bytes 2211848 | tf_op jit(solution)/shard_map/ppermute | solution.py:434
  61.2 13.3 %collective-permute-start.16 = (bf16[192,768]{1,0:T(8,128)(2,1)S(1)}, bf16[192,768]{1,0:T(8,128)(2,1)}, u32[]{:S(2)}, u32[]{:S(2)}) collective-permute-start(bf16[192,768]{1,0:T(8,128)(2,1)S(1)} %broadcast_select_fusion.3), channel_id=1, source_target_pairs={{0,2},{2,4},{4,6},{6,0},{16,22},{18,16},{20,18},{22,20},{1,3},{3,5... | collective-permute-start | bytes 884744 | tf_op jit(solution)/shard_map/ppermute | solution.py:434
  61.5 15.2 %collective-permute-start.10 = (bf16[2,192,1152]{2,1,0:T(8,128)(2,1)S(1)}, bf16[2,192,1152]{2,1,0:T(8,128)(2,1)S(1)}, u32[]{:S(2)}, u32[]{:S(2)}) collective-permute-start(bf16[2,192,1152]{2,1,0:T(8,128)(2,1)S(1)} %collective-permute-done.8.refs_4_), channel_id=1, source_target_pairs={{0,32},{32,64},{64,96},{96,128},{128,160},{160,192},{192,224},{224... | collective-permute-start | bytes 2654216 | tf_op jit(solution)/shard_map/ppermute | solution.py:429
  75.7 12.4 %collective-permute-start.17 = (bf16[480,768]{1,0:T(8,128)(2,1)S(1)}, bf16[480,768]{1,0:T(8,128)(2,1)S(1)}, u32[]{:S(2)}, u32[]{:S(2)}) collective-permute-start(bf16[480,768]{1,0:T(8,128)(2,1)S(1)} %broadcast_select_fusion), channel_id=1, source_target_pairs={{0,2},{2,4},{4,6},{6,0},{16,22},{18,16},{20,18},{22,20},{1,3},{3,5... | collective-permute-start | bytes 2211848 | tf_op jit(solution)/shard_map/ppermute | solution.py:434
  76.7 2.9 %collective-permute-start.12 = (bf16[2,192,1152]{2,1,0:T(8,128)(2,1)S(1)}, bf16[2,192,1152]{2,1,0:T(8,128)(2,1)S(1)}, u32[]{:S(2)}, u32[]{:S(2)}) collective-permute-start(bf16[2,192,1152]{2,1,0:T(8,128)(2,1)S(1)} %collective-permute-done.10.refs_1_), channel_id=1, source_target_pairs={{0,16},{16,0},{1,17},{17,1},{2,18},{18,2},{3,19},{19,3},{4,20},{20... | collective-permute-start | bytes 2654216 | tf_op jit(solution)/shard_map/ppermute | solution.py:440
  77.1 8.0 %collective-permute-start.11 = (bf16[192,1152]{1,0:T(8,128)(2,1)S(1)}, bf16[192,1152]{1,0:T(8,128)(2,1)S(1)}, u32[]{:S(2)}, u32[]{:S(2)}) collective-permute-start(bf16[192,1152]{1,0:T(8,128)(2,1)S(1)} %slice_bitcast_fusion), channel_id=1, source_target_pairs={{0,32},{32,64},{64,96},{96,128},{128,160},{160,192},{192,224},{224... | collective-permute-start | bytes 1327112 | tf_op jit(solution)/shard_map/ppermute | solution.py:429
  79.1 11.3 %collective-permute-start.18 = (bf16[480,768]{1,0:T(8,128)(2,1)}, bf16[480,768]{1,0:T(8,128)(2,1)S(1)}, u32[]{:S(2)}, u32[]{:S(2)}) collective-permute-start(bf16[480,768]{1,0:T(8,128)(2,1)} %collective-permute-done.5.refs_2_), channel_id=1, source_target_pairs={{0,16},{16,0},{1,17},{17,1},{2,18},{18,2},{3,19},{19,3},{4,20},{20... | collective-permute-start | bytes 2211848 | tf_op jit(solution)/shard_map/ppermute | solution.py:440
  79.4 19.1 %collective-permute-start.19 = (bf16[480,768]{1,0:T(8,128)(2,1)}, bf16[480,768]{1,0:T(8,128)(2,1)S(1)}, u32[]{:S(2)}, u32[]{:S(2)}) collective-permute-start(bf16[480,768]{1,0:T(8,128)(2,1)} %collective-permute-done.15.refs_3_), channel_id=1, source_target_pairs={{0,16},{16,0},{1,17},{17,1},{2,18},{18,2},{3,19},{19,3},{4,20},{20... | collective-permute-start | bytes 2211848 | tf_op jit(solution)/shard_map/ppermute | solution.py:440
  88.2 10.3 %copy-start.4 = (bf16[480,768]{1,0:T(8,128)(2,1)}, bf16[480,768]{1,0:T(8,128)(2,1)S(1)}, u32[]{:S(2)}) copy-start(bf16[480,768]{1,0:T(8,128)(2,1)S(1)} %collective-permute-done.17.refs_6_) | copy-start | bytes 2211844
  88.2 10.3 %collective-permute-start.20 = (bf16[480,768]{1,0:T(8,128)(2,1)S(1)}, bf16[480,768]{1,0:T(8,128)(2,1)S(1)}, u32[]{:S(2)}, u32[]{:S(2)}) collective-permute-start(bf16[480,768]{1,0:T(8,128)(2,1)S(1)} %collective-permute-done.17.refs_6_), channel_id=1, source_target_pairs={{0,16},{16,0},{1,17},{17,1},{2,18},{18,2},{3,19},{19,3},{4,20},{20... | collective-permute-start | bytes 2211848 | tf_op jit(solution)/shard_map/ppermute | solution.py:440
  89.9 14.2 %collective-permute-start.21 = (bf16[192,768]{1,0:T(8,128)(2,1)}, bf16[192,768]{1,0:T(8,128)(2,1)}, u32[]{:S(2)}, u32[]{:S(2)}) collective-permute-start(bf16[192,768]{1,0:T(8,128)(2,1)} %collective-permute-done.refs_10_), channel_id=1, source_target_pairs={{0,16},{16,0},{1,17},{17,1},{2,18},{18,2},{3,19},{19,3},{4,20},{20... | collective-permute-start | bytes 884744 | tf_op jit(solution)/shard_map/ppermute | solution.py:440
  90.0 14.1 %collective-permute-start.22 = (bf16[192,768]{1,0:T(8,128)(2,1)}, bf16[192,768]{1,0:T(8,128)(2,1)}, u32[]{:S(2)}, u32[]{:S(2)}) collective-permute-start(bf16[192,768]{1,0:T(8,128)(2,1)} %collective-permute-done.6.refs_11_), channel_id=1, source_target_pairs={{0,16},{16,0},{1,17},{17,1},{2,18},{18,2},{3,19},{19,3},{4,20},{20... | collective-permute-start | bytes 884744 | tf_op jit(solution)/shard_map/ppermute | solution.py:440
  90.4 8.1 %copy-start.5 = (bf16[480,768]{1,0:T(8,128)(2,1)}, bf16[480,768]{1,0:T(8,128)(2,1)S(1)}, u32[]{:S(2)}) copy-start(bf16[480,768]{1,0:T(8,128)(2,1)S(1)} %collective-permute-done.18.refs_4_) | copy-start | bytes 2211844
  90.4 13.7 %collective-permute-start.23 = (bf16[192,768]{1,0:T(8,128)(2,1)}, bf16[192,768]{1,0:T(8,128)(2,1)}, u32[]{:S(2)}, u32[]{:S(2)}) collective-permute-start(bf16[192,768]{1,0:T(8,128)(2,1)} %collective-permute-done.16.refs_14_), channel_id=1, source_target_pairs={{0,16},{16,0},{1,17},{17,1},{2,18},{18,2},{3,19},{19,3},{4,20},{20... | collective-permute-start | bytes 884744 | tf_op jit(solution)/shard_map/ppermute | solution.py:440
  90.5 14.7 %all-to-all-start.1 = ((bf16[16,48,144]{2,1,0:T(8,128)(2,1)}), bf16[16,48,144]{2,1,0:T(8,128)(2,1)S(1)}, u32[]{:S(2)}, u32[]{:S(2)}) async-start(bf16[16,48,144]{2,1,0:T(8,128)(2,1)} %attend_last.1), calls=%async_computation.1 | async-start | bytes 786432 | tf_op jit(solution)/shard_map/all_to_all | solution.py:511
  98.5 0.9 copy-start.6
  98.5 1.1 copy-start.7
  105.2 0.8 copy-start.8

commit v5 on v4

--- a/solution.py
+++ b/solution.py
@@ -496,7 +496,7 @@
     down_last = around_y(jnp.where(lower, w_down_y, down_far_y))
     parts = [(chunk, 0), (one, 0), (one_x, 1), (two, 0), (two_x, 1)]
     state = attend(qg, parts, bias, 0, None, False)
-    state, up_far_y, down_last = lax.optimization_barrier((state, up_far_y, down_last))
+    state, three = lax.optimization_barrier((state, three))
     four = around(three[0])
     up_last = around_y(jnp.where(lower, up_y, up_far_y))
     three_x = cross(three)

time: 131 us -> 139 us (1.061)
  starting transfers between devices: 37.5 us -> 42.6 us
  waiting for transfers between devices: 21.5 us -> 26.3 us
    ppermute x6, starting transfers between devices: 6.44 us -> 12 us  [around_y(): return lax.ppermute(array, ('core', 'y'), up + down)]
    ppermute x6, waiting for transfers between devices: 4.65 us -> 9.33 us  [around_y(): return lax.ppermute(array, ('core', 'y'), up + down)]
    unnamed x34 -> x36, local copies, waits for them, and re-layouts: 3.63 us -> 2.85 us
  transfers between devices with their start and end apart: 26 -> 26, of which waited for: 7 -> 9; matrix products, arithmetic and copies ran while one was open for 8% -> 8% of each run, Pallas kernels for 24% -> 22%
where the time goes in v5:
time: 139 us; the launch traced here: 138 us
  starting transfers between devices  42.6 us (31%)
  Pallas kernels  39 us (28%)
  waiting for transfers between devices  26.3 us (19%)
  blocking collectives  14.2 us (10%)
  local copies, waits for them, and re-layouts  8.65 us (6%)
  other arithmetic  6.98 us (5%)
    all_to_all x1, blocking collectives, per_device(): out = lax.all_to_all(out, COL, split_axis=0, concat_axis=0, tiled=True)  14.2 us
    ppermute x4, starting transfers between devices, around(): return lax.ppermute(array, ('z', 'core'), up + down)  12.1 us
    ppermute x6, starting transfers between devices, around_y(): return lax.ppermute(array, ('core', 'y'), up + down)  12 us
    pallas_call x3, Pallas kernels, attend(): pl.pallas_call(functools.partial(attend_kernel, state is None, last, pick...  9.95 us
    ppermute x6, waiting for transfers between devices, around_y(): return lax.ppermute(array, ('core', 'y'), up + down)  9.33 us
    pallas_call x1, Pallas kernels, transition(): pl.pallas_call(transition_kernel, in_specs=in_vmem(4) + [pl.BlockSpec(mem...  9.07 us
    pallas_call x1, Pallas kernels, project(): pl.pallas_call(project_kernel, grid_spec=pltpu.PrefetchScalarGridSpec(num...  7.1 us
    all_to_all x1, waiting for transfers between devices, per_device(): lax.all_to_all(tiles, PLANE, split_axis=0, concat_axis=0, tiled=True)  6.92 us
  transfers between devices with their start and end apart: 26, of which 9 were waited for; matrix products, arithmetic and copies ran while one was open for 8% of the time, Pallas kernels for 22%

profile of v5, /device:TPU:1, one launch (start us, length us, event | category | flops | bytes accessed | tf_op | source)
XLA Modules:
  0.0 138.1 jit_solution(12689252834136405244)
XLA Ops:
  0.0 3.6 %collective-permute-start = (bf16[192,768]{1,0:T(8,128)(2,1)}, bf16[192,768]{1,0:T(8,128)(2,1)S(1)}, u32[]{:S(2)}, u32[]{:S(2)}) collective-permute-start(bf16[192,768]{1,0:T(8,128)(2,1)} %refs_8_.3), channel_id=1, source_target_pairs={{0,2},{2,4},{4,6},{6,0},{16,22},{18,16},{20,18},{22,20},{1,3},{3,5... | collective-permute-start | bytes 884744 | tf_op jit(solution)/shard_map/ppermute | solution.py:434
  3.6 2.5 %collective-permute-start.1 = (bf16[192,768]{1,0:T(8,128)(2,1)}, bf16[192,768]{1,0:T(8,128)(2,1)S(1)}, u32[]{:S(2)}, u32[]{:S(2)}) collective-permute-start(bf16[192,768]{1,0:T(8,128)(2,1)} %refs_8_.3), channel_id=1, source_target_pairs={{0,9},{9,0},{1,8},{8,1},{2,11},{11,2},{3,10},{10,3},{4,13},{13,4},... | collective-permute-start | bytes 884744 | tf_op jit(solution)/shard_map/ppermute | solution.py:437
  6.0 0.7 stack.91.place
  6.7 7.1 %project.1 = (bf16[96,1152]{1,0:T(8,128)(2,1)}, bf16[3,96,1152]{2,1,0:T(8,128)(2,1)}) custom-call(s32[9]{0:T(128)} %stack.91.place, bf16[12,96,768]{2,1,0:T(8,128)(2,1)} %acts.1, bf16[12,96,384]{2,1,0:T(8,128)(2,1)} %cond.1, bf16[384,768]{1,0:T(8,128)(2,1)} %scale.1, bf16[384,768]{1,0:T(8,128)(2,1)} %shift.1, bf16[4,96,768]{2,1,0:T(8,128)(2,1)} %bitcast.61), custom_call_target="tpu_custom_call" | custom-call | bytes 27200000 | tf_op jit(solution)/shard_map/project/pallas_call | solution.py:87
  13.9 0.5 collective-permute-start.2
  14.4 1.9 %collective-permute-done.2 = bf16[3,96,1152]{2,1,0:T(8,128)(2,1)S(1)} collective-permute-done((bf16[3,96,1152]{2,1,0:T(8,128)(2,1)}, bf16[3,96,1152]{2,1,0:T(8,128)(2,1)S(1)}, u32[]{:S(2)}, u32[]{:S(2)}) %collective-permute-start.2) | collective-permute-done | bytes 663584 | tf_op jit(solution)/shard_map/ppermute | solution.py:440
  16.4 1.4 select_bitcast_fusion.3
  18.0 5.6 %collective-permute-start.3 = (bf16[2,192,1152]{2,1,0:T(8,128)(2,1)S(1)}, bf16[2,192,1152]{2,1,0:T(8,128)(2,1)S(1)}, u32[]{:S(2)}, u32[]{:S(2)}) collective-permute-start(bf16[2,192,1152]{2,1,0:T(8,128)(2,1)S(1)} %pad_maximum_fusion.refs_1_), channel_id=1, source_target_pairs={{0,32},{32,64},{64,96},{96,128},{128,160},{160,192},{192,224},{224... | collective-permute-start | bytes 2654216 | tf_op jit(solution)/shard_map/ppermute | solution.py:429
  23.7 0.8 collective-permute-start.5
  24.5 2.3 %collective-permute-start.4 = (bf16[240,768]{1,0:T(8,128)(2,1)S(1)}, bf16[240,768]{1,0:T(8,128)(2,1)}, u32[]{:S(2)}, u32[]{:S(2)}) collective-permute-start(bf16[240,768]{1,0:T(8,128)(2,1)S(1)} %constant_dynamic-slice_fusion.2), channel_id=1, source_target_pairs={{0,9},{9,0},{1,8},{8,1},{2,11},{11,2},{3,10},{10,3},{4,13},{13,4},... | collective-permute-start | bytes 1105928 | tf_op jit(solution)/shard_map/ppermute | solution.py:437
  27.0 1.7 %copy-done = bf16[48,192,128]{2,1,0:T(8,128)(2,1)S(1)} copy-done((bf16[48,192,128]{2,1,0:T(8,128)(2,1)S(1)}, bf16[48,192,128]{2,1,0:T(8,128)(2,1)}, u32[]{:S(2)}) %copy-start) | copy-done | bytes 2359320
  28.7 3.9 %tile_bias.1 = bf16[16,72,128]{2,1,0:T(8,128)(2,1)S(1)} custom-call(bf16[48,192,128]{2,1,0:T(8,128)(2,1)S(1)} %copy-done, bf16[16,128]{1,0:T(8,128)(2,1)S(1)} %bitcast.58), custom_call_target="tpu_custom_call" | custom-call | bytes 20400000 | tf_op jit(solution)/shard_map/tile_bias/pallas_call | solution.py:138
  32.7 4.6 %collective-permute-done.6.refs_11_ = bf16[192,768]{1,0:T(8,128)(2,1)} collective-permute-done((bf16[192,768]{1,0:T(8,128)(2,1)S(1)}, bf16[192,768]{1,0:T(8,128)(2,1)}, u32[]{:S(2)}, u32[]{:S(2)}) %collective-permute-start.6) | collective-permute-done | bytes 294944 | tf_op jit(solution)/shard_map/ppermute | solution.py:434
  37.3 1.5 %collective-permute-done.7 = bf16[16,72,128]{2,1,0:T(8,128)(2,1)S(1)} collective-permute-done((bf16[16,72,128]{2,1,0:T(8,128)(2,1)S(1)}, bf16[16,72,128]{2,1,0:T(8,128)(2,1)S(1)}, u32[]{:S(2)}, u32[]{:S(2)}) %collective-permute-start.7) | collective-permute-done | bytes 294944 | tf_op jit(solution)/shard_map/ppermute | solution.py:476
  38.8 2.6 %collective-permute-start.9 = (bf16[2,192,1152]{2,1,0:T(8,128)(2,1)S(1)}, bf16[2,192,1152]{2,1,0:T(8,128)(2,1)S(1)}, u32[]{:S(2)}, u32[]{:S(2)}) collective-permute-start(bf16[2,192,1152]{2,1,0:T(8,128)(2,1)S(1)} %collective-permute-done.3.refs_2_), channel_id=1, source_target_pairs={{0,32},{32,64},{64,96},{96,128},{128,160},{160,192},{192,224},{224... | collective-permute-start | bytes 2654216 | tf_op jit(solution)/shard_map/ppermute | solution.py:429
  41.5 0.9 copy.20
  42.4 3.9 %all-to-all-start = ((bf16[16,2,72,128]{3,2,1,0:T(8,128)(2,1)}), bf16[16,2,72,128]{3,2,1,0:T(8,128)(2,1)S(1)}, u32[]{:S(2)}, u32[]{:S(2)}) async-start(bf16[16,2,72,128]{3,2,1,0:T(8,128)(2,1)} %copy.20), calls=%async_computation | async-start | bytes 1179648 | tf_op jit(solution)/shard_map/all_to_all | solution.py:482
  46.4 1.2 broadcast_select_fusion.2
  47.6 0.9 pad_maximum_fusion.1.refs_1_
  48.5 2.9 %collective-permute-done.9.refs_4_ = bf16[2,192,1152]{2,1,0:T(8,128)(2,1)S(1)} collective-permute-done((bf16[2,192,1152]{2,1,0:T(8,128)(2,1)S(1)}, bf16[2,192,1152]{2,1,0:T(8,128)(2,1)S(1)}, u32[]{:S(2)}, u32[]{:S(2)}) %collective-permute-start.9) | collective-permute-done | bytes 884768 | tf_op jit(solution)/shard_map/ppermute | solution.py:429
  51.5 6.9 %all-to-all-done = bf16[16,2,72,128]{3,2,1,0:T(8,128)(2,1)S(1)} async-done(((bf16[16,2,72,128]{3,2,1,0:T(8,128)(2,1)}), bf16[16,2,72,128]{3,2,1,0:T(8,128)(2,1)S(1)}, u32[]{:S(2)}, u32[]{:S(2)}) %all-to-all-start) | async-done | bytes 589856 | tf_op jit(solution)/shard_map/all_to_all | solution.py:482
  58.4 1.6 %collective-permute-start.15 = (bf16[480,768]{1,0:T(8,128)(2,1)}, bf16[480,768]{1,0:T(8,128)(2,1)}, u32[]{:S(2)}, u32[]{:S(2)}) collective-permute-start(bf16[480,768]{1,0:T(8,128)(2,1)} %pad_maximum_fusion.1.refs_1_), channel_id=1, source_target_pairs={{0,2},{2,4},{4,6},{6,0},{16,22},{18,16},{20,18},{22,20},{1,3},{3,5... | collective-permute-start | bytes 2211848 | tf_op jit(solution)/shard_map/ppermute | solution.py:434
  60.9 1.9 %collective-permute-start.12 = (bf16[2,192,1152]{2,1,0:T(8,128)(2,1)S(1)}, bf16[2,192,1152]{2,1,0:T(8,128)(2,1)S(1)}, u32[]{:S(2)}, u32[]{:S(2)}) collective-permute-start(bf16[2,192,1152]{2,1,0:T(8,128)(2,1)S(1)} %collective-permute-done.9.refs_4_), channel_id=1, source_target_pairs={{0,32},{32,64},{64,96},{96,128},{128,160},{160,192},{192,224},{224... | collective-permute-start | bytes 2654216 | tf_op jit(solution)/shard_map/ppermute | solution.py:429
  62.7 1.0 broadcast_select_fusion.5
  63.8 4.5 %assemble.1.refs_6_.refs_3_.refs_2_ = f32[8,192,384]{2,1,0:T(8,128)S(1)} custom-call(s32[11]{0:T(128)S(1)} %stack.105.place, bf16[8,2,2,72,128]{4,3,2,1,0:T(8,128)(2,1)S(1)} %bitcast.55, bf16[8,2,2,72,128]{4,3,2,1,0:T(8,128)(2,1)S(1)} %bitcast.56, s32[8,1,192]{2,1,0:T(1,128)S(1)} %reshape.34.refs_2_.refs_3_.refs_6_, ...), custom_call_target="tpu_custom_call" | custom-call | bytes 17000000 | tf_op jit(solution)/shard_map/assemble/pallas_call | solution.py:197
  68.3 1.0 collective-permute-done.15.refs_3_
  69.3 1.2 broadcast_select_fusion
  70.5 2.8 %collective-permute-start.16 = (bf16[480,768]{1,0:T(8,128)(2,1)S(1)}, bf16[480,768]{1,0:T(8,128)(2,1)S(1)}, u32[]{:S(2)}, u32[]{:S(2)}) collective-permute-start(bf16[480,768]{1,0:T(8,128)(2,1)S(1)} %broadcast_select_fusion), channel_id=1, source_target_pairs={{0,2},{2,4},{4,6},{6,0},{16,22},{18,16},{20,18},{22,20},{1,3},{3,5... | collective-permute-start | bytes 2211848 | tf_op jit(solution)/shard_map/ppermute | solution.py:434
  73.3 4.3 %attend.2.refs_4_ = f32[3,2,56,384]{3,2,1,0:T(8,128)S(1)} custom-call(bf16[192,1152]{1,0:T(8,128)(2,1)S(1)} %pad_maximum_fusion.3.refs_0_, bf16[2,192,1152]{2,1,0:T(8,128)(2,1)S(1)} %pad_maximum_fusion.refs_1_, bf16[2,192,1152]{2,1,0:T(8,128)(2,1)S(1)} %collective-permute-done.3.refs_2_, bf16[2,192,1152]{2,1,0:T(8,128)(2,1)S(1)} %collective-permute-done.8.refs_3_, ...), custom_call_target="tpu_custom_call" | custom-call | bytes 23800000 | tf_op jit(solution)/shard_map/attend/pallas_call | solution.py:288
  77.7 0.6 collective-permute-start.14
  78.3 1.9 %collective-permute-start.13 = (bf16[192,1152]{1,0:T(8,128)(2,1)S(1)}, bf16[192,1152]{1,0:T(8,128)(2,1)S(1)}, u32[]{:S(2)}, u32[]{:S(2)}) collective-permute-start(bf16[192,1152]{1,0:T(8,128)(2,1)S(1)} %slice_bitcast_fusion), channel_id=1, source_target_pairs={{0,32},{32,64},{64,96},{96,128},{128,160},{160,192},{192,224},{224... | collective-permute-start | bytes 1327112 | tf_op jit(solution)/shard_map/ppermute | solution.py:429
  80.8 2.6 %attend.3.refs_3_ = f32[3,2,56,384]{3,2,1,0:T(8,128)S(1)} custom-call(bf16[192,1152]{1,0:T(8,128)(2,1)S(1)} %pad_maximum_fusion.3.refs_0_, bf16[2,192,1152]{2,1,0:T(8,128)(2,1)S(1)} %collective-permute-done.12.refs_1_, bf16[2,192,1152]{2,1,0:T(8,128)(2,1)S(1)} %collective-permute-done.14.refs_2_, f32[8,192,384]{2,1,0:T(8,128)S(1)} %assemble.1.refs_6_.refs_3_.refs_2_, ...), custom_call_target="tpu_custom_call" | custom-call | bytes 13600000 | tf_op jit(solution)/shard_map/attend/pallas_call | solution.py:288
  83.3 2.5 %collective-permute-done.13.refs_1_ = bf16[192,1152]{1,0:T(8,128)(2,1)S(1)} collective-permute-done((bf16[192,1152]{1,0:T(8,128)(2,1)S(1)}, bf16[192,1152]{1,0:T(8,128)(2,1)S(1)}, u32[]{:S(2)}, u32[]{:S(2)}) %collective-permute-start.13) | collective-permute-done | bytes 442400 | tf_op jit(solution)/shard_map/ppermute | solution.py:429
  85.8 3.1 %attend_last.1 = bf16[16,48,144]{2,1,0:T(8,128)(2,1)} custom-call(bf16[192,1152]{1,0:T(8,128)(2,1)S(1)} %pad_maximum_fusion.3.refs_0_, bf16[192,1152]{1,0:T(8,128)(2,1)S(1)} %collective-permute-done.13.refs_1_, f32[8,192,384]{2,1,0:T(8,128)S(1)} %assemble.1.refs_6_.refs_3_.refs_2_, f32[3,2,56,384]{3,2,1,0:T(8,128)S(1)} %attend.3.refs_3_), custom_call_target="tpu_custom_call" | custom-call | bytes 10200000 | tf_op jit(solution)/shard_map/attend_last/pallas_call | solution.py:288
  88.9 2.1 %collective-permute-start.19 = (bf16[480,768]{1,0:T(8,128)(2,1)S(1)}, bf16[480,768]{1,0:T(8,128)(2,1)S(1)}, u32[]{:S(2)}, u32[]{:S(2)}) collective-permute-start(bf16[480,768]{1,0:T(8,128)(2,1)S(1)} %collective-permute-done.16.refs_6_), channel_id=1, source_target_pairs={{0,16},{16,0},{1,17},{17,1},{2,18},{18,2},{3,19},{19,3},{4,20},{20... | collective-permute-start | bytes 2211848 | tf_op jit(solution)/shard_map/ppermute | solution.py:440
  91.0 1.0 broadcast_select_fusion.3
  92.0 3.0 %collective-permute-start.22 = (bf16[192,768]{1,0:T(8,128)(2,1)S(1)}, bf16[192,768]{1,0:T(8,128)(2,1)}, u32[]{:S(2)}, u32[]{:S(2)}) collective-permute-start(bf16[192,768]{1,0:T(8,128)(2,1)S(1)} %broadcast_select_fusion.3), channel_id=1, source_target_pairs={{0,2},{2,4},{4,6},{6,0},{16,22},{18,16},{20,18},{22,20},{1,3},{3,5... | collective-permute-start | bytes 884744 | tf_op jit(solution)/shard_map/ppermute | solution.py:434
  95.0 3.7 %collective-permute-done.22.refs_14_ = bf16[192,768]{1,0:T(8,128)(2,1)} collective-permute-done((bf16[192,768]{1,0:T(8,128)(2,1)S(1)}, bf16[192,768]{1,0:T(8,128)(2,1)}, u32[]{:S(2)}, u32[]{:S(2)}) %collective-permute-start.22) | collective-permute-done | bytes 294944 | tf_op jit(solution)/shard_map/ppermute | solution.py:434
  98.7 0.5 collective-permute-start.21
  99.3 4.8 %all-to-all-start.1 = ((bf16[16,48,144]{2,1,0:T(8,128)(2,1)}), bf16[16,48,144]{2,1,0:T(8,128)(2,1)}, u32[]{:S(2)}, u32[]{:S(2)}) async-start(bf16[16,48,144]{2,1,0:T(8,128)(2,1)} %attend_last.1), calls=%async_computation.1 | async-start | bytes 786432 | tf_op jit(solution)/shard_map/all_to_all | solution.py:511
  104.1 1.5 %constant_dynamic-slice_fusion = bf16[3,48,384]{2,1,0:T(8,128)(2,1)} fusion(bf16[12,96,384]{2,1,0:T(8,128)(2,1)} %cond.1, s32[]{:T(128)S(6)} %select_n.174, s32[]{:T(128)S(6)} %select_n.175), kind=kLoop, calls=%fused_computation.19 | loop fusion | bytes 221192 | tf_op jit(solution)/shard_map/dynamic_slice | solution.py:516
  105.6 1.7 %constant_dynamic-slice_fusion.1 = bf16[3,48,768]{2,1,0:T(8,128)(2,1)} fusion(bf16[12,96,768]{2,1,0:T(8,128)(2,1)} %acts.1, s32[]{:T(128)S(6)} %select_n.174, s32[]{:T(128)S(6)} %select_n.175), kind=kLoop, calls=%fused_computation.20 | loop fusion | bytes 442376 | tf_op jit(solution)/shard_map/dynamic_slice | solution.py:516
  107.3 0.8 copy-done.6
  108.4 4.5 %condition.1.mix = f32[4,144,768]{2,1,0:T(8,128)} custom-call(s32[9]{0:T(128)} %stack.91.place, bf16[144,384]{1,0:T(8,128)(2,1)} %bitcast.63, bf16[480,768]{1,0:T(8,128)(2,1)} %copy-done.3, bf16[480,768]{1,0:T(8,128)(2,1)} %pad_maximum_fusion.1.refs_1_, bf16[480,768]{1,0:T(8,128)(2,1)} %collective-permute-done.5.refs_2_, ...), custom_call_target="tpu_custom_call" | custom-call | bytes 13600000 | tf_op jit(solution)/shard_map/condition/pallas_call | solution.py:327
  113.0 1.1 all-to-all-done.1.heads
  114.1 9.1 %transition.1 = bf16[8,144,96]{2,1,0:T(8,128)(2,1)} custom-call(bf16[16,48,144]{2,1,0:T(8,128)(2,1)} %all-to-all-done.1.heads, bf16[144,768]{1,0:T(8,128)(2,1)} %bitcast.60, f32[4,144,768]{2,1,0:T(8,128)} %condition.1.mix, bf16[768,768]{1,0:T(8,128)(2,1)} %w_out.1, bf16[480,768]{1,0:T(8,128)(2,1)} %copy-done.3, bf16[480,768]{1,0:T(8,128)(2,1)} %pad_maximum_fusion.1.refs_1_, ...), custom_call_target="tpu_custom_call" | custom-call | bytes 27200000 | tf_op jit(solution)/shard_map/transition/pallas_call | solution.py:385
  123.2 14.2 %all_to_all.15 = bf16[8,144,96]{2,1,0:T(8,128)(2,1)S(1)} all-to-all(bf16[8,144,96]{2,1,0:T(8,128)(2,1)} %transition.1), channel_id=1, replica_groups=mesh['z'=8,'core'=2,'xh'=2,'y'=4,'samp'=2] {'xh','y'}, dimensions={0} | all-to-all | bytes 442368 | tf_op jit(solution)/shard_map/all_to_all | solution.py:523
  137.3 0.7 copy.21
  (70 shorter events, 2.5 us)
Async XLA Ops:
  0.0 13.8 %collective-permute-start = (bf16[192,768]{1,0:T(8,128)(2,1)}, bf16[192,768]{1,0:T(8,128)(2,1)S(1)}, u32[]{:S(2)}, u32[]{:S(2)}) collective-permute-start(bf16[192,768]{1,0:T(8,128)(2,1)} %refs_8_.3), channel_id=1, source_target_pairs={{0,2},{2,4},{4,6},{6,0},{16,22},{18,16},{20,18},{22,20},{1,3},{3,5... | collective-permute-start | bytes 884744 | tf_op jit(solution)/shard_map/ppermute | solution.py:434
  3.6 10.3 %collective-permute-start.1 = (bf16[192,768]{1,0:T(8,128)(2,1)}, bf16[192,768]{1,0:T(8,128)(2,1)S(1)}, u32[]{:S(2)}, u32[]{:S(2)}) collective-permute-start(bf16[192,768]{1,0:T(8,128)(2,1)} %refs_8_.3), channel_id=1, source_target_pairs={{0,9},{9,0},{1,8},{8,1},{2,11},{11,2},{3,10},{10,3},{4,13},{13,4},... | collective-permute-start | bytes 884744 | tf_op jit(solution)/shard_map/ppermute | solution.py:437
  13.8 4.0 %copy-start.8 = (bf16[192,768]{1,0:T(8,128)(2,1)}, bf16[192,768]{1,0:T(8,128)(2,1)S(1)}, u32[]{:S(2)}) copy-start(bf16[192,768]{1,0:T(8,128)(2,1)S(1)} %collective-permute-done.refs_10_) | copy-start | bytes 884740
  13.9 13.0 %copy-start.12 = (bf16[192,768]{1,0:T(8,128)(2,1)}, bf16[192,768]{1,0:T(8,128)(2,1)S(1)}, u32[]{:S(2)}) copy-start(bf16[192,768]{1,0:T(8,128)(2,1)S(1)} %collective-permute-done.1.refs_9_) | copy-start | bytes 884740
  13.9 2.5 %collective-permute-start.2 = (bf16[3,96,1152]{2,1,0:T(8,128)(2,1)}, bf16[3,96,1152]{2,1,0:T(8,128)(2,1)S(1)}, u32[]{:S(2)}, u32[]{:S(2)}) collective-permute-start(bf16[3,96,1152]{2,1,0:T(8,128)(2,1)} %get-tuple-element.28), channel_id=1, source_target_pairs={{0,16},{16,0},{1,17},{17,1},{2,18},{18,2},{3,19},{19,3},{4,20},{20... | collective-permute-start | bytes 1990664 | tf_op jit(solution)/shard_map/ppermute | solution.py:440
  16.4 1.4 copy-start.10
  17.7 5.8 %copy-start.11 = (bf16[2,768,192]{1,2,0:T(8,128)(2,1)S(1)}, bf16[2,768,192]{1,2,0:T(8,128)(2,1)}, u32[]{:S(2)}) copy-start(bf16[2,768,192]{1,2,0:T(8,128)(2,1)} %param.31) | copy-start | bytes 1769476
  17.8 5.8 %copy-start.14 = (bf16[384,96]{0,1:T(8,128)(2,1)S(1)}, bf16[384,96]{0,1:T(8,128)(2,1)}, u32[]{:S(2)}) copy-start(bf16[384,96]{0,1:T(8,128)(2,1)} %param.33) | copy-start | bytes 221188
  17.8 5.8 %copy-start.15 = (bf16[384,96]{0,1:T(8,128)(2,1)S(1)}, bf16[384,96]{0,1:T(8,128)(2,1)}, u32[]{:S(2)}) copy-start(bf16[384,96]{0,1:T(8,128)(2,1)} %param.28) | copy-start | bytes 221188
  18.0 9.1 %copy-start.1 = (bf16[128,16]{0,1:T(8,128)(2,1)S(1)}, bf16[128,16]{0,1:T(8,128)(2,1)}, u32[]{:S(2)}) copy-start(bf16[128,16]{0,1:T(8,128)(2,1)} %param.22) | copy-start | bytes 12292
  18.0 20.8 %collective-permute-start.3 = (bf16[2,192,1152]{2,1,0:T(8,128)(2,1)S(1)}, bf16[2,192,1152]{2,1,0:T(8,128)(2,1)S(1)}, u32[]{:S(2)}, u32[]{:S(2)}) collective-permute-start(bf16[2,192,1152]{2,1,0:T(8,128)(2,1)S(1)} %pad_maximum_fusion.refs_1_), channel_id=1, source_target_pairs={{0,32},{32,64},{64,96},{96,128},{128,160},{160,192},{192,224},{224... | collective-permute-start | bytes 2654216 | tf_op jit(solution)/shard_map/ppermute | solution.py:429
  23.6 8.9 %copy-start.3 = (bf16[480,768]{1,0:T(8,128)(2,1)}, bf16[480,768]{1,0:T(8,128)(2,1)S(1)}, u32[]{:S(2)}) copy-start(bf16[480,768]{1,0:T(8,128)(2,1)S(1)} %maximum_maximum_fusion.refs_0_) | copy-start | bytes 2211844
  23.7 15.2 %collective-permute-start.5 = (bf16[480,768]{1,0:T(8,128)(2,1)S(1)}, bf16[480,768]{1,0:T(8,128)(2,1)}, u32[]{:S(2)}, u32[]{:S(2)}) collective-permute-start(bf16[480,768]{1,0:T(8,128)(2,1)S(1)} %maximum_maximum_fusion.refs_0_), channel_id=1, source_target_pairs={{0,2},{2,4},{4,6},{6,0},{16,22},{18,16},{20,18},{22,20},{1,3},{3,5... | collective-permute-start | bytes 2211848 | tf_op jit(solution)/shard_map/ppermute | solution.py:434
  24.5 14.3 %collective-permute-start.4 = (bf16[240,768]{1,0:T(8,128)(2,1)S(1)}, bf16[240,768]{1,0:T(8,128)(2,1)}, u32[]{:S(2)}, u32[]{:S(2)}) collective-permute-start(bf16[240,768]{1,0:T(8,128)(2,1)S(1)} %constant_dynamic-slice_fusion.2), channel_id=1, source_target_pairs={{0,9},{9,0},{1,8},{8,1},{2,11},{11,2},{3,10},{10,3},{4,13},{13,4},... | collective-permute-start | bytes 1105928 | tf_op jit(solution)/shard_map/ppermute | solution.py:437
  26.8 10.5 %collective-permute-start.6 = (bf16[192,768]{1,0:T(8,128)(2,1)S(1)}, bf16[192,768]{1,0:T(8,128)(2,1)}, u32[]{:S(2)}, u32[]{:S(2)}) collective-permute-start(bf16[192,768]{1,0:T(8,128)(2,1)S(1)} %collective-permute-done.1.refs_9_), channel_id=1, source_target_pairs={{0,2},{2,4},{4,6},{6,0},{16,22},{18,16},{20,18},{22,20},{1,3},{3,5... | collective-permute-start | bytes 884744 | tf_op jit(solution)/shard_map/ppermute | solution.py:434
  27.0 1.7 %copy-start = (bf16[48,192,128]{2,1,0:T(8,128)(2,1)S(1)}, bf16[48,192,128]{2,1,0:T(8,128)(2,1)}, u32[]{:S(2)}) copy-start(bf16[48,192,128]{2,1,0:T(8,128)(2,1)} %pair.1) | copy-start | bytes 7077892
  32.6 6.2 %collective-permute-start.7 = (bf16[16,72,128]{2,1,0:T(8,128)(2,1)S(1)}, bf16[16,72,128]{2,1,0:T(8,128)(2,1)S(1)}, u32[]{:S(2)}, u32[]{:S(2)}) collective-permute-start(bf16[16,72,128]{2,1,0:T(8,128)(2,1)S(1)} %tile_bias.1), channel_id=1, source_target_pairs={{0,1},{1,0},{2,3},{3,2},{4,5},{5,4},{6,7},{7,6},{8,9},{9,8},{10,11... | collective-permute-start | bytes 884744 | tf_op jit(solution)/shard_map/ppermute | solution.py:476
  38.8 12.6 %collective-permute-start.9 = (bf16[2,192,1152]{2,1,0:T(8,128)(2,1)S(1)}, bf16[2,192,1152]{2,1,0:T(8,128)(2,1)S(1)}, u32[]{:S(2)}, u32[]{:S(2)}) collective-permute-start(bf16[2,192,1152]{2,1,0:T(8,128)(2,1)S(1)} %collective-permute-done.3.refs_2_), channel_id=1, source_target_pairs={{0,32},{32,64},{64,96},{96,128},{128,160},{160,192},{192,224},{224... | collective-permute-start | bytes 2654216 | tf_op jit(solution)/shard_map/ppermute | solution.py:429
  41.5 4.9 %collective-permute-start.10 = (bf16[240,768]{1,0:T(8,128)(2,1)}, bf16[240,768]{1,0:T(8,128)(2,1)}, u32[]{:S(2)}, u32[]{:S(2)}) collective-permute-start(bf16[240,768]{1,0:T(8,128)(2,1)} %collective-permute-done.4), channel_id=1, source_target_pairs={{0,16},{16,0},{1,17},{17,1},{2,18},{18,2},{3,19},{19,3},{4,20},{20... | collective-permute-start | bytes 1105928 | tf_op jit(solution)/shard_map/ppermute | solution.py:440
  42.4 16.0 %all-to-all-start = ((bf16[16,2,72,128]{3,2,1,0:T(8,128)(2,1)}), bf16[16,2,72,128]{3,2,1,0:T(8,128)(2,1)S(1)}, u32[]{:S(2)}, u32[]{:S(2)}) async-start(bf16[16,2,72,128]{3,2,1,0:T(8,128)(2,1)} %copy.20), calls=%async_computation | async-start | bytes 1179648 | tf_op jit(solution)/shard_map/all_to_all | solution.py:482
  46.3 13.7 %copy-start.16 = (s32[1536]{0:T(1024)S(1)}, s32[1536]{0:T(1024)}, u32[]{:S(2)}) copy-start(s32[1536]{0:T(1024)} %param.20) | copy-start | bytes 18436
  46.3 13.8 %copy-start.17 = (s32[1536]{0:T(1024)S(1)}, s32[1536]{0:T(1024)}, u32[]{:S(2)}) copy-start(s32[1536]{0:T(1024)} %param.21) | copy-start | bytes 18436
  46.3 16.4 %copy-start.13 = (bf16[96,1152]{1,0:T(8,128)(2,1)S(1)}, bf16[96,1152]{1,0:T(8,128)(2,1)}, u32[]{:S(2)}) copy-start(bf16[96,1152]{1,0:T(8,128)(2,1)} %get-tuple-element.26) | copy-start | bytes 663556
  47.6 16.2 %copy-start.2 = (f32[2]{0:T(128)S(1)}, f32[2]{0:T(128)}, u32[]{:S(2)}) copy-start(f32[2]{0:T(128)} %refs_7_.1) | copy-start | bytes 28
  58.4 10.9 %collective-permute-start.15 = (bf16[480,768]{1,0:T(8,128)(2,1)}, bf16[480,768]{1,0:T(8,128)(2,1)}, u32[]{:S(2)}, u32[]{:S(2)}) collective-permute-start(bf16[480,768]{1,0:T(8,128)(2,1)} %pad_maximum_fusion.1.refs_1_), channel_id=1, source_target_pairs={{0,2},{2,4},{4,6},{6,0},{16,22},{18,16},{20,18},{22,20},{1,3},{3,5... | collective-permute-start | bytes 2211848 | tf_op jit(solution)/shard_map/ppermute | solution.py:434
  60.3 13.0 %collective-permute-start.8 = (bf16[2,192,1152]{2,1,0:T(8,128)(2,1)S(1)}, bf16[2,192,1152]{2,1,0:T(8,128)(2,1)S(1)}, u32[]{:S(2)}, u32[]{:S(2)}) collective-permute-start(bf16[2,192,1152]{2,1,0:T(8,128)(2,1)S(1)} %collective-permute-done.3.refs_2_), channel_id=1, source_target_pairs={{0,16},{16,0},{1,17},{17,1},{2,18},{18,2},{3,19},{19,3},{4,20},{20... | collective-permute-start | bytes 2654216 | tf_op jit(solution)/shard_map/ppermute | solution.py:440
  60.4 13.0 %collective-permute-start.11 = (bf16[2,192,1152]{2,1,0:T(8,128)(2,1)S(1)}, bf16[2,192,1152]{2,1,0:T(8,128)(2,1)S(1)}, u32[]{:S(2)}, u32[]{:S(2)}) collective-permute-start(bf16[2,192,1152]{2,1,0:T(8,128)(2,1)S(1)} %collective-permute-done.9.refs_4_), channel_id=1, source_target_pairs={{0,16},{16,0},{1,17},{17,1},{2,18},{18,2},{3,19},{19,3},{4,20},{20... | collective-permute-start | bytes 2654216 | tf_op jit(solution)/shard_map/ppermute | solution.py:440
  60.9 16.8 %collective-permute-start.12 = (bf16[2,192,1152]{2,1,0:T(8,128)(2,1)S(1)}, bf16[2,192,1152]{2,1,0:T(8,128)(2,1)S(1)}, u32[]{:S(2)}, u32[]{:S(2)}) collective-permute-start(bf16[2,192,1152]{2,1,0:T(8,128)(2,1)S(1)} %collective-permute-done.9.refs_4_), channel_id=1, source_target_pairs={{0,32},{32,64},{64,96},{96,128},{128,160},{160,192},{192,224},{224... | collective-permute-start | bytes 2654216 | tf_op jit(solution)/shard_map/ppermute | solution.py:429
  70.5 18.4 %collective-permute-start.16 = (bf16[480,768]{1,0:T(8,128)(2,1)S(1)}, bf16[480,768]{1,0:T(8,128)(2,1)S(1)}, u32[]{:S(2)}, u32[]{:S(2)}) collective-permute-start(bf16[480,768]{1,0:T(8,128)(2,1)S(1)} %broadcast_select_fusion), channel_id=1, source_target_pairs={{0,2},{2,4},{4,6},{6,0},{16,22},{18,16},{20,18},{22,20},{1,3},{3,5... | collective-permute-start | bytes 2211848 | tf_op jit(solution)/shard_map/ppermute | solution.py:434
  77.7 3.1 %collective-permute-start.14 = (bf16[2,192,1152]{2,1,0:T(8,128)(2,1)S(1)}, bf16[2,192,1152]{2,1,0:T(8,128)(2,1)S(1)}, u32[]{:S(2)}, u32[]{:S(2)}) collective-permute-start(bf16[2,192,1152]{2,1,0:T(8,128)(2,1)S(1)} %collective-permute-done.12.refs_1_), channel_id=1, source_target_pairs={{0,16},{16,0},{1,17},{17,1},{2,18},{18,2},{3,19},{19,3},{4,20},{20... | collective-permute-start | bytes 2654216 | tf_op jit(solution)/shard_map/ppermute | solution.py:440
  78.3 7.5 %collective-permute-start.13 = (bf16[192,1152]{1,0:T(8,128)(2,1)S(1)}, bf16[192,1152]{1,0:T(8,128)(2,1)S(1)}, u32[]{:S(2)}, u32[]{:S(2)}) collective-permute-start(bf16[192,1152]{1,0:T(8,128)(2,1)S(1)} %slice_bitcast_fusion), channel_id=1, source_target_pairs={{0,32},{32,64},{64,96},{96,128},{128,160},{160,192},{192,224},{224... | collective-permute-start | bytes 1327112 | tf_op jit(solution)/shard_map/ppermute | solution.py:429
  80.3 18.9 %collective-permute-start.17 = (bf16[480,768]{1,0:T(8,128)(2,1)}, bf16[480,768]{1,0:T(8,128)(2,1)S(1)}, u32[]{:S(2)}, u32[]{:S(2)}) collective-permute-start(bf16[480,768]{1,0:T(8,128)(2,1)} %collective-permute-done.5.refs_2_), channel_id=1, source_target_pairs={{0,16},{16,0},{1,17},{17,1},{2,18},{18,2},{3,19},{19,3},{4,20},{20... | collective-permute-start | bytes 2211848 | tf_op jit(solution)/shard_map/ppermute | solution.py:440
  80.3 27.0 %collective-permute-start.18 = (bf16[480,768]{1,0:T(8,128)(2,1)}, bf16[480,768]{1,0:T(8,128)(2,1)S(1)}, u32[]{:S(2)}, u32[]{:S(2)}) collective-permute-start(bf16[480,768]{1,0:T(8,128)(2,1)} %collective-permute-done.15.refs_3_), channel_id=1, source_target_pairs={{0,16},{16,0},{1,17},{17,1},{2,18},{18,2},{3,19},{19,3},{4,20},{20... | collective-permute-start | bytes 2211848 | tf_op jit(solution)/shard_map/ppermute | solution.py:440
  83.3 7.6 %copy-start.9 = (bf16[192,768]{1,0:T(8,128)(2,1)S(1)}, bf16[192,768]{1,0:T(8,128)(2,1)}, u32[]{:S(2)}) copy-start(bf16[192,768]{1,0:T(8,128)(2,1)} %copy-done.8) | copy-start | bytes 884740
  88.9 18.4 %copy-start.4 = (bf16[480,768]{1,0:T(8,128)(2,1)}, bf16[480,768]{1,0:T(8,128)(2,1)S(1)}, u32[]{:S(2)}) copy-start(bf16[480,768]{1,0:T(8,128)(2,1)S(1)} %collective-permute-done.16.refs_6_) | copy-start | bytes 2211844
  88.9 18.4 %collective-permute-start.19 = (bf16[480,768]{1,0:T(8,128)(2,1)S(1)}, bf16[480,768]{1,0:T(8,128)(2,1)S(1)}, u32[]{:S(2)}, u32[]{:S(2)}) collective-permute-start(bf16[480,768]{1,0:T(8,128)(2,1)S(1)} %collective-permute-done.16.refs_6_), channel_id=1, source_target_pairs={{0,16},{16,0},{1,17},{17,1},{2,18},{18,2},{3,19},{19,3},{4,20},{20... | collective-permute-start | bytes 2211848 | tf_op jit(solution)/shard_map/ppermute | solution.py:440
  92.0 6.7 %collective-permute-start.22 = (bf16[192,768]{1,0:T(8,128)(2,1)S(1)}, bf16[192,768]{1,0:T(8,128)(2,1)}, u32[]{:S(2)}, u32[]{:S(2)}) collective-permute-start(bf16[192,768]{1,0:T(8,128)(2,1)S(1)} %broadcast_select_fusion.3), channel_id=1, source_target_pairs={{0,2},{2,4},{4,6},{6,0},{16,22},{18,16},{20,18},{22,20},{1,3},{3,5... | collective-permute-start | bytes 884744 | tf_op jit(solution)/shard_map/ppermute | solution.py:434
  95.0 17.9 %collective-permute-start.20 = (bf16[192,768]{1,0:T(8,128)(2,1)S(1)}, bf16[192,768]{1,0:T(8,128)(2,1)}, u32[]{:S(2)}, u32[]{:S(2)}) collective-permute-start(bf16[192,768]{1,0:T(8,128)(2,1)S(1)} %copy-done.9), channel_id=1, source_target_pairs={{0,16},{16,0},{1,17},{17,1},{2,18},{18,2},{3,19},{19,3},{4,20},{20... | collective-permute-start | bytes 884744 | tf_op jit(solution)/shard_map/ppermute | solution.py:440
  98.7 14.3 %collective-permute-start.21 = (bf16[192,768]{1,0:T(8,128)(2,1)}, bf16[192,768]{1,0:T(8,128)(2,1)}, u32[]{:S(2)}, u32[]{:S(2)}) collective-permute-start(bf16[192,768]{1,0:T(8,128)(2,1)} %collective-permute-done.6.refs_11_), channel_id=1, source_target_pairs={{0,16},{16,0},{1,17},{17,1},{2,18},{18,2},{3,19},{19,3},{4,20},{20... | collective-permute-start | bytes 884744 | tf_op jit(solution)/shard_map/ppermute | solution.py:440
  99.2 8.2 %copy-start.5 = (bf16[480,768]{1,0:T(8,128)(2,1)}, bf16[480,768]{1,0:T(8,128)(2,1)S(1)}, u32[]{:S(2)}) copy-start(bf16[480,768]{1,0:T(8,128)(2,1)S(1)} %collective-permute-done.17.refs_4_) | copy-start | bytes 2211844
  99.2 13.8 %collective-permute-start.23 = (bf16[192,768]{1,0:T(8,128)(2,1)}, bf16[192,768]{1,0:T(8,128)(2,1)}, u32[]{:S(2)}, u32[]{:S(2)}) collective-permute-start(bf16[192,768]{1,0:T(8,128)(2,1)} %collective-permute-done.22.refs_14_), channel_id=1, source_target_pairs={{0,16},{16,0},{1,17},{17,1},{2,18},{18,2},{3,19},{19,3},{4,20},{20... | collective-permute-start | bytes 884744 | tf_op jit(solution)/shard_map/ppermute | solution.py:440
  99.3 14.8 %all-to-all-start.1 = ((bf16[16,48,144]{2,1,0:T(8,128)(2,1)}), bf16[16,48,144]{2,1,0:T(8,128)(2,1)}, u32[]{:S(2)}, u32[]{:S(2)}) async-start(bf16[16,48,144]{2,1,0:T(8,128)(2,1)} %attend_last.1), calls=%async_computation.1 | async-start | bytes 786432 | tf_op jit(solution)/shard_map/all_to_all | solution.py:511
  107.3 0.9 copy-start.6
  107.3 1.1 copy-start.7
